TPU v7x, 256 devices: a whole 4x4x8 slice. The times are simulated.
256 devices in a mesh: tm: 4 (over y), space: 64 (over x, z, core).
Axes of the slice: x: 4, y: 4, z: 8, core: 2. Of those that a mesh axis runs over, the one named last changes fastest.
Arguments:
- forcing: float32 [12, 8, 512, 512], P('tm', None, 'space'), may hold values from -6 to 6
- courant: float32 [2, 8, 512, 512], P(None, None, 'space'), may hold values from 0.05 to 0.45
- innovation: bfloat16 [12, 256, 16384], P('tm', None, 'space'), may hold values from -6 to 6
- obs_cells: int32 [12, 4, 16384], P('tm', None, 'space'), may hold values from 0 to 4095
- obs_weight: bfloat16 [12, 4, 16384], P('tm', None, 'space'), may hold values from 0 to 1
- obs_owner: int32 [12, 16384, 1], P('tm', 'space'), may hold values from 0 to 63; in each aligned block of 256 rows (0 to 255, 256 to 511, ..., all dimensions but the last counted through in order) at most 16 rows name the same one
- channel_weight: float32 [256, 8], replicated, may hold values from -2 to 2
- channel_rinv: float32 [256], replicated, may hold values from 0.1 to 0.5
Outputs:
- gradient: float32 [12, 8, 512, 512], P('tm', None, 'space')
Inputs may be any that keep to these rules, and one draw needn't show every extreme that they name: `obs_owner`: in each sub-window, no tile is named by more than 16 of the 256 records of one device (the rows of one device form an aligned block), a bound that some block reaches.
All inputs are finite; a program needn't handle non-finite values.
Results may differ from a plain program's by a relative error of at most 0.00075.
Values may be sent and summed in bfloat16 or wider, within the bound.
No kernel may reach another device: no remote copies, remote signals or barrier semaphores. Data moves between devices by JAX's collectives and lax.ppermute only.
A program may use at most 64 MiB of HBM per device.

v0:
```python
import math

import jax
import jax.numpy as jnp
from jax import lax
from jax.sharding import PartitionSpec as P

STEPS = 2


highest = lax.Precision.HIGHEST


def shifted(array, axis, by):
    count = lax.axis_size(axis)
    pairs = [(i, i + by) for i in range(count) if 0 <= i + by < count]
    return lax.ppermute(array, axis, pairs)


def forward_step(current, wind_x, wind_y):
    from_below = shifted(current[:, -1:, :], "space", 1)
    previous_y = jnp.concatenate([from_below, current[:, :-1, :]], axis=1)
    previous_x = jnp.roll(current, 1, axis=2)
    return current - wind_x * (current - previous_x) - wind_y * (current - previous_y)


def adjoint_step(current, wind_x, wind_y):
    carried = wind_y * current
    from_above = shifted(carried[:, :1, :], "space", -1)
    following = jnp.concatenate([carried[:, 1:, :], from_above], axis=1)
    return current * (1.0 - wind_x - wind_y) + jnp.roll(wind_x * current, -1, axis=2) + following


def stencil_matrix(cells, weights, size):
    cell_ids = jnp.arange(size, dtype=jnp.int32)
    matrix = jnp.zeros((cells.shape[1], size), jnp.float32)
    for corner in range(cells.shape[0]):
        matrix = matrix + jnp.where(
            cells[corner][:, None] == cell_ids[None, :],
            weights[corner].astype(jnp.float32)[:, None],
            0.0,
        )
    return matrix


def slot_blocks(cells, weights):
    slots = cells.shape[1]
    block = math.gcd(slots, 512)
    count = slots // block
    cell_blocks = jnp.transpose(cells.reshape(cells.shape[0], count, block), (1, 0, 2))
    weight_blocks = jnp.transpose(weights.reshape(weights.shape[0], count, block), (1, 0, 2))
    return (cell_blocks, weight_blocks, count, block)


def interpolate(flat_state, cells, weights):
    cell_blocks, weight_blocks, count, block = slot_blocks(cells, weights)
    size = flat_state.shape[1]

    def one_block(pair):
        matrix = stencil_matrix(pair[0], pair[1], size)
        return jnp.dot(flat_state, matrix.T, precision=highest, preferred_element_type=jnp.float32)

    blocks = lax.map(one_block, (cell_blocks, weight_blocks))
    return jnp.transpose(blocks, (1, 0, 2)).reshape(flat_state.shape[0], count * block)


def spread(cells, weights, adjoint_cols, size):
    cell_blocks, weight_blocks, count, block = slot_blocks(cells, weights)
    levels = adjoint_cols.shape[0]
    col_blocks = jnp.transpose(adjoint_cols.reshape(levels, count, block), (1, 0, 2))

    def add_block(total, items):
        matrix = stencil_matrix(items[0], items[1], size)
        return (
            total
            + jnp.dot(items[2], matrix, precision=highest, preferred_element_type=jnp.float32),
            None,
        )

    total, unused = lax.scan(
        add_block, jnp.zeros((levels, size), jnp.float32), (cell_blocks, weight_blocks, col_blocks)
    )
    return total


def slot_onehot(slot_index, total_slots):
    slot_ids = jnp.arange(total_slots, dtype=jnp.int32)
    return slot_index[:, :, None] == slot_ids[None, None, :]


def place_slots(values, placement):
    matrix = placement.astype(values.dtype)
    placed = jnp.einsum("scr,srt->sct", values, matrix, preferred_element_type=jnp.float32)
    return placed.astype(values.dtype)


def place_integers(values, placement):
    return jnp.sum(jnp.where(placement[:, None, :, :], values[:, :, :, None], 0), axis=2)


def obs_adjoint(columns, innovation, channel_weight, channel_rinv):
    evolved = jnp.einsum("cl,slm->scm", channel_weight, columns, precision=highest)
    departure = channel_rinv[None, :, None] * (evolved - innovation.astype(jnp.float32))
    return jnp.einsum(
        "cl,scm->slm", channel_weight, channel_rinv[None, :, None] * departure, precision=highest
    )


def shards(
    forcing, courant, innovation, obs_cells, obs_weight, obs_owner, channel_weight, channel_rinv
):
    sub_count = forcing.shape[0]
    levels = forcing.shape[1]
    tile_rows = forcing.shape[2]
    tile_width = forcing.shape[3]
    step_count = STEPS
    tile_count = lax.axis_size("space")
    windows_count = lax.axis_size("tm")
    wind_x = courant[0]
    wind_y = courant[1]
    zero_field = jnp.zeros((levels, tile_rows, tile_width), jnp.float32)
    incoming = zero_field
    end_states = []
    for rounds in range(windows_count):
        current = incoming
        end_states = []
        for sub_index in range(sub_count):
            forward_current = current + forcing[sub_index]
            for forward_step_index in range(step_count):
                forward_current = forward_step(forward_current, wind_x, wind_y)
            current = forward_current
            end_states.append(current)
        if rounds + 1 < windows_count:
            incoming = shifted(current, "tm", 1)
    flat_states = jnp.stack(end_states).reshape(sub_count, levels, tile_rows * tile_width)
    owner_tile = obs_owner[:, :, 0]
    record_count = owner_tile.shape[1]
    capacity = 4 * record_count // tile_count
    total_slots = tile_count * capacity
    record_ids = jnp.arange(record_count, dtype=jnp.int32)
    earlier = record_ids[:, None] <= record_ids[None, :]
    same_owner = owner_tile[:, :, None] == owner_tile[:, None, :]
    slot_rank = jnp.sum(jnp.logical_and(same_owner, earlier[None]).astype(jnp.int32), axis=1) - 1
    slot_index = owner_tile * capacity + slot_rank
    placement = slot_onehot(slot_index, total_slots)
    cell_buffer = place_integers(obs_cells, placement)
    weight_buffer = place_slots(obs_weight, placement)
    innovation_buffer = place_slots(innovation, placement)
    cell_in, weight_in, innovation_in = (
        lax.all_to_all(cell_buffer, "space", split_axis=2, concat_axis=2, tiled=True),
        lax.all_to_all(weight_buffer, "space", split_axis=2, concat_axis=2, tiled=True),
        lax.all_to_all(innovation_buffer, "space", split_axis=2, concat_axis=2, tiled=True),
    )
    columns = jax.vmap(interpolate)(flat_states, cell_in, weight_in)
    adjoint_cols = obs_adjoint(columns, innovation_in, channel_weight, channel_rinv)

    def spread_window(cells, weights, window_cols):
        return spread(cells, weights, window_cols, tile_rows * tile_width)

    forcing_adjoint = jax.vmap(spread_window)(cell_in, weight_in, adjoint_cols)
    forcing_adjoint = forcing_adjoint.reshape(sub_count, levels, tile_rows, tile_width)
    gradients = [None] * sub_count
    incoming = zero_field
    for rounds in range(windows_count):
        current = incoming
        for sub_index in reversed(range(sub_count)):
            adjoint_current = current + forcing_adjoint[sub_index]
            for step_index in range(step_count):
                adjoint_current = adjoint_step(adjoint_current, wind_x, wind_y)
            current = adjoint_current
            gradients[sub_index] = current
        if rounds + 1 < windows_count:
            incoming = shifted(current, "tm", -1)
    return jnp.stack(gradients)


def solution(mesh):
    return jax.shard_map(
        shards,
        mesh=mesh,
        in_specs=(
            P("tm", None, "space", None),
            P(None, None, "space", None),
            P("tm", None, "space"),
            P("tm", None, "space"),
            P("tm", None, "space"),
            P("tm", "space", None),
            P(),
            P(),
        ),
        out_specs=P("tm", None, "space", None),
        check_vma=False,
    )
```

profile of v0, /device:TPU:4, one launch (start us, length us, event | category | flops | bytes accessed | tf_op | source)
XLA Modules:
  0.0 568.5 jit_solution(9179756847241494613)
XLA Ops:
  3.0 6.6 %collective-permute-done = f32[8,1,512]{2,1,0:T(1,128)S(1)} collective-permute-done((f32[8,1,512]{2,1,0:T(1,128)S(1)}, f32[8,1,512]{2,1,0:T(1,128)S(1)}, u32[]{:S(2)}, u32[]{:S(2)}) %collective-permute-start) | collective-permute-done | bytes 16416 | tf_op jit(solution)/shard_map/ppermute | solution.py:17
  175.4 9.1 %all-to-all-start.1 = ((bf16[3,4,1024]{1,0,2:T(4,128)(2,1)}), bf16[3,4,1024]{1,0,2:T(4,128)(2,1)}, u32[]{:S(2)}, u32[]{:S(2)}) async-start(bf16[3,4,1024]{1,0,2:T(4,128)(2,1)} %copy.33), calls=%async_computation.1 | async-start | bytes 2097152 | tf_op jit(solution)/shard_map/all_to_all | solution.py:151
  188.8 19.8 %collective-permute-done.24 = f32[8,1,512]{2,1,0:T(1,128)S(1)} collective-permute-done((f32[8,1,512]{2,1,0:T(1,128)S(1)}, f32[8,1,512]{2,1,0:T(1,128)S(1)}, u32[]{:S(2)}, u32[]{:S(2)}) %collective-permute-start.24) | collective-permute-done | bytes 16416 | tf_op jit(solution)/shard_map/ppermute | solution.py:17
  217.9 11.2 %all-to-all-start = ((s32[64,1,192]{2,1,0:T(1,128)}), s32[64,1,192]{2,1,0:T(1,128)S(1)}, u32[]{:S(2)}, u32[]{:S(2)}) async-start(s32[64,1,192]{2,1,0:T(1,128)} %reshape.136), calls=%async_computation | async-start | bytes 131072 | tf_op jit(solution)/shard_map/all_to_all | solution.py:150
  237.0 7.8 %all-to-all-start.2 = ((bf16[3,256,1024]{1,0,2:T(4,128)(2,1)}), bf16[3,256,1024]{1,0,2:T(4,128)(2,1)}, u32[]{:S(2)}, u32[]{:S(2)}) async-start(bf16[3,256,1024]{1,0,2:T(4,128)(2,1)} %copy.37), calls=%async_computation.2 | async-start | bytes 4194304 | tf_op jit(solution)/shard_map/all_to_all | solution.py:152
  248.9 63.1 %while.21 = (s32[]{:T(128)}, f32[2,3,8,512]{3,2,1,0:T(8,128)S(1)}, s32[2,3,4,512]{3,1,2,0:T(4,128)S(1)}, bf16[2,3,4,512]{3,1,2,0:T(4,128)(2,1)S(1)}, f32[3,8,4096]{2,1,0:T(8,128)S(1)}, /*index=5*/s32[]{:T(128)}) while((s32[]{:T(128)}, f32[2,3,8,512]{3,2,1,0:T(8,128)S(1)}, s32[2,3,4,512]{3,1,2,0:T(4,128)S(1)}, ...), condition=%wide.region_3.4_spmd, body=%wide.region_2.3_spmd.sunk | while | flops 673191936 | bytes 667737 | solution.py:63
  249.0 31.5 %fusion.237 = f32[2,3,8,512]{3,2,1,0:T(8,128)S(1)} fusion(f32[2,3,8,512]{3,2,1,0:T(8,128)S(1)} %get-tuple-element.302, s32[]{:T(128)S(6)} %copy.122, f32[3,8,4096]{2,1,0:T(8,128)S(1)} %get-tuple-element.311, f32[3,512]{1,0:T(4,128)S(1)} %get-tuple-element.274, s32[3,512]{1,0:T(4,128)S(1)} %get-tuple-element.275, ...), kind=kOutput, calls=%fused_computation.22.clone.1 | convolution fusion | flops 673185792 | bytes 507908 | tf_op jit(solution)/shard_map/vmap()/while/body/eval_jaxpr/dot_general | solution.py:61
  280.6 31.5 %fusion.237 = f32[2,3,8,512]{3,2,1,0:T(8,128)S(1)} fusion(f32[2,3,8,512]{3,2,1,0:T(8,128)S(1)} %get-tuple-element.302, s32[]{:T(128)S(6)} %copy.122, f32[3,8,4096]{2,1,0:T(8,128)S(1)} %get-tuple-element.311, f32[3,512]{1,0:T(4,128)S(1)} %get-tuple-element.274, s32[3,512]{1,0:T(4,128)S(1)} %get-tuple-element.275, ...), kind=kOutput, calls=%fused_computation.22.clone.1 | convolution fusion | flops 673185792 | bytes 507908 | tf_op jit(solution)/shard_map/vmap()/while/body/eval_jaxpr/dot_general | solution.py:61
  320.1 53.8 %while.22 = (s32[]{:T(128)}, f32[3,8,4096]{2,1,0:T(8,128)}, f32[2,3,8,512]{3,2,1,0:T(8,128)S(1)}, s32[2,3,4,512]{3,1,2,0:T(4,128)}, bf16[2,3,4,512]{3,1,2,0:T(4,128)(2,1)}, /*index=5*/s32[]{:T(128)}, s32[]{:T(128)}) while((s32[]{:T(128)}, f32[3,8,4096]{2,1,0:T(8,128)}, f32[2,3,8,512]{3,2,1,0:T(8,128)S(1)}, ...), condition=%wide.region_5.6_spmd.clone, body=%wide.region_4.5_spmd.clone.sunk | while | flops 673388544 | bytes 1060971 | solution.py:80
  321.9 24.8 %fusion.241 = f32[3,8,4096]{2,1,0:T(8,128)} fusion(f32[3,512]{1,0:T(4,128)S(1)} %get-tuple-element.287, s32[3,512]{1,0:T(4,128)S(1)} %get-tuple-element.288, f32[3,512]{1,0:T(4,128)S(1)} %get-tuple-element.289, s32[3,512]{1,0:T(4,128)S(1)} %get-tuple-element.290, f32[3,512]{1,0:T(4,128)S(1)} %get-tuple-element.291, ...), kind=kOutput, calls=%fused_computation.59.clone.1 | convolution fusion | flops 673382400 | bytes 901125 | tf_op jit(solution)/shard_map/vmap()/while/body/eval_jaxpr/dot_general | solution.py:76
  348.2 25.7 %fusion.241 = f32[3,8,4096]{2,1,0:T(8,128)} fusion(f32[3,512]{1,0:T(4,128)S(1)} %get-tuple-element.287, s32[3,512]{1,0:T(4,128)S(1)} %get-tuple-element.288, f32[3,512]{1,0:T(4,128)S(1)} %get-tuple-element.289, s32[3,512]{1,0:T(4,128)S(1)} %get-tuple-element.290, f32[3,512]{1,0:T(4,128)S(1)} %get-tuple-element.291, ...), kind=kOutput, calls=%fused_computation.59.clone.1 | convolution fusion | flops 673382400 | bytes 901125 | tf_op jit(solution)/shard_map/vmap()/while/body/eval_jaxpr/dot_general | solution.py:76
  381.0 5.7 %collective-permute-start.28 = (f32[8,1,512]{2,1,0:T(1,128)S(1)}, f32[8,1,512]{2,1,0:T(1,128)S(1)}, u32[]{:S(2)}, u32[]{:S(2)}) collective-permute-start(f32[8,1,512]{2,1,0:T(1,128)S(1)} %slice.1000), channel_id=1, source_target_pairs={{1,0},{2,1},{3,2},{4,3},{5,4},{6,5},{7,6},{8,7},{9,8},{10,9},{11,1... | collective-permute-start | bytes 49160 | tf_op jit(solution)/shard_map/ppermute | solution.py:17
  388.4 5.7 %collective-permute-start.29 = (f32[8,1,512]{2,1,0:T(1,128)S(1)}, f32[8,1,512]{2,1,0:T(1,128)S(1)}, u32[]{:S(2)}, u32[]{:S(2)}) collective-permute-start(f32[8,1,512]{2,1,0:T(1,128)S(1)} %slice.1004), channel_id=1, source_target_pairs={{1,0},{2,1},{3,2},{4,3},{5,4},{6,5},{7,6},{8,7},{9,8},{10,9},{11,1... | collective-permute-start | bytes 49160 | tf_op jit(solution)/shard_map/ppermute | solution.py:17
  395.7 5.7 %collective-permute-start.30 = (f32[8,1,512]{2,1,0:T(1,128)S(1)}, f32[8,1,512]{2,1,0:T(1,128)S(1)}, u32[]{:S(2)}, u32[]{:S(2)}) collective-permute-start(f32[8,1,512]{2,1,0:T(1,128)S(1)} %slice.1008), channel_id=1, source_target_pairs={{1,0},{2,1},{3,2},{4,3},{5,4},{6,5},{7,6},{8,7},{9,8},{10,9},{11,1... | collective-permute-start | bytes 49160 | tf_op jit(solution)/shard_map/ppermute | solution.py:17
  403.0 5.7 %collective-permute-start.31 = (f32[8,1,512]{2,1,0:T(1,128)S(1)}, f32[8,1,512]{2,1,0:T(1,128)S(1)}, u32[]{:S(2)}, u32[]{:S(2)}) collective-permute-start(f32[8,1,512]{2,1,0:T(1,128)S(1)} %slice.1012), channel_id=1, source_target_pairs={{1,0},{2,1},{3,2},{4,3},{5,4},{6,5},{7,6},{8,7},{9,8},{10,9},{11,1... | collective-permute-start | bytes 49160 | tf_op jit(solution)/shard_map/ppermute | solution.py:17
  410.3 5.7 %collective-permute-start.32 = (f32[8,1,512]{2,1,0:T(1,128)S(1)}, f32[8,1,512]{2,1,0:T(1,128)S(1)}, u32[]{:S(2)}, u32[]{:S(2)}) collective-permute-start(f32[8,1,512]{2,1,0:T(1,128)S(1)} %slice.1016), channel_id=1, source_target_pairs={{1,0},{2,1},{3,2},{4,3},{5,4},{6,5},{7,6},{8,7},{9,8},{10,9},{11,1... | collective-permute-start | bytes 49160 | tf_op jit(solution)/shard_map/ppermute | solution.py:17
  418.8 6.0 %collective-permute-done.33 = f32[8,8,512]{2,1,0:T(8,128)S(1)} collective-permute-done((f32[8,8,512]{2,1,0:T(8,128)S(1)}, f32[8,8,512]{2,1,0:T(8,128)S(1)}, u32[]{:S(2)}, u32[]{:S(2)}) %collective-permute-start.33) | collective-permute-done | bytes 131104 | tf_op jit(solution)/shard_map/ppermute | solution.py:17
  431.4 5.7 %collective-permute-start.35 = (f32[8,1,512]{2,1,0:T(1,128)S(1)}, f32[8,1,512]{2,1,0:T(1,128)S(1)}, u32[]{:S(2)}, u32[]{:S(2)}) collective-permute-start(f32[8,1,512]{2,1,0:T(1,128)S(1)} %slice.1024), channel_id=1, source_target_pairs={{1,0},{2,1},{3,2},{4,3},{5,4},{6,5},{7,6},{8,7},{9,8},{10,9},{11,1... | collective-permute-start | bytes 49160 | tf_op jit(solution)/shard_map/ppermute | solution.py:17
  438.8 5.7 %collective-permute-start.36 = (f32[8,1,512]{2,1,0:T(1,128)S(1)}, f32[8,1,512]{2,1,0:T(1,128)S(1)}, u32[]{:S(2)}, u32[]{:S(2)}) collective-permute-start(f32[8,1,512]{2,1,0:T(1,128)S(1)} %slice.1028), channel_id=1, source_target_pairs={{1,0},{2,1},{3,2},{4,3},{5,4},{6,5},{7,6},{8,7},{9,8},{10,9},{11,1... | collective-permute-start | bytes 49160 | tf_op jit(solution)/shard_map/ppermute | solution.py:17
  446.0 5.7 %collective-permute-start.37 = (f32[8,1,512]{2,1,0:T(1,128)S(1)}, f32[8,1,512]{2,1,0:T(1,128)S(1)}, u32[]{:S(2)}, u32[]{:S(2)}) collective-permute-start(f32[8,1,512]{2,1,0:T(1,128)S(1)} %slice.1032), channel_id=1, source_target_pairs={{1,0},{2,1},{3,2},{4,3},{5,4},{6,5},{7,6},{8,7},{9,8},{10,9},{11,1... | collective-permute-start | bytes 49160 | tf_op jit(solution)/shard_map/ppermute | solution.py:17
  453.4 5.7 %collective-permute-start.38 = (f32[8,1,512]{2,1,0:T(1,128)S(1)}, f32[8,1,512]{2,1,0:T(1,128)S(1)}, u32[]{:S(2)}, u32[]{:S(2)}) collective-permute-start(f32[8,1,512]{2,1,0:T(1,128)S(1)} %slice.1036), channel_id=1, source_target_pairs={{1,0},{2,1},{3,2},{4,3},{5,4},{6,5},{7,6},{8,7},{9,8},{10,9},{11,1... | collective-permute-start | bytes 49160 | tf_op jit(solution)/shard_map/ppermute | solution.py:17
  460.7 5.7 %collective-permute-start.39 = (f32[8,1,512]{2,1,0:T(1,128)S(1)}, f32[8,1,512]{2,1,0:T(1,128)S(1)}, u32[]{:S(2)}, u32[]{:S(2)}) collective-permute-start(f32[8,1,512]{2,1,0:T(1,128)S(1)} %slice.1040), channel_id=1, source_target_pairs={{1,0},{2,1},{3,2},{4,3},{5,4},{6,5},{7,6},{8,7},{9,8},{10,9},{11,1... | collective-permute-start | bytes 49160 | tf_op jit(solution)/shard_map/ppermute | solution.py:17
  481.1 5.7 %collective-permute-start.42 = (f32[8,1,512]{2,1,0:T(1,128)S(1)}, f32[8,1,512]{2,1,0:T(1,128)S(1)}, u32[]{:S(2)}, u32[]{:S(2)}) collective-permute-start(f32[8,1,512]{2,1,0:T(1,128)S(1)} %slice.1048), channel_id=1, source_target_pairs={{1,0},{2,1},{3,2},{4,3},{5,4},{6,5},{7,6},{8,7},{9,8},{10,9},{11,1... | collective-permute-start | bytes 49160 | tf_op jit(solution)/shard_map/ppermute | solution.py:17
  510.3 5.7 %collective-permute-start.46 = (f32[8,1,512]{2,1,0:T(1,128)S(1)}, f32[8,1,512]{2,1,0:T(1,128)S(1)}, u32[]{:S(2)}, u32[]{:S(2)}) collective-permute-start(f32[8,1,512]{2,1,0:T(1,128)S(1)} %slice.1064), channel_id=1, source_target_pairs={{1,0},{2,1},{3,2},{4,3},{5,4},{6,5},{7,6},{8,7},{9,8},{10,9},{11,1... | collective-permute-start | bytes 49160 | tf_op jit(solution)/shard_map/ppermute | solution.py:17
  (385 shorter events, 322.9 us)
Async XLA Ops:
  1.0 8.6 %collective-permute-start = (f32[8,1,512]{2,1,0:T(1,128)S(1)}, f32[8,1,512]{2,1,0:T(1,128)S(1)}, u32[]{:S(2)}, u32[]{:S(2)}) collective-permute-start(f32[8,1,512]{2,1,0:T(1,128)S(1)} %slice.899), channel_id=1, source_target_pairs={{0,1},{1,2},{2,3},{3,4},{4,5},{5,6},{6,7},{7,8},{8,9},{9,10},{10,1... | collective-permute-start | bytes 49160 | tf_op jit(solution)/shard_map/ppermute | solution.py:17
  171.4 13.2 %collective-permute-start.23 = (f32[8,1,512]{2,1,0:T(1,128)S(1)}, f32[8,1,512]{2,1,0:T(1,128)S(1)}, u32[]{:S(2)}, u32[]{:S(2)}) collective-permute-start(f32[8,1,512]{2,1,0:T(1,128)S(1)} %slice.979), channel_id=1, source_target_pairs={{0,1},{1,2},{2,3},{3,4},{4,5},{5,6},{6,7},{7,8},{8,9},{9,10},{10,1... | collective-permute-start | bytes 49160 | tf_op jit(solution)/shard_map/ppermute | solution.py:17
  175.4 42.5 %all-to-all-start.1 = ((bf16[3,4,1024]{1,0,2:T(4,128)(2,1)}), bf16[3,4,1024]{1,0,2:T(4,128)(2,1)}, u32[]{:S(2)}, u32[]{:S(2)}) async-start(bf16[3,4,1024]{1,0,2:T(4,128)(2,1)} %copy.33), calls=%async_computation.1 | async-start | bytes 2097152 | tf_op jit(solution)/shard_map/all_to_all | solution.py:151
  184.7 23.8 %collective-permute-start.24 = (f32[8,1,512]{2,1,0:T(1,128)S(1)}, f32[8,1,512]{2,1,0:T(1,128)S(1)}, u32[]{:S(2)}, u32[]{:S(2)}) collective-permute-start(f32[8,1,512]{2,1,0:T(1,128)S(1)} %slice.983), channel_id=1, source_target_pairs={{0,1},{1,2},{2,3},{3,4},{4,5},{5,6},{6,7},{7,8},{8,9},{9,10},{10,1... | collective-permute-start | bytes 49160 | tf_op jit(solution)/shard_map/ppermute | solution.py:17
  216.0 32.7 %collective-permute-start.26 = (f32[8,1,512]{2,1,0:T(1,128)S(1)}, f32[8,1,512]{2,1,0:T(1,128)S(1)}, u32[]{:S(2)}, u32[]{:S(2)}) collective-permute-start(f32[8,1,512]{2,1,0:T(1,128)S(1)} %slice.991), channel_id=1, source_target_pairs={{0,1},{1,2},{2,3},{3,4},{4,5},{5,6},{6,7},{7,8},{8,9},{9,10},{10,1... | collective-permute-start | bytes 49160 | tf_op jit(solution)/shard_map/ppermute | solution.py:17
  217.9 19.1 %all-to-all-start = ((s32[64,1,192]{2,1,0:T(1,128)}), s32[64,1,192]{2,1,0:T(1,128)S(1)}, u32[]{:S(2)}, u32[]{:S(2)}) async-start(s32[64,1,192]{2,1,0:T(1,128)} %reshape.136), calls=%async_computation | async-start | bytes 131072 | tf_op jit(solution)/shard_map/all_to_all | solution.py:150
  237.0 78.3 %all-to-all-start.2 = ((bf16[3,256,1024]{1,0,2:T(4,128)(2,1)}), bf16[3,256,1024]{1,0,2:T(4,128)(2,1)}, u32[]{:S(2)}, u32[]{:S(2)}) async-start(bf16[3,256,1024]{1,0,2:T(4,128)(2,1)} %copy.37), calls=%async_computation.2 | async-start | bytes 4194304 | tf_op jit(solution)/shard_map/all_to_all | solution.py:152
  381.0 7.2 %collective-permute-start.28 = (f32[8,1,512]{2,1,0:T(1,128)S(1)}, f32[8,1,512]{2,1,0:T(1,128)S(1)}, u32[]{:S(2)}, u32[]{:S(2)}) collective-permute-start(f32[8,1,512]{2,1,0:T(1,128)S(1)} %slice.1000), channel_id=1, source_target_pairs={{1,0},{2,1},{3,2},{4,3},{5,4},{6,5},{7,6},{8,7},{9,8},{10,9},{11,1... | collective-permute-start | bytes 49160 | tf_op jit(solution)/shard_map/ppermute | solution.py:17
  388.4 7.2 %collective-permute-start.29 = (f32[8,1,512]{2,1,0:T(1,128)S(1)}, f32[8,1,512]{2,1,0:T(1,128)S(1)}, u32[]{:S(2)}, u32[]{:S(2)}) collective-permute-start(f32[8,1,512]{2,1,0:T(1,128)S(1)} %slice.1004), channel_id=1, source_target_pairs={{1,0},{2,1},{3,2},{4,3},{5,4},{6,5},{7,6},{8,7},{9,8},{10,9},{11,1... | collective-permute-start | bytes 49160 | tf_op jit(solution)/shard_map/ppermute | solution.py:17
  395.7 7.2 %collective-permute-start.30 = (f32[8,1,512]{2,1,0:T(1,128)S(1)}, f32[8,1,512]{2,1,0:T(1,128)S(1)}, u32[]{:S(2)}, u32[]{:S(2)}) collective-permute-start(f32[8,1,512]{2,1,0:T(1,128)S(1)} %slice.1008), channel_id=1, source_target_pairs={{1,0},{2,1},{3,2},{4,3},{5,4},{6,5},{7,6},{8,7},{9,8},{10,9},{11,1... | collective-permute-start | bytes 49160 | tf_op jit(solution)/shard_map/ppermute | solution.py:17
  403.0 7.2 %collective-permute-start.31 = (f32[8,1,512]{2,1,0:T(1,128)S(1)}, f32[8,1,512]{2,1,0:T(1,128)S(1)}, u32[]{:S(2)}, u32[]{:S(2)}) collective-permute-start(f32[8,1,512]{2,1,0:T(1,128)S(1)} %slice.1012), channel_id=1, source_target_pairs={{1,0},{2,1},{3,2},{4,3},{5,4},{6,5},{7,6},{8,7},{9,8},{10,9},{11,1... | collective-permute-start | bytes 49160 | tf_op jit(solution)/shard_map/ppermute | solution.py:17
  410.3 7.2 %collective-permute-start.32 = (f32[8,1,512]{2,1,0:T(1,128)S(1)}, f32[8,1,512]{2,1,0:T(1,128)S(1)}, u32[]{:S(2)}, u32[]{:S(2)}) collective-permute-start(f32[8,1,512]{2,1,0:T(1,128)S(1)} %slice.1016), channel_id=1, source_target_pairs={{1,0},{2,1},{3,2},{4,3},{5,4},{6,5},{7,6},{8,7},{9,8},{10,9},{11,1... | collective-permute-start | bytes 49160 | tf_op jit(solution)/shard_map/ppermute | solution.py:17
  417.5 7.3 %collective-permute-start.33 = (f32[8,8,512]{2,1,0:T(8,128)S(1)}, f32[8,8,512]{2,1,0:T(8,128)S(1)}, u32[]{:S(2)}, u32[]{:S(2)}) collective-permute-start(f32[8,8,512]{2,1,0:T(8,128)S(1)} %fusion.177), channel_id=1, source_target_pairs={{64,0},{128,64},{192,128},{65,1},{129,65},{193,129},{66,2},{130,66... | collective-permute-start | bytes 393224 | tf_op jit(solution)/shard_map/ppermute | solution.py:17
  431.4 7.2 %collective-permute-start.35 = (f32[8,1,512]{2,1,0:T(1,128)S(1)}, f32[8,1,512]{2,1,0:T(1,128)S(1)}, u32[]{:S(2)}, u32[]{:S(2)}) collective-permute-start(f32[8,1,512]{2,1,0:T(1,128)S(1)} %slice.1024), channel_id=1, source_target_pairs={{1,0},{2,1},{3,2},{4,3},{5,4},{6,5},{7,6},{8,7},{9,8},{10,9},{11,1... | collective-permute-start | bytes 49160 | tf_op jit(solution)/shard_map/ppermute | solution.py:17
  446.0 7.2 %collective-permute-start.37 = (f32[8,1,512]{2,1,0:T(1,128)S(1)}, f32[8,1,512]{2,1,0:T(1,128)S(1)}, u32[]{:S(2)}, u32[]{:S(2)}) collective-permute-start(f32[8,1,512]{2,1,0:T(1,128)S(1)} %slice.1032), channel_id=1, source_target_pairs={{1,0},{2,1},{3,2},{4,3},{5,4},{6,5},{7,6},{8,7},{9,8},{10,9},{11,1... | collective-permute-start | bytes 49160 | tf_op jit(solution)/shard_map/ppermute | solution.py:17
  453.4 7.2 %collective-permute-start.38 = (f32[8,1,512]{2,1,0:T(1,128)S(1)}, f32[8,1,512]{2,1,0:T(1,128)S(1)}, u32[]{:S(2)}, u32[]{:S(2)}) collective-permute-start(f32[8,1,512]{2,1,0:T(1,128)S(1)} %slice.1036), channel_id=1, source_target_pairs={{1,0},{2,1},{3,2},{4,3},{5,4},{6,5},{7,6},{8,7},{9,8},{10,9},{11,1... | collective-permute-start | bytes 49160 | tf_op jit(solution)/shard_map/ppermute | solution.py:17
  460.7 7.2 %collective-permute-start.39 = (f32[8,1,512]{2,1,0:T(1,128)S(1)}, f32[8,1,512]{2,1,0:T(1,128)S(1)}, u32[]{:S(2)}, u32[]{:S(2)}) collective-permute-start(f32[8,1,512]{2,1,0:T(1,128)S(1)} %slice.1040), channel_id=1, source_target_pairs={{1,0},{2,1},{3,2},{4,3},{5,4},{6,5},{7,6},{8,7},{9,8},{10,9},{11,1... | collective-permute-start | bytes 49160 | tf_op jit(solution)/shard_map/ppermute | solution.py:17
  488.4 7.2 %collective-permute-start.43 = (f32[8,1,512]{2,1,0:T(1,128)S(1)}, f32[8,1,512]{2,1,0:T(1,128)S(1)}, u32[]{:S(2)}, u32[]{:S(2)}) collective-permute-start(f32[8,1,512]{2,1,0:T(1,128)S(1)} %slice.1052), channel_id=1, source_target_pairs={{1,0},{2,1},{3,2},{4,3},{5,4},{6,5},{7,6},{8,7},{9,8},{10,9},{11,1... | collective-permute-start | bytes 49160 | tf_op jit(solution)/shard_map/ppermute | solution.py:17
  495.7 7.2 %collective-permute-start.44 = (f32[8,1,512]{2,1,0:T(1,128)S(1)}, f32[8,1,512]{2,1,0:T(1,128)S(1)}, u32[]{:S(2)}, u32[]{:S(2)}) collective-permute-start(f32[8,1,512]{2,1,0:T(1,128)S(1)} %slice.1056), channel_id=1, source_target_pairs={{1,0},{2,1},{3,2},{4,3},{5,4},{6,5},{7,6},{8,7},{9,8},{10,9},{11,1... | collective-permute-start | bytes 49160 | tf_op jit(solution)/shard_map/ppermute | solution.py:17
  503.0 7.2 %collective-permute-start.45 = (f32[8,1,512]{2,1,0:T(1,128)S(1)}, f32[8,1,512]{2,1,0:T(1,128)S(1)}, u32[]{:S(2)}, u32[]{:S(2)}) collective-permute-start(f32[8,1,512]{2,1,0:T(1,128)S(1)} %slice.1060), channel_id=1, source_target_pairs={{1,0},{2,1},{3,2},{4,3},{5,4},{6,5},{7,6},{8,7},{9,8},{10,9},{11,1... | collective-permute-start | bytes 49160 | tf_op jit(solution)/shard_map/ppermute | solution.py:17
  510.3 7.2 %collective-permute-start.46 = (f32[8,1,512]{2,1,0:T(1,128)S(1)}, f32[8,1,512]{2,1,0:T(1,128)S(1)}, u32[]{:S(2)}, u32[]{:S(2)}) collective-permute-start(f32[8,1,512]{2,1,0:T(1,128)S(1)} %slice.1064), channel_id=1, source_target_pairs={{1,0},{2,1},{3,2},{4,3},{5,4},{6,5},{7,6},{8,7},{9,8},{10,9},{11,1... | collective-permute-start | bytes 49160 | tf_op jit(solution)/shard_map/ppermute | solution.py:17
  530.7 7.2 %collective-permute-start.49 = (f32[8,1,512]{2,1,0:T(1,128)S(1)}, f32[8,1,512]{2,1,0:T(1,128)S(1)}, u32[]{:S(2)}, u32[]{:S(2)}) collective-permute-start(f32[8,1,512]{2,1,0:T(1,128)S(1)} %slice.1072), channel_id=1, source_target_pairs={{1,0},{2,1},{3,2},{4,3},{5,4},{6,5},{7,6},{8,7},{9,8},{10,9},{11,1... | collective-permute-start | bytes 49160 | tf_op jit(solution)/shard_map/ppermute | solution.py:17
  538.1 7.2 %collective-permute-start.50 = (f32[8,1,512]{2,1,0:T(1,128)S(1)}, f32[8,1,512]{2,1,0:T(1,128)S(1)}, u32[]{:S(2)}, u32[]{:S(2)}) collective-permute-start(f32[8,1,512]{2,1,0:T(1,128)S(1)} %slice.1076), channel_id=1, source_target_pairs={{1,0},{2,1},{3,2},{4,3},{5,4},{6,5},{7,6},{8,7},{9,8},{10,9},{11,1... | collective-permute-start | bytes 49160 | tf_op jit(solution)/shard_map/ppermute | solution.py:17
  545.4 7.2 %collective-permute-start.51 = (f32[8,1,512]{2,1,0:T(1,128)S(1)}, f32[8,1,512]{2,1,0:T(1,128)S(1)}, u32[]{:S(2)}, u32[]{:S(2)}) collective-permute-start(f32[8,1,512]{2,1,0:T(1,128)S(1)} %slice.1080), channel_id=1, source_target_pairs={{1,0},{2,1},{3,2},{4,3},{5,4},{6,5},{7,6},{8,7},{9,8},{10,9},{11,1... | collective-permute-start | bytes 49160 | tf_op jit(solution)/shard_map/ppermute | solution.py:17
  (44 other events, 786.9 us)
where the time goes:
time: 579 us; the launch traced here: 569 us
  starting transfers between devices  224 us (39%)
  waiting for transfers between devices  182 us (31%)
  matrix products  122 us (21%)
  local copies, waits for them, and re-layouts  24.4 us (4%)
  other arithmetic  13.2 us (2%)
    ppermute x54, starting transfers between devices, shifted(): return lax.ppermute(array, axis, pairs)  196 us
    ppermute x54, waiting for transfers between devices, shifted(): return lax.ppermute(array, axis, pairs)  179 us
    dot_general x2, matrix products, one_block(): jnp.dot(flat_state, matrix.T, precision=highest, preferred_element_type=j...  62.9 us
    dot_general x2, matrix products, add_block(): jnp.dot(items[2], matrix, precision=highest, preferred_element_type=jnp.f...  50.6 us
  transfers between devices with their start and end apart: 57, of which 53 were waited for; matrix products, arithmetic and copies ran while one was open for 16% of the time, Pallas kernels for 0%

commit v1 on v0

v1 whole, which is shorter than its diff:
```python
import functools

import jax
import jax.numpy as jnp
from jax import lax
from jax.experimental import pallas as pl
from jax.experimental.pallas import tpu as pltpu
from jax.sharding import PartitionSpec as P

LEVELS = 8
ROWS = 8
WIDTH = 512
SUBS = 3
TILES = 64
PARTS = 4
RECORDS = 256
CORNERS = 4
HALF = 256
PIECES = WIDTH // HALF * ROWS
CHUNKS = 8
LANES = 128

f32 = jnp.float32
bf16 = jnp.bfloat16
highest = lax.Precision.HIGHEST


def struct(*shape, dtype=f32):
    return jax.ShapeDtypeStruct(shape, dtype)


def split(value):
    top = value.astype(bf16)
    return top, (value - top.astype(f32)).astype(bf16)


def forward_step(current, wind_x, wind_y, low):
    result = {}
    for row in range(low + 1, ROWS):
        here = current[row]
        left = pltpu.roll(here, 1, 1)
        result[row] = (
            here - wind_x(row) * (here - left) - wind_y(row) * (here - current[row - 1])
        )
    return result


def adjoint_step(current, wind_x, wind_y, high):
    result = {}
    for row in range(high - 1):
        here = current[row]
        along, across = wind_x(row), wind_y(row)
        result[row] = (
            here * (1.0 - along - across)
            + pltpu.roll(along * here, WIDTH - 1, 1)
            + wind_y(row + 1) * current[row + 1]
        )
    return result


def forward_steps(current, winds, low, count):
    for _ in range(count):
        current = forward_step(current, winds[0], winds[1], low)
        low += 1
    return current, low


def adjoint_steps(current, winds, high, count):
    for _ in range(count):
        current = adjoint_step(current, winds[0], winds[1], high)
        high -= 1
    return current, high


WINDS = 2
FIELDS = WINDS + SUBS
DOWN_EDGE = 3
UP_EDGE = 4
EXTRA = 4


def lower_reader(own, below, edge, field):
    def read(row):
        if row >= 0:
            return own[field * ROWS + row]
        if row >= -ROWS:
            return below[field * ROWS + row + ROWS]
        return edge[field * DOWN_EDGE + row + ROWS + DOWN_EDGE]

    return read


def upper_reader(own, above, edge, field):
    def read(row):
        if row < ROWS:
            return own[field * ROWS + row]
        if row < 2 * ROWS:
            return above[field * ROWS + row - ROWS]
        return edge[field * UP_EDGE + row - 2 * ROWS]

    return read


def lower_fields(fields, below, edge):
    readers = [lower_reader(fields, below, edge, field) for field in range(FIELDS)]
    return readers[:WINDS], readers[WINDS:]


def upper_winds(fields, above, edge):
    return [upper_reader(fields, above, edge, field) for field in range(WINDS)]


def add_rows(current, other, low, high):
    return {row: current[row] + other(row) for row in range(low, high)}


def rows_kernel(forcing, courant, fields, winds, down_edge, up_edge):
    for field in range(FIELDS):
        source = courant[field] if field < WINDS else forcing[field - WINDS]
        turned = jnp.swapaxes(source, 0, 1)
        fields[pl.ds(field * ROWS, ROWS)] = turned
        if field < WINDS:
            winds[pl.ds(field * ROWS, ROWS)] = turned
            up_edge[pl.ds(field * UP_EDGE, UP_EDGE)] = turned[:UP_EDGE]
        if field <= WINDS:
            down_edge[pl.ds(field * DOWN_EDGE, DOWN_EDGE)] = turned[ROWS - DOWN_EDGE :]


def pack_kernel(innovation, cells, weight, owner, channel_weight, rinv, send, mixing):
    sub_id = lax.broadcasted_iota(jnp.int32, (RECORDS, RECORDS), 0)
    lane_id = lax.broadcasted_iota(jnp.int32, (RECORDS, RECORDS), 1)
    same_place = sub_id == lane_id
    not_later = lane_id <= sub_id

    eye = (
        lax.broadcasted_iota(jnp.int32, (LEVELS, LEVELS), 0)
        == lax.broadcasted_iota(jnp.int32, (LEVELS, LEVELS), 1)
    ).astype(f32)
    turned = lax.dot_general(
        eye, channel_weight[...], (((1,), (1,)), ((), ())),
        precision=highest, preferred_element_type=f32,
    )
    scaled = turned * (rinv[...] * rinv[...])
    matrix = jnp.dot(scaled, channel_weight[...], precision=highest, preferred_element_type=f32)
    for level in range(LEVELS):
        mixing[level] = jnp.broadcast_to(matrix[:, level : level + 1], (LEVELS, LANES))
    top = scaled.astype(bf16)
    rest = scaled - top.astype(f32)
    middle = rest.astype(bf16)
    low = (rest - middle.astype(f32)).astype(bf16)

    spread_row = lax.broadcasted_iota(jnp.int32, (2 * LEVELS, LANES), 0)
    spread_lane = lax.broadcasted_iota(jnp.int32, (2 * LEVELS, LANES), 1)
    repeat = (
        (spread_lane // 64 == spread_row // LEVELS) & (spread_lane % LEVELS == spread_row % LEVELS)
    ).astype(f32)
    slot_lane = lax.broadcasted_iota(jnp.int32, (RECORDS, LANES), 1)
    slot_rank = ((slot_lane % 64) // LEVELS) * 2
    tile_id = lax.broadcasted_iota(jnp.int32, (TILES, RECORDS), 0)
    ones = jnp.ones((RECORDS, LANES), bf16)
    for sub in range(SUBS):
        data = innovation[sub]
        projected = (
            jnp.dot(top, data, preferred_element_type=f32)
            + jnp.dot(middle, data, preferred_element_type=f32)
            + jnp.dot(low, data, preferred_element_type=f32)
        )
        payload = jnp.concatenate(
            [cells[sub].astype(f32), weight[sub].astype(f32), projected], axis=0
        )
        owner_column = jnp.broadcast_to(owner[sub], (RECORDS, RECORDS))
        owner_row = jnp.sum(jnp.where(same_place, owner_column, 0), axis=0, keepdims=True)
        earlier = jnp.where((owner_column == owner_row) & not_later, 1.0, 0.0).astype(bf16)
        rank = jnp.dot(earlier, ones, preferred_element_type=f32).astype(jnp.int32) - 1
        repeated = lax.dot_general(
            payload, repeat, (((0,), (0,)), ((), ())),
            precision=highest, preferred_element_type=f32,
        )
        target = (tile_id == owner_row).astype(f32)
        for half in range(2):
            chosen = jnp.where(rank == slot_rank + half, repeated, 0.0)
            send[pl.ds(2 * sub + half, TILES, stride=8), :] = jnp.dot(
                target, chosen, precision=highest, preferred_element_type=f32
            )
    for spare in range(2 * SUBS, 8):
        send[pl.ds(spare, TILES, stride=8), :] = jnp.zeros((TILES, LANES), f32)


def observe(received, mixing, states, slots, pieces, total):
    rows_id = lax.broadcasted_iota(jnp.int32, (HALF, LANES), 0)

    def one_sub(sub, _):
        for half in range(2):
            pieces[pl.ds(half * TILES, TILES), :] = received[
                pl.ds(2 * sub + half, TILES, stride=8), :
            ]
        slots[...] = pieces[...].T
        top, low = split(states[sub])
        left = jnp.concatenate([top, low], axis=0)
        total[...] = jnp.zeros_like(total)

        def one_chunk(chunk, _):
            place = pl.multiple_of(chunk * LEVELS, LEVELS)
            record = slots[pl.ds(place, LEVELS), :]
            projected = slots[pl.ds(TILES + place, LEVELS), :]
            cell = record.astype(jnp.int32)
            piece = cell // HALF
            column = cell - piece * HALF
            stencil = jnp.concatenate(
                [
                    jnp.where(
                        rows_id == column[corner : corner + 1],
                        record[CORNERS + corner : CORNERS + corner + 1],
                        0.0,
                    ).astype(bf16)
                    for corner in range(CORNERS)
                ],
                axis=1,
            )
            found = jnp.dot(left, stencil, preferred_element_type=f32)
            values = jnp.zeros((LEVELS, LANES), f32)
            marks = []
            for corner in range(CORNERS):
                wanted = jnp.broadcast_to(piece[corner : corner + 1], (LEVELS, LANES))
                part = slice(corner * LANES, (corner + 1) * LANES)
                for number in range(PIECES):
                    hit = wanted == number
                    marks.append(hit)
                    high = number * LEVELS
                    lowest = (PIECES + number) * LEVELS
                    both = found[high : high + LEVELS, part] + found[lowest : lowest + LEVELS, part]
                    values = values + jnp.where(hit, both, 0.0)
            adjoint = -projected
            for level in range(LEVELS):
                adjoint = adjoint + mixing[level] * values[level : level + 1]
            first, second = split(adjoint)
            first, second = first.astype(f32), second.astype(f32)
            spread = jnp.concatenate(
                [
                    jnp.concatenate(
                        [
                            jnp.where(marks[corner * PIECES + number], source, 0.0)
                            for source in (first, second)
                            for number in range(PIECES)
                        ],
                        axis=0,
                    ).astype(bf16)
                    for corner in range(CORNERS)
                ],
                axis=1,
            )
            total[...] += lax.dot_general(
                spread, stencil, (((1,), (1,)), ((), ())), preferred_element_type=f32
            )
            return 0

        lax.fori_loop(0, CHUNKS, one_chunk, 0)
        size = PIECES * LEVELS
        states[sub] = total[pl.ds(0, size), :] + total[pl.ds(size, size), :]
        return 0

    lax.fori_loop(0, SUBS, one_sub, 0)


def forward_local_kernel(fields, below, edge, own, extended):
    winds, forces = lower_fields(fields, below, edge)
    low = -(ROWS + 2)
    current = {row: forces[0](row) for row in range(low, ROWS)}
    current, low = forward_steps(current, winds, low, 2)
    for sub in range(1, SUBS):
        current = add_rows(current, forces[sub], low, ROWS)
        current, low = forward_steps(current, winds, low, 2)
    for row in range(ROWS):
        own[row] = current[row]
    for row in range(-EXTRA, ROWS):
        extended[row + EXTRA] = current[row]


def lower_state(own, extended, low):
    return {row: own[row] if row >= 0 else extended[row + ROWS + EXTRA] for row in range(low, ROWS)}


def forward_pair_kernel(
    fields, below, edge, mine, before_own, before_extended, own, extended
):
    winds, _ = lower_fields(fields, below, edge)
    low = -(ROWS + 2)
    current, low = forward_steps(lower_state(before_own, before_extended, low), winds, low, 6)
    for row in range(-EXTRA, ROWS):
        value = current[row] + mine[row + EXTRA]
        extended[row + EXTRA] = value
        if row >= 0:
            own[row] = value


def forward_final_kernel(
    fields, below, edge,
    before_own, before_extended, pair_own, pair_extended, received, mixing,
    result, result_edge,
    states, slots, pieces, total,
):
    winds, forces = lower_fields(fields, below, edge)
    low = -(ROWS + EXTRA)
    current, low = forward_steps(lower_state(pair_own, pair_extended, low), winds, low, 6)
    before = lower_state(before_own, before_extended, low)
    current = {row: current[row] + before[row] for row in current}
    for sub in range(SUBS):
        current = add_rows(current, forces[sub], low, ROWS)
        current, low = forward_steps(current, winds, low, 2)
        for row in range(ROWS):
            for half in range(2):
                place = (2 * row + half) * LEVELS
                states[sub, place : place + LEVELS, :] = current[row][
                    :, half * HALF : (half + 1) * HALF
                ]
    observe(received, mixing, states, slots, pieces, total)
    for sub in range(SUBS):
        for row in range(ROWS):
            for half in range(2):
                place = (2 * row + half) * LEVELS
                value = states[sub, place : place + LEVELS, :]
                result[sub, row, :, half * HALF : (half + 1) * HALF] = value
                if sub == SUBS - 1 and row < 2:
                    result_edge[row, :, half * HALF : (half + 1) * HALF] = value


def source_reader(own, above, edge, sub):
    def read(row):
        if row < ROWS:
            return own[sub, row]
        if row < 2 * ROWS:
            return above[sub, row - ROWS]
        return edge[row - 2 * ROWS]

    return read


def adjoint_local_kernel(
    source, source_above, source_edge, fields, above, edge, own, extended
):
    winds = upper_winds(fields, above, edge)
    high = 2 * ROWS + 2
    sources = [source_reader(source, source_above, source_edge, sub) for sub in range(SUBS)]
    current = {row: sources[SUBS - 1](row) for row in range(high)}
    current, high = adjoint_steps(current, winds, high, 2)
    for sub in reversed(range(SUBS - 1)):
        current = add_rows(current, sources[sub], 0, high)
        current, high = adjoint_steps(current, winds, high, 2)
    for row in range(ROWS):
        own[row] = current[row]
    for row in range(ROWS + EXTRA):
        extended[row] = current[row]


def upper_state(own, extended, high):
    return {row: own[row] if row < ROWS else extended[row - ROWS] for row in range(high)}


def adjoint_pair_kernel(
    fields, above, edge, mine, after_own, after_extended, own, extended
):
    winds = upper_winds(fields, above, edge)
    high = 2 * ROWS + 2
    current, high = adjoint_steps(upper_state(after_own, after_extended, high), winds, high, 6)
    for row in range(ROWS + EXTRA):
        value = current[row] + mine[row]
        extended[row] = value
        if row < ROWS:
            own[row] = value


def adjoint_final_kernel(
    source, source_above, fields, above, edge,
    after_own, after_extended, pair_own, pair_extended, gradient,
):
    winds = upper_winds(fields, above, edge)
    high = 2 * ROWS + EXTRA
    current, high = adjoint_steps(upper_state(pair_own, pair_extended, high), winds, high, 6)
    after = upper_state(after_own, after_extended, high)
    current = {row: current[row] + after[row] for row in current}
    for sub in reversed(range(SUBS)):
        current = add_rows(current, source_reader(source, source_above, None, sub), 0, high)
        current, high = adjoint_steps(current, winds, high, 2)
        gradient[sub] = jnp.swapaxes(jnp.stack([current[row] for row in range(ROWS)]), 0, 1)


def run(kernel, outputs, arguments, scratch=(), name=None, flops=2_000_000):
    moved = sum(a.size * a.dtype.itemsize for a in arguments)
    return pl.pallas_call(
        kernel,
        out_shape=outputs,
        scratch_shapes=scratch,
        compiler_params=pltpu.CompilerParams(vmem_limit_bytes=40 * 1024 * 1024),
        cost_estimate=pl.CostEstimate(flops=flops, bytes_accessed=moved, transcendentals=0),
        name=name,
    )(*arguments)


def moved(array, parts, tiles):
    pairs = []
    for part in range(PARTS):
        for tile in range(TILES):
            to_part, to_tile = part + parts, tile + tiles
            if 0 <= to_part < PARTS and 0 <= to_tile < TILES:
                pairs.append((part * TILES + tile, to_part * TILES + to_tile))
    return lax.ppermute(array, ("tm", "space"), pairs)


def shards(
    forcing, courant, innovation, obs_cells, obs_weight, obs_owner, channel_weight, channel_rinv
):
    fields, winds, down_edge, up_edge = run(
        rows_kernel,
        (
            struct(FIELDS * ROWS, LEVELS, WIDTH),
            struct(WINDS * ROWS, LEVELS, WIDTH),
            struct((WINDS + 1) * DOWN_EDGE, LEVELS, WIDTH),
            struct(WINDS * UP_EDGE, LEVELS, WIDTH),
        ),
        (forcing, courant),
        name="rows",
    )
    below = moved(fields, 0, 1)
    above = moved(winds, 0, -1)
    down_edge = moved(down_edge, 0, 2)
    up_edge = moved(up_edge, 0, -2)
    send, mixing = run(
        pack_kernel,
        (struct(TILES * 8, LANES), struct(LEVELS, LEVELS, LANES)),
        (
            innovation, obs_cells, obs_weight, obs_owner, channel_weight,
            channel_rinv.reshape(1, -1),
        ),
        name="pack",
    )
    received = lax.all_to_all(
        send.reshape(TILES, 8, LANES), "space", split_axis=0, concat_axis=0, tiled=True
    ).reshape(TILES * 8, LANES)

    pair_shapes = (struct(ROWS, LEVELS, WIDTH), struct(ROWS + EXTRA, LEVELS, WIDTH))
    own, extended = run(
        forward_local_kernel,
        pair_shapes,
        (fields, below, down_edge),
        name="forward_local",
    )
    before = (moved(own, 1, 0), moved(extended, 1, 1))
    own, extended = run(
        forward_pair_kernel,
        pair_shapes,
        (fields, below, down_edge, extended, *before),
        name="forward_pair",
    )
    pair = (moved(own, 2, 0), moved(extended, 2, 1))
    size = PIECES * LEVELS
    source, source_edge = run(
        forward_final_kernel,
        (struct(SUBS, ROWS, LEVELS, WIDTH), struct(2, LEVELS, WIDTH)),
        (
            fields, below, down_edge, *before, *pair, received, mixing,
        ),
        scratch=(
            pltpu.VMEM((SUBS, size, HALF), f32),
            pltpu.VMEM((LANES, LANES), f32),
            pltpu.VMEM((LANES, LANES), f32),
            pltpu.VMEM((2 * size, HALF), f32),
        ),
        name="forward_final",
    )

    source_above = moved(source, 0, -1)
    source_edge = moved(source_edge, 0, -2)
    own, extended = run(
        adjoint_local_kernel,
        pair_shapes,
        (source, source_above, source_edge, fields, above, up_edge),
        name="adjoint_local",
    )
    after = (moved(own, -1, 0), moved(extended, -1, -1))
    own, extended = run(
        adjoint_pair_kernel,
        pair_shapes,
        (fields, above, up_edge, extended, *after),
        name="adjoint_pair",
    )
    pair = (moved(own, -2, 0), moved(extended, -2, -1))
    gradient = run(
        adjoint_final_kernel,
        struct(SUBS, LEVELS, ROWS, WIDTH),
        (source, source_above, fields, above, up_edge, *after, *pair),
        name="adjoint_final",
    )
    return gradient


def solution(mesh):
    return jax.shard_map(
        shards,
        mesh=mesh,
        in_specs=(
            P("tm", None, "space", None),
            P(None, None, "space", None),
            P("tm", None, "space"),
            P("tm", None, "space"),
            P("tm", None, "space"),
            P("tm", "space", None),
            P(),
            P(),
        ),
        out_specs=P("tm", None, "space", None),
        check_vma=False,
    )
```

time: 579 us -> 108 us (0.19); the launches traced: 569 us -> 107 us
  starting transfers between devices: 224 us -> 49.2 us
  waiting for transfers between devices: 182 us -> 33.3 us
  matrix products: 122 us -> 0 us
  Pallas kernels: 0 us -> 21.5 us
  local copies, waits for them, and re-layouts: 24.4 us -> 2.94 us
  other arithmetic: 13.2 us -> 0 us
    ppermute x54 -> x14, starting transfers between devices: 196 us -> 37.5 us  [moved(): return lax.ppermute(array, ('tm', 'space'), pairs)]
    ppermute x54 -> x14, waiting for transfers between devices: 179 us -> 33.3 us  [moved(): return lax.ppermute(array, ('tm', 'space'), pairs)]
    dot_general x8 -> x0, matrix products: 122 us -> none  [the longest x2 62.9 us: one_block(): jnp.dot(flat_state, matrix.T, precision=highest, preferred_element_type=j...]
    pallas_call x0 -> x8, Pallas kernels: none -> 21.5 us  [run(): pl.pallas_call(kernel, out_shape=outputs, scratch_shapes=scratch, compile...]
    all_to_all x3 -> x1, starting transfers between devices: 28.2 us -> 11.6 us  [shards(): lax.all_to_all(send.reshape(TILES, 8, LANES), 'space', split_axis=0, conc...]
    slice x145 -> x0, local copies, waits for them, and re-layouts: 6.17 us -> none  [the longest x48 2.31 us: adjoint_step(): jnp.roll(wind_x * current, -1, axis=2)]
  transfers between devices with their start and end apart: 57 -> 15, of which waited for: 53 -> 6; matrix products, arithmetic and copies ran while one was open for 16% -> 0% of each run, Pallas kernels for 0% -> 4%
where the time goes in v1:
time: 108 us; the launch traced here: 107 us
  starting transfers between devices  49.2 us (46%)
  waiting for transfers between devices  33.3 us (31%)
  Pallas kernels  21.5 us (20%)
  local copies, waits for them, and re-layouts  2.94 us (3%)
    ppermute x14, starting transfers between devices, moved(): return lax.ppermute(array, ('tm', 'space'), pairs)  37.5 us
    ppermute x14, waiting for transfers between devices, moved(): return lax.ppermute(array, ('tm', 'space'), pairs)  33.3 us
    pallas_call x8, Pallas kernels, run(): pl.pallas_call(kernel, out_shape=outputs, scratch_shapes=scratch, compile...  21.5 us
    all_to_all x1, starting transfers between devices, shards(): lax.all_to_all(send.reshape(TILES, 8, LANES), 'space', split_axis=0, conc...  11.6 us
    unnamed x18, local copies, waits for them, and re-layouts  2.94 us
  transfers between devices with their start and end apart: 15, of which 6 were waited for; matrix products, arithmetic and copies ran while one was open for 0% of the time, Pallas kernels for 4%

profile of v1, /device:TPU:4, one launch (start us, length us, event | category | flops | bytes accessed | tf_op | source)
XLA Modules:
  0.0 107.2 jit_solution(1084340271478774977)
XLA Ops:
  0.0 1.0 copy-done
  2.1 2.1 %collective-permute-start = (f32[40,8,512]{2,1,0:T(8,128)S(1)}, f32[40,8,512]{2,1,0:T(8,128)S(1)}, u32[]{:S(2)}, u32[]{:S(2)}) collective-permute-start(f32[40,8,512]{2,1,0:T(8,128)S(1)} %get-tuple-element.21.fields), channel_id=1, source_target_pairs={{0,1},{1,2},{2,3},{3,4},{4,5},{5,6},{6,7},{7,8},{8,9},{9,10},{10,1... | collective-permute-start | bytes 1966088 | tf_op jit(solution)/shard_map/ppermute | solution.py:406
  4.2 3.8 %collective-permute-start.1 = (f32[9,8,512]{2,1,0:T(8,128)S(1)}, f32[9,8,512]{2,1,0:T(8,128)S(1)}, u32[]{:S(2)}, u32[]{:S(2)}) collective-permute-start(f32[9,8,512]{2,1,0:T(8,128)S(1)} %get-tuple-element.22), channel_id=1, source_target_pairs={{0,2},{1,3},{2,4},{3,5},{4,6},{5,7},{6,8},{7,9},{8,10},{9,11},{10,... | collective-permute-start | bytes 442376 | tf_op jit(solution)/shard_map/ppermute | solution.py:406
  9.0 3.6 %pack.1 = (f32[512,128]{1,0:T(8,128)}, f32[8,8,128]{2,1,0:T(8,128)S(1)}) custom-call(bf16[3,256,256]{2,1,0:T(8,128)(2,1)S(1)} %copy-done.1, s32[3,4,256]{2,1,0:T(4,128)S(1)} %copy-done.3, bf16[3,4,256]{2,1,0:T(4,128)(2,1)S(1)} %copy-done.4, s32[3,256,1]{2,1,0:T(8,128)S(1)} %copy.9.owner, f32[256,8]{1,0:T(8,128)S(1)} %copy.10.channel_weight, f32[1,256]{1,0:T(1,128)S(1)} %bitcast.4), custom_call_target="tpu_custom_call" | custom-call | flops 2000000 | bytes 423936 | tf_op jit(solution)/shard_map/pack/pallas_call | solution.py:389
  12.7 11.6 %all-to-all-start = ((f32[64,8,128]{2,1,0:T(8,128)}), f32[64,8,128]{2,1,0:T(8,128)S(1)}, u32[]{:S(2)}, u32[]{:S(2)}) async-start(f32[64,8,128]{2,1,0:T(8,128)} %bitcast.1), calls=%async_computation | async-start | bytes 524288 | tf_op jit(solution)/shard_map/all_to_all | solution.py:436
  24.8 3.2 %collective-permute-start.3 = (f32[12,8,512]{2,1,0:T(8,128)S(1)}, f32[12,8,512]{2,1,0:T(8,128)S(1)}, u32[]{:S(2)}, u32[]{:S(2)}) collective-permute-start(f32[12,8,512]{2,1,0:T(8,128)S(1)} %get-tuple-element.24.mine), channel_id=1, source_target_pairs={{0,65},{1,66},{2,67},{3,68},{4,69},{5,70},{6,71},{7,72},{8,73},{9,... | collective-permute-start | bytes 589832 | tf_op jit(solution)/shard_map/ppermute | solution.py:406
  28.1 3.5 %collective-permute-start.2 = (f32[8,8,512]{2,1,0:T(8,128)S(1)}, f32[8,8,512]{2,1,0:T(8,128)S(1)}, u32[]{:S(2)}, u32[]{:S(2)}) collective-permute-start(f32[8,8,512]{2,1,0:T(8,128)S(1)} %get-tuple-element.23), channel_id=1, source_target_pairs={{0,64},{1,65},{2,66},{3,67},{4,68},{5,69},{6,70},{7,71},{8,72},{9,... | collective-permute-start | bytes 393224 | tf_op jit(solution)/shard_map/ppermute | solution.py:406
  31.6 5.4 %collective-permute-done.2.before_own = f32[8,8,512]{2,1,0:T(8,128)S(1)} collective-permute-done((f32[8,8,512]{2,1,0:T(8,128)S(1)}, f32[8,8,512]{2,1,0:T(8,128)S(1)}, u32[]{:S(2)}, u32[]{:S(2)}) %collective-permute-start.2) | collective-permute-done | bytes 131104 | tf_op jit(solution)/shard_map/ppermute | solution.py:406
  37.5 5.6 %collective-permute-start.5 = (f32[12,8,512]{2,1,0:T(8,128)S(1)}, f32[12,8,512]{2,1,0:T(8,128)S(1)}, u32[]{:S(2)}, u32[]{:S(2)}) collective-permute-start(f32[12,8,512]{2,1,0:T(8,128)S(1)} %get-tuple-element.26), channel_id=1, source_target_pairs={{0,129},{1,130},{2,131},{3,132},{4,133},{5,134},{6,135},{7,136},{8... | collective-permute-start | bytes 589832 | tf_op jit(solution)/shard_map/ppermute | solution.py:406
  43.2 1.6 %collective-permute-start.4 = (f32[8,8,512]{2,1,0:T(8,128)S(1)}, f32[8,8,512]{2,1,0:T(8,128)S(1)}, u32[]{:S(2)}, u32[]{:S(2)}) collective-permute-start(f32[8,8,512]{2,1,0:T(8,128)S(1)} %get-tuple-element.25), channel_id=1, source_target_pairs={{0,128},{1,129},{2,130},{3,131},{4,132},{5,133},{6,134},{7,135},{8... | collective-permute-start | bytes 393224 | tf_op jit(solution)/shard_map/ppermute | solution.py:406
  44.7 6.5 %collective-permute-done.4.pair_own = f32[8,8,512]{2,1,0:T(8,128)S(1)} collective-permute-done((f32[8,8,512]{2,1,0:T(8,128)S(1)}, f32[8,8,512]{2,1,0:T(8,128)S(1)}, u32[]{:S(2)}, u32[]{:S(2)}) %collective-permute-start.4) | collective-permute-done | bytes 131104 | tf_op jit(solution)/shard_map/ppermute | solution.py:406
  51.2 14.0 %forward_final.1 = (f32[3,8,8,512]{3,2,1,0:T(8,128)S(1)}, f32[2,8,512]{2,1,0:T(8,128)S(1)}) custom-call(f32[40,8,512]{2,1,0:T(8,128)S(1)} %get-tuple-element.21.fields, f32[40,8,512]{2,1,0:T(8,128)S(1)} %collective-permute-done.below, f32[9,8,512]{2,1,0:T(8,128)S(1)} %collective-permute-done.1.edge, f32[8,8,512]{2,1,0:T(8,128)S(1)} %collective-permute-done.2.before_own, ...), custom_call_target="tpu_custom_call" | custom-call | flops 2000000 | bytes 2408448 | tf_op jit(solution)/shard_map/forward_final/pallas_call | solution.py:389
  65.2 2.3 %collective-permute-start.6 = (f32[3,8,8,512]{3,2,1,0:T(8,128)S(1)}, f32[3,8,8,512]{3,2,1,0:T(8,128)S(1)}, u32[]{:S(2)}, u32[]{:S(2)}) collective-permute-start(f32[3,8,8,512]{3,2,1,0:T(8,128)S(1)} %get-tuple-element.29.source), channel_id=1, source_target_pairs={{1,0},{2,1},{3,2},{4,3},{5,4},{6,5},{7,6},{8,7},{9,8},{10,9},{11,1... | collective-permute-start | bytes 1179656 | tf_op jit(solution)/shard_map/ppermute | solution.py:406
  67.5 3.5 %collective-permute-start.7 = (f32[16,8,512]{2,1,0:T(8,128)S(1)}, f32[16,8,512]{2,1,0:T(8,128)S(1)}, u32[]{:S(2)}, u32[]{:S(2)}) collective-permute-start(f32[16,8,512]{2,1,0:T(8,128)S(1)} %get-tuple-element.30), channel_id=1, source_target_pairs={{1,0},{2,1},{3,2},{4,3},{5,4},{6,5},{7,6},{8,7},{9,8},{10,9},{11,1... | collective-permute-start | bytes 786440 | tf_op jit(solution)/shard_map/ppermute | solution.py:406
  71.0 3.2 %collective-permute-start.8 = (f32[8,8,512]{2,1,0:T(8,128)S(1)}, f32[8,8,512]{2,1,0:T(8,128)S(1)}, u32[]{:S(2)}, u32[]{:S(2)}) collective-permute-start(f32[8,8,512]{2,1,0:T(8,128)S(1)} %get-tuple-element.31), channel_id=1, source_target_pairs={{2,0},{3,1},{4,2},{5,3},{6,4},{7,5},{8,6},{9,7},{10,8},{11,9},{12,... | collective-permute-start | bytes 393224 | tf_op jit(solution)/shard_map/ppermute | solution.py:406
  74.2 3.6 %collective-permute-start.9 = (f32[2,8,512]{2,1,0:T(8,128)S(1)}, f32[2,8,512]{2,1,0:T(8,128)S(1)}, u32[]{:S(2)}, u32[]{:S(2)}) collective-permute-start(f32[2,8,512]{2,1,0:T(8,128)S(1)} %get-tuple-element.32), channel_id=1, source_target_pairs={{2,0},{3,1},{4,2},{5,3},{6,4},{7,5},{8,6},{9,7},{10,8},{11,9},{12,... | collective-permute-start | bytes 98312 | tf_op jit(solution)/shard_map/ppermute | solution.py:406
  77.8 1.9 %collective-permute-done.8.edge = f32[8,8,512]{2,1,0:T(8,128)S(1)} collective-permute-done((f32[8,8,512]{2,1,0:T(8,128)S(1)}, f32[8,8,512]{2,1,0:T(8,128)S(1)}, u32[]{:S(2)}, u32[]{:S(2)}) %collective-permute-start.8) | collective-permute-done | bytes 131104 | tf_op jit(solution)/shard_map/ppermute | solution.py:406
  80.6 1.3 %collective-permute-start.11 = (f32[12,8,512]{2,1,0:T(8,128)S(1)}, f32[12,8,512]{2,1,0:T(8,128)S(1)}, u32[]{:S(2)}, u32[]{:S(2)}) collective-permute-start(f32[12,8,512]{2,1,0:T(8,128)S(1)} %get-tuple-element.34.mine), channel_id=1, source_target_pairs={{65,0},{66,1},{67,2},{68,3},{69,4},{70,5},{71,6},{72,7},{73,8},{74... | collective-permute-start | bytes 589832 | tf_op jit(solution)/shard_map/ppermute | solution.py:406
  81.9 1.3 %collective-permute-start.10 = (f32[8,8,512]{2,1,0:T(8,128)S(1)}, f32[8,8,512]{2,1,0:T(8,128)S(1)}, u32[]{:S(2)}, u32[]{:S(2)}) collective-permute-start(f32[8,8,512]{2,1,0:T(8,128)S(1)} %get-tuple-element.33), channel_id=1, source_target_pairs={{64,0},{65,1},{66,2},{67,3},{68,4},{69,5},{70,6},{71,7},{72,8},{73... | collective-permute-start | bytes 393224 | tf_op jit(solution)/shard_map/ppermute | solution.py:406
  83.2 8.4 %collective-permute-done.10.after_own = f32[8,8,512]{2,1,0:T(8,128)S(1)} collective-permute-done((f32[8,8,512]{2,1,0:T(8,128)S(1)}, f32[8,8,512]{2,1,0:T(8,128)S(1)}, u32[]{:S(2)}, u32[]{:S(2)}) %collective-permute-start.10) | collective-permute-done | bytes 131104 | tf_op jit(solution)/shard_map/ppermute | solution.py:406
  92.0 1.3 %collective-permute-start.13 = (f32[12,8,512]{2,1,0:T(8,128)S(1)}, f32[12,8,512]{2,1,0:T(8,128)S(1)}, u32[]{:S(2)}, u32[]{:S(2)}) collective-permute-start(f32[12,8,512]{2,1,0:T(8,128)S(1)} %get-tuple-element.36), channel_id=1, source_target_pairs={{129,0},{130,1},{131,2},{132,3},{133,4},{134,5},{135,6},{136,7},{1... | collective-permute-start | bytes 589832 | tf_op jit(solution)/shard_map/ppermute | solution.py:406
  93.3 1.3 %collective-permute-start.12 = (f32[8,8,512]{2,1,0:T(8,128)S(1)}, f32[8,8,512]{2,1,0:T(8,128)S(1)}, u32[]{:S(2)}, u32[]{:S(2)}) collective-permute-start(f32[8,8,512]{2,1,0:T(8,128)S(1)} %get-tuple-element.35), channel_id=1, source_target_pairs={{128,0},{129,1},{130,2},{131,3},{132,4},{133,5},{134,6},{135,7},{1... | collective-permute-start | bytes 393224 | tf_op jit(solution)/shard_map/ppermute | solution.py:406
  94.6 10.8 %collective-permute-done.12.pair_own = f32[8,8,512]{2,1,0:T(8,128)S(1)} collective-permute-done((f32[8,8,512]{2,1,0:T(8,128)S(1)}, f32[8,8,512]{2,1,0:T(8,128)S(1)}, u32[]{:S(2)}, u32[]{:S(2)}) %collective-permute-start.12) | collective-permute-done | bytes 131104 | tf_op jit(solution)/shard_map/ppermute | solution.py:406
  105.5 1.7 %adjoint_final.1 = f32[3,8,8,512]{3,2,1,0:T(8,128)} custom-call(f32[3,8,8,512]{3,2,1,0:T(8,128)S(1)} %get-tuple-element.29.source, f32[3,8,8,512]{3,2,1,0:T(8,128)S(1)} %collective-permute-done.6.source_above, f32[40,8,512]{2,1,0:T(8,128)S(1)} %get-tuple-element.21.fields, f32[16,8,512]{2,1,0:T(8,128)S(1)} %collective-permute-done.7.above, ...), custom_call_target="tpu_custom_call" | custom-call | flops 2000000 | bytes 2490368 | tf_op jit(solution)/shard_map/adjoint_final/pallas_call | solution.py:389
  (32 shorter events, 4.4 us)
Async XLA Ops:
  0.0 1.0 copy-start
  1.0 0.9 copy-start.2
  1.9 6.0 %copy-start.6 = (f32[256,8]{0,1:T(8,128)S(1)}, f32[256,8]{0,1:T(8,128)}, u32[]{:S(2)}) copy-start(f32[256,8]{0,1:T(8,128)} %param.14) | copy-start | bytes 24580
  1.9 6.2 %copy-start.7 = (s32[3,256,1]{1,2,0:T(1,128)S(1)}, s32[3,256,1]{1,2,0:T(1,128)}, u32[]{:S(2)}) copy-start(s32[3,256,1]{1,2,0:T(1,128)} %param.13) | copy-start | bytes 9220
  2.1 6.3 %copy-start.1 = (bf16[3,256,256]{2,1,0:T(8,128)(2,1)S(1)}, bf16[3,256,256]{2,1,0:T(8,128)(2,1)}, u32[]{:S(2)}) copy-start(bf16[3,256,256]{2,1,0:T(8,128)(2,1)} %innovation.1) | copy-start | bytes 1179652
  2.1 22.2 %collective-permute-start = (f32[40,8,512]{2,1,0:T(8,128)S(1)}, f32[40,8,512]{2,1,0:T(8,128)S(1)}, u32[]{:S(2)}, u32[]{:S(2)}) collective-permute-start(f32[40,8,512]{2,1,0:T(8,128)S(1)} %get-tuple-element.21.fields), channel_id=1, source_target_pairs={{0,1},{1,2},{2,3},{3,4},{4,5},{5,6},{6,7},{7,8},{8,9},{9,10},{10,1... | collective-permute-start | bytes 1966088 | tf_op jit(solution)/shard_map/ppermute | solution.py:406
  4.2 20.2 %collective-permute-start.1 = (f32[9,8,512]{2,1,0:T(8,128)S(1)}, f32[9,8,512]{2,1,0:T(8,128)S(1)}, u32[]{:S(2)}, u32[]{:S(2)}) collective-permute-start(f32[9,8,512]{2,1,0:T(8,128)S(1)} %get-tuple-element.22), channel_id=1, source_target_pairs={{0,2},{1,3},{2,4},{3,5},{4,6},{5,7},{6,8},{7,9},{8,10},{9,11},{10,... | collective-permute-start | bytes 442376 | tf_op jit(solution)/shard_map/ppermute | solution.py:406
  8.1 0.7 copy-start.3
  8.2 0.7 copy-start.4
  8.4 0.7 copy-start.5
  12.7 32.1 %all-to-all-start = ((f32[64,8,128]{2,1,0:T(8,128)}), f32[64,8,128]{2,1,0:T(8,128)S(1)}, u32[]{:S(2)}, u32[]{:S(2)}) async-start(f32[64,8,128]{2,1,0:T(8,128)} %bitcast.1), calls=%async_computation | async-start | bytes 524288 | tf_op jit(solution)/shard_map/all_to_all | solution.py:436
  24.8 12.1 %collective-permute-start.3 = (f32[12,8,512]{2,1,0:T(8,128)S(1)}, f32[12,8,512]{2,1,0:T(8,128)S(1)}, u32[]{:S(2)}, u32[]{:S(2)}) collective-permute-start(f32[12,8,512]{2,1,0:T(8,128)S(1)} %get-tuple-element.24.mine), channel_id=1, source_target_pairs={{0,65},{1,66},{2,67},{3,68},{4,69},{5,70},{6,71},{7,72},{8,73},{9,... | collective-permute-start | bytes 589832 | tf_op jit(solution)/shard_map/ppermute | solution.py:406
  28.1 8.9 %collective-permute-start.2 = (f32[8,8,512]{2,1,0:T(8,128)S(1)}, f32[8,8,512]{2,1,0:T(8,128)S(1)}, u32[]{:S(2)}, u32[]{:S(2)}) collective-permute-start(f32[8,8,512]{2,1,0:T(8,128)S(1)} %get-tuple-element.23), channel_id=1, source_target_pairs={{0,64},{1,65},{2,66},{3,67},{4,68},{5,69},{6,70},{7,71},{8,72},{9,... | collective-permute-start | bytes 393224 | tf_op jit(solution)/shard_map/ppermute | solution.py:406
  37.5 13.7 %collective-permute-start.5 = (f32[12,8,512]{2,1,0:T(8,128)S(1)}, f32[12,8,512]{2,1,0:T(8,128)S(1)}, u32[]{:S(2)}, u32[]{:S(2)}) collective-permute-start(f32[12,8,512]{2,1,0:T(8,128)S(1)} %get-tuple-element.26), channel_id=1, source_target_pairs={{0,129},{1,130},{2,131},{3,132},{4,133},{5,134},{6,135},{7,136},{8... | collective-permute-start | bytes 589832 | tf_op jit(solution)/shard_map/ppermute | solution.py:406
  43.2 8.1 %collective-permute-start.4 = (f32[8,8,512]{2,1,0:T(8,128)S(1)}, f32[8,8,512]{2,1,0:T(8,128)S(1)}, u32[]{:S(2)}, u32[]{:S(2)}) collective-permute-start(f32[8,8,512]{2,1,0:T(8,128)S(1)} %get-tuple-element.25), channel_id=1, source_target_pairs={{0,128},{1,129},{2,130},{3,131},{4,132},{5,133},{6,134},{7,135},{8... | collective-permute-start | bytes 393224 | tf_op jit(solution)/shard_map/ppermute | solution.py:406
  65.2 14.9 %collective-permute-start.6 = (f32[3,8,8,512]{3,2,1,0:T(8,128)S(1)}, f32[3,8,8,512]{3,2,1,0:T(8,128)S(1)}, u32[]{:S(2)}, u32[]{:S(2)}) collective-permute-start(f32[3,8,8,512]{3,2,1,0:T(8,128)S(1)} %get-tuple-element.29.source), channel_id=1, source_target_pairs={{1,0},{2,1},{3,2},{4,3},{5,4},{6,5},{7,6},{8,7},{9,8},{10,9},{11,1... | collective-permute-start | bytes 1179656 | tf_op jit(solution)/shard_map/ppermute | solution.py:406
  67.5 12.2 %collective-permute-start.7 = (f32[16,8,512]{2,1,0:T(8,128)S(1)}, f32[16,8,512]{2,1,0:T(8,128)S(1)}, u32[]{:S(2)}, u32[]{:S(2)}) collective-permute-start(f32[16,8,512]{2,1,0:T(8,128)S(1)} %get-tuple-element.30), channel_id=1, source_target_pairs={{1,0},{2,1},{3,2},{4,3},{5,4},{6,5},{7,6},{8,7},{9,8},{10,9},{11,1... | collective-permute-start | bytes 786440 | tf_op jit(solution)/shard_map/ppermute | solution.py:406
  71.0 8.7 %collective-permute-start.8 = (f32[8,8,512]{2,1,0:T(8,128)S(1)}, f32[8,8,512]{2,1,0:T(8,128)S(1)}, u32[]{:S(2)}, u32[]{:S(2)}) collective-permute-start(f32[8,8,512]{2,1,0:T(8,128)S(1)} %get-tuple-element.31), channel_id=1, source_target_pairs={{2,0},{3,1},{4,2},{5,3},{6,4},{7,5},{8,6},{9,7},{10,8},{11,9},{12,... | collective-permute-start | bytes 393224 | tf_op jit(solution)/shard_map/ppermute | solution.py:406
  74.2 5.9 %collective-permute-start.9 = (f32[2,8,512]{2,1,0:T(8,128)S(1)}, f32[2,8,512]{2,1,0:T(8,128)S(1)}, u32[]{:S(2)}, u32[]{:S(2)}) collective-permute-start(f32[2,8,512]{2,1,0:T(8,128)S(1)} %get-tuple-element.32), channel_id=1, source_target_pairs={{2,0},{3,1},{4,2},{5,3},{6,4},{7,5},{8,6},{9,7},{10,8},{11,9},{12,... | collective-permute-start | bytes 98312 | tf_op jit(solution)/shard_map/ppermute | solution.py:406
  80.6 11.0 %collective-permute-start.11 = (f32[12,8,512]{2,1,0:T(8,128)S(1)}, f32[12,8,512]{2,1,0:T(8,128)S(1)}, u32[]{:S(2)}, u32[]{:S(2)}) collective-permute-start(f32[12,8,512]{2,1,0:T(8,128)S(1)} %get-tuple-element.34.mine), channel_id=1, source_target_pairs={{65,0},{66,1},{67,2},{68,3},{69,4},{70,5},{71,6},{72,7},{73,8},{74... | collective-permute-start | bytes 589832 | tf_op jit(solution)/shard_map/ppermute | solution.py:406
  81.9 9.7 %collective-permute-start.10 = (f32[8,8,512]{2,1,0:T(8,128)S(1)}, f32[8,8,512]{2,1,0:T(8,128)S(1)}, u32[]{:S(2)}, u32[]{:S(2)}) collective-permute-start(f32[8,8,512]{2,1,0:T(8,128)S(1)} %get-tuple-element.33), channel_id=1, source_target_pairs={{64,0},{65,1},{66,2},{67,3},{68,4},{69,5},{70,6},{71,7},{72,8},{73... | collective-permute-start | bytes 393224 | tf_op jit(solution)/shard_map/ppermute | solution.py:406
  92.0 13.4 %collective-permute-start.13 = (f32[12,8,512]{2,1,0:T(8,128)S(1)}, f32[12,8,512]{2,1,0:T(8,128)S(1)}, u32[]{:S(2)}, u32[]{:S(2)}) collective-permute-start(f32[12,8,512]{2,1,0:T(8,128)S(1)} %get-tuple-element.36), channel_id=1, source_target_pairs={{129,0},{130,1},{131,2},{132,3},{133,4},{134,5},{135,6},{136,7},{1... | collective-permute-start | bytes 589832 | tf_op jit(solution)/shard_map/ppermute | solution.py:406
  93.3 12.1 %collective-permute-start.12 = (f32[8,8,512]{2,1,0:T(8,128)S(1)}, f32[8,8,512]{2,1,0:T(8,128)S(1)}, u32[]{:S(2)}, u32[]{:S(2)}) collective-permute-start(f32[8,8,512]{2,1,0:T(8,128)S(1)} %get-tuple-element.35), channel_id=1, source_target_pairs={{128,0},{129,1},{130,2},{131,3},{132,4},{133,5},{134,6},{135,7},{1... | collective-permute-start | bytes 393224 | tf_op jit(solution)/shard_map/ppermute | solution.py:406

commit v2 on v1

v2 whole, which is shorter than its diff:
```python
import functools

import jax
import jax.numpy as jnp
from jax import lax
from jax.experimental import pallas as pl
from jax.experimental.pallas import tpu as pltpu
from jax.sharding import PartitionSpec as P

LEVELS = 8
ROWS = 8
WIDTH = 512
SUBS = 3
TILES = 64
PARTS = 4
RECORDS = 256
CORNERS = 4
HALF = 256
PIECES = WIDTH // HALF * ROWS
CHUNKS = 8
LANES = 128

f32 = jnp.float32
bf16 = jnp.bfloat16
highest = lax.Precision.HIGHEST


def struct(*shape, dtype=f32):
    return jax.ShapeDtypeStruct(shape, dtype)


def split(value):
    top = value.astype(bf16)
    return top, (value - top.astype(f32)).astype(bf16)


LEVEL_TOP = 32766.0
SCALE_BITS = 22
SCALE_BIAS = 256
WIND_MIDDLE = 0.25
WIND_REACH = 0.21


def nearest(value):
    return jnp.floor(value + 0.5).astype(jnp.int32)


def join(first, second):
    return jnp.left_shift(first, 16) | (second & 0xFFFF)


def parted(both):
    return jnp.right_shift(both, 16), jnp.right_shift(jnp.left_shift(both, 16), 16)


def scale_of(code):
    exponent = (jnp.right_shift(code, SCALE_BITS) - SCALE_BIAS).astype(f32)
    mantissa = (code & ((1 << SCALE_BITS) - 1)).astype(f32) * (0.5 ** 20)
    return mantissa * jnp.exp2(exponent)


def encode(values, message):
    count = len(values)
    lane = lax.broadcasted_iota(jnp.int32, (LEVELS, LANES), 1)
    largest = jnp.full((LEVELS, LANES), 1e-30, f32)
    for number, value in enumerate(values):
        top = jnp.max(jnp.abs(value), axis=1, keepdims=True)
        largest = jnp.where(lane == number, jnp.maximum(top, 1e-30), largest)
    exponent = jnp.floor(jnp.log2(largest))
    mantissa = (largest * jnp.exp2(-exponent) * 2.0 ** 20).astype(jnp.int32) + 16
    code = jnp.left_shift(exponent.astype(jnp.int32) + SCALE_BIAS, SCALE_BITS) + mantissa
    factor = LEVEL_TOP / scale_of(code)
    half = count // 2
    whole = [nearest(value * factor[:, n : n + 1]) for n, value in enumerate(values)]
    for number in range(half):
        message[number] = join(whole[number], whole[number + half])
    message[half] = jnp.concatenate([code] * (WIDTH // LANES), axis=1)


def decode(message, count):
    half = count // 2
    factor = scale_of(message[half][:, :LANES]) * (1.0 / LEVEL_TOP)
    values = [None] * count
    for number in range(half):
        pair = parted(message[number])
        for place, value in zip((number, number + half), pair):
            values[place] = value.astype(f32) * factor[:, place : place + 1]
    return values


def encode_wind(first, second):
    steps = LEVEL_TOP / WIND_REACH
    return join(nearest((first - WIND_MIDDLE) * steps), nearest((second - WIND_MIDDLE) * steps))


def decode_wind(both):
    step = WIND_REACH / LEVEL_TOP
    return [value.astype(f32) * step + WIND_MIDDLE for value in parted(both)]


def forward_step(current, wind_x, wind_y, low):
    result = {}
    for row in range(low + 1, ROWS):
        here = current[row]
        left = pltpu.roll(here, 1, 1)
        result[row] = (
            here - wind_x(row) * (here - left) - wind_y(row) * (here - current[row - 1])
        )
    return result


def adjoint_step(current, wind_x, wind_y, high):
    result = {}
    for row in range(high - 1):
        here = current[row]
        along, across = wind_x(row), wind_y(row)
        result[row] = (
            here * (1.0 - along - across)
            + pltpu.roll(along * here, WIDTH - 1, 1)
            + wind_y(row + 1) * current[row + 1]
        )
    return result


def forward_steps(current, winds, low, count):
    for _ in range(count):
        current = forward_step(current, winds[0], winds[1], low)
        low += 1
    return current, low


def adjoint_steps(current, winds, high, count):
    for _ in range(count):
        current = adjoint_step(current, winds[0], winds[1], high)
        high -= 1
    return current, high


WINDS = 2
FIELDS = WINDS + SUBS
DOWN_EDGE = 3
UP_EDGE = 4
EXTRA = 4
OWN_MESSAGE = ROWS // 2 + 1
EXTENDED_MESSAGE = (ROWS + EXTRA) // 2 + 1
FORCE_MESSAGE = SUBS * ROWS // 2 + 1


def lower_winds(winds, winds_below, edge):
    def reader(field):
        def read(row):
            if row >= 0:
                return winds[field * ROWS + row]
            if row >= -ROWS:
                return winds_below[field * ROWS + row + ROWS]
            return edge[field * DOWN_EDGE + row + ROWS + DOWN_EDGE]

        return read

    return [reader(field) for field in range(WINDS)]


def upper_winds(winds, winds_above, edge):
    def reader(field):
        def read(row):
            if row < ROWS:
                return winds[field * ROWS + row]
            if row < 2 * ROWS:
                return winds_above[field * ROWS + row - ROWS]
            return edge[field * UP_EDGE + row - 2 * ROWS]

        return read

    return [reader(field) for field in range(WINDS)]


def lower_forces(forces, forces_below):
    def reader(sub):
        def read(row):
            if row >= 0:
                return forces[sub * ROWS + row]
            return forces_below[sub * ROWS + row + ROWS]

        return read

    return [reader(sub) for sub in range(SUBS)]


def add_rows(current, other, low, high):
    return {row: current[row] + other(row) for row in range(low, high)}


def fetch(pairs, sems):
    copies = [
        pltpu.make_async_copy(source, target, sems.at[number])
        for number, (source, target) in enumerate(pairs)
    ]
    for copy in copies:
        copy.start()
    return copies


def rows_kernel(
    forcing_far, courant_far, winds, forces, below, down_edge, forcing, courant, sems
):
    copies = fetch(
        [(courant_far.at[field], courant.at[field]) for field in range(WINDS)]
        + [(forcing_far.at[sub], forcing.at[sub]) for sub in range(SUBS)],
        sems,
    )
    for copy in copies[:WINDS]:
        copy.wait()
    for field in range(WINDS):
        winds[pl.ds(field * ROWS, ROWS)] = jnp.swapaxes(courant[field], 0, 1)
    encode_winds(winds, range(ROWS), below, 0)
    encode_winds(winds, range(ROWS - DOWN_EDGE, ROWS), down_edge, 0)
    rows = []
    for sub in range(SUBS):
        copies[WINDS + sub].wait()
        turned = jnp.swapaxes(forcing[sub], 0, 1)
        forces[pl.ds(sub * ROWS, ROWS)] = turned
        rows += [turned[row] for row in range(ROWS)]
    encode(rows, below.at[pl.ds(ROWS, FORCE_MESSAGE)])
    encode(rows[ROWS - 2 : ROWS], down_edge.at[pl.ds(DOWN_EDGE, 2)])


def encode_winds(winds, rows, message, start):
    for number, row in enumerate(rows):
        message[start + number] = encode_wind(winds[row], winds[ROWS + row])


def unpack_winds(message, rows, result, start=0):
    for row in range(rows):
        first, second = decode_wind(message[start + row])
        result[row] = first
        result[rows + row] = second


def choose_kernel(
    innovation_far, cells_far, weight_far, owner_far, channel_far, rinv_far,
    chosen, target, mixing,
    innovation, cells, weight, owner, channel_weight, rinv, sems,
):
    copies = fetch(
        [
            (channel_far, channel_weight), (rinv_far, rinv), (owner_far, owner),
            (cells_far, cells), (weight_far, weight),
        ]
        + [(innovation_far.at[sub], innovation.at[sub]) for sub in range(SUBS)],
        sems,
    )
    for copy in copies:
        copy.wait()
    sub_id = lax.broadcasted_iota(jnp.int32, (RECORDS, RECORDS), 0)
    lane_id = lax.broadcasted_iota(jnp.int32, (RECORDS, RECORDS), 1)
    not_later = lane_id <= sub_id

    scaled = channel_weight[...] * (rinv[...] * rinv[...])
    matrix = lax.dot_general(
        scaled, channel_weight[...], (((1,), (1,)), ((), ())),
        precision=highest, preferred_element_type=f32,
    )
    for level in range(LEVELS):
        mixing[level] = jnp.broadcast_to(matrix[:, level : level + 1], (LEVELS, LANES))
    top = scaled.astype(bf16)
    rest = scaled - top.astype(f32)
    middle = rest.astype(bf16)
    low = (rest - middle.astype(f32)).astype(bf16)

    spread_row = lax.broadcasted_iota(jnp.int32, (2 * LEVELS, LANES), 0)
    spread_lane = lax.broadcasted_iota(jnp.int32, (2 * LEVELS, LANES), 1)
    repeat = (
        (spread_lane // 64 == spread_row // LEVELS) & (spread_lane % LEVELS == spread_row % LEVELS)
    ).astype(f32)
    slot_lane = lax.broadcasted_iota(jnp.int32, (RECORDS, LANES), 1)
    slot_rank = ((slot_lane % 64) // LEVELS) * 2
    tile_id = lax.broadcasted_iota(jnp.int32, (TILES, RECORDS), 0)
    ones = jnp.ones((RECORDS, LANES), bf16)
    for sub in range(SUBS):
        data = innovation[sub]
        projected = (
            jnp.dot(top, data, preferred_element_type=f32)
            + jnp.dot(middle, data, preferred_element_type=f32)
            + jnp.dot(low, data, preferred_element_type=f32)
        )
        payload = jnp.concatenate(
            [cells[sub].astype(f32), weight[sub].astype(f32), projected], axis=0
        )
        owner_row = owner[sub]
        owner_rows = jnp.broadcast_to(owner_row, (RECORDS, RECORDS))
        earlier = jnp.where((owner_rows.T == owner_rows) & not_later, 1.0, 0.0).astype(bf16)
        rank = jnp.dot(earlier, ones, preferred_element_type=f32).astype(jnp.int32) - 1
        repeated = lax.dot_general(
            payload, repeat, (((0,), (0,)), ((), ())),
            precision=highest, preferred_element_type=f32,
        )
        target[sub] = (tile_id == owner_row).astype(f32)
        for half in range(2):
            chosen[2 * sub + half] = jnp.where(rank == slot_rank + half, repeated, 0.0)


def place_kernel(chosen, target, after, send):
    del after
    for sub in range(SUBS):
        for half in range(2):
            send[pl.ds(2 * sub + half, TILES, stride=8), :] = jnp.dot(
                target[sub], chosen[2 * sub + half],
                precision=highest, preferred_element_type=f32,
            )
    for spare in range(2 * SUBS, 8):
        send[pl.ds(spare, TILES, stride=8), :] = jnp.zeros((TILES, LANES), f32)


def stencil_kernel(received, slots, stencil, pieces):
    rows_id = lax.broadcasted_iota(jnp.int32, (HALF, LANES), 0)

    def one_sub(sub, _):
        for half in range(2):
            pieces[pl.ds(half * TILES, TILES), :] = received[
                pl.ds(2 * sub + half, TILES, stride=8), :
            ]
        slots[sub] = pieces[...].T
        for chunk in range(CHUNKS):
            record = slots[sub, pl.ds(chunk * LEVELS, LEVELS), :]
            column = record.astype(jnp.int32) & (HALF - 1)
            for corner in range(CORNERS):
                stencil[sub, chunk, :, corner * LANES : (corner + 1) * LANES] = jnp.where(
                    rows_id == column[corner : corner + 1],
                    record[CORNERS + corner : CORNERS + corner + 1],
                    0.0,
                ).astype(bf16)
        return 0

    lax.fori_loop(0, SUBS, one_sub, 0)


def observe(slots, stencil, mixing, states, found, spread):
    size = PIECES * LEVELS

    def one_sub(sub, _):
        top, low = split(states[sub])
        left = jnp.concatenate([top, low], axis=0)
        for chunk in range(CHUNKS):
            found[chunk] = jnp.dot(left, stencil[sub, chunk], preferred_element_type=f32)
        for chunk in range(CHUNKS):
            record = slots[sub, pl.ds(chunk * LEVELS, LEVELS), :]
            adjoint = -slots[sub, pl.ds(TILES + chunk * LEVELS, LEVELS), :]
            piece = jnp.right_shift(record.astype(jnp.int32), 8)
            sums = []
            wanted = []
            for corner in range(CORNERS):
                wanted.append(jnp.broadcast_to(piece[corner : corner + 1], (LEVELS, LANES)))
                part = pl.ds(corner * LANES, LANES)
                value = None
                for number in range(PIECES):
                    both = (
                        found[chunk, pl.ds(number * LEVELS, LEVELS), part]
                        + found[chunk, pl.ds(size + number * LEVELS, LEVELS), part]
                    )
                    value = both if value is None else jnp.where(wanted[corner] == number, both, value)
                sums.append(value)
            values = (sums[0] + sums[1]) + (sums[2] + sums[3])
            for level in range(LEVELS):
                adjoint = adjoint + mixing[level] * values[level : level + 1]
            first, second = split(adjoint)
            sources = first.astype(f32), second.astype(f32)
            for corner in range(CORNERS):
                part = pl.ds(corner * LANES, LANES)
                for place, source in enumerate(sources):
                    spread[chunk, pl.ds(place * size, size), part] = jnp.concatenate(
                        [jnp.where(wanted[corner] == number, source, 0.0) for number in range(PIECES)],
                        axis=0,
                    ).astype(bf16)
        total = jnp.zeros((2 * size, HALF), f32)
        for chunk in range(CHUNKS):
            total = total + lax.dot_general(
                spread[chunk], stencil[sub, chunk], (((1,), (1,)), ((), ())),
                preferred_element_type=f32,
            )
        states[sub] = total[:size] + total[size:]
        return 0

    lax.fori_loop(0, SUBS, one_sub, 0)


def forward_local_kernel(
    winds, forces, below, down_edge,
    own, extended, mine, winds_below, lower_edge, forces_below,
):
    unpack_winds(below, ROWS, winds_below)
    unpack_winds(down_edge, DOWN_EDGE, lower_edge)
    rows = decode(below.at[pl.ds(ROWS, FORCE_MESSAGE)], SUBS * ROWS)
    for number, row in enumerate(rows):
        forces_below[number] = row
    edge = decode(down_edge.at[pl.ds(DOWN_EDGE, 2)], 2)
    across = lower_winds(winds, winds_below, lower_edge)
    forced = lower_forces(forces, forces_below)
    low = -(ROWS + 2)
    current = {row: edge[row - low] for row in (low, low + 1)}
    for row in range(-ROWS, ROWS):
        current[row] = forced[0](row)
    current, low = forward_steps(current, across, low, 2)
    for sub in range(1, SUBS):
        current = add_rows(current, forced[sub], low, ROWS)
        current, low = forward_steps(current, across, low, 2)
    listed = [current[row] for row in range(-EXTRA, ROWS)]
    for number, row in enumerate(listed):
        mine[number] = row
    encode(listed[EXTRA:], own)
    encode(listed, extended)


def lower_state(own, extended, low):
    here = decode(own, ROWS)
    under = decode(extended, ROWS + EXTRA)
    return {row: here[row] if row >= 0 else under[row + ROWS + EXTRA] for row in range(low, ROWS)}


def forward_pair_kernel(
    winds, winds_below, lower_edge, mine, before_own, before_extended, own, extended
):
    across = lower_winds(winds, winds_below, lower_edge)
    low = -(ROWS + 2)
    current, low = forward_steps(lower_state(before_own, before_extended, low), across, low, 6)
    listed = [current[row] + mine[row + EXTRA] for row in range(-EXTRA, ROWS)]
    encode(listed[EXTRA:], own)
    encode(listed, extended)


def forward_final_kernel(
    winds, forces, winds_below, lower_edge, forces_below,
    before_own, before_extended, pair_own, pair_extended, slots, stencil, mixing,
    result, result_above, result_edge,
    states, found, spread,
):
    across = lower_winds(winds, winds_below, lower_edge)
    forced = lower_forces(forces, forces_below)
    low = -(ROWS + EXTRA)
    current, low = forward_steps(lower_state(pair_own, pair_extended, low), across, low, 6)
    before = lower_state(before_own, before_extended, low)
    current = {row: current[row] + before[row] for row in current}
    for sub in range(SUBS):
        current = add_rows(current, forced[sub], low, ROWS)
        current, low = forward_steps(current, across, low, 2)
        for row in range(ROWS):
            for half in range(2):
                place = (2 * row + half) * LEVELS
                states[sub, place : place + LEVELS, :] = current[row][
                    :, half * HALF : (half + 1) * HALF
                ]
    observe(slots, stencil, mixing, states, found, spread)
    listed = []
    for sub in range(SUBS):
        for row in range(ROWS):
            places = [(2 * row + half) * LEVELS for half in range(2)]
            value = jnp.concatenate(
                [states[sub, place : place + LEVELS, :] for place in places], axis=1
            )
            result[sub, row] = value
            listed.append(value)
    encode(listed, result_above.at[pl.ds(0, FORCE_MESSAGE)])
    encode_winds(winds, range(ROWS), result_above, FORCE_MESSAGE)
    encode(listed[-ROWS : 2 - ROWS], result_edge.at[pl.ds(0, 2)])
    encode_winds(winds, range(UP_EDGE), result_edge, 2)


def adjoint_local_kernel(
    source, source_above, source_edge, winds,
    own, extended, mine, unpacked, winds_above, upper_edge,
):
    unpack_winds(source_above, ROWS, winds_above, FORCE_MESSAGE)
    unpack_winds(source_edge, UP_EDGE, upper_edge, 2)
    across = upper_winds(winds, winds_above, upper_edge)
    high = 2 * ROWS + 2
    above = decode(source_above.at[pl.ds(0, FORCE_MESSAGE)], SUBS * ROWS)
    edge = decode(source_edge.at[pl.ds(0, 2)], 2)
    for number, row in enumerate(above):
        unpacked[number] = row

    def source_row(sub):
        return lambda row: source[sub, row] if row < ROWS else unpacked[sub * ROWS + row - ROWS]

    current = {row: source_row(SUBS - 1)(row) for row in range(2 * ROWS)}
    for number, row in enumerate(edge):
        current[2 * ROWS + number] = row
    current, high = adjoint_steps(current, across, high, 2)
    for sub in reversed(range(SUBS - 1)):
        current = add_rows(current, source_row(sub), 0, high)
        current, high = adjoint_steps(current, across, high, 2)
    listed = [current[row] for row in range(ROWS + EXTRA)]
    for number, row in enumerate(listed):
        mine[number] = row
    encode(listed[:ROWS], own)
    encode(listed, extended)


def upper_state(own, extended, high):
    here = decode(own, ROWS)
    over = decode(extended, ROWS + EXTRA)
    return {row: here[row] if row < ROWS else over[row - ROWS] for row in range(high)}


def adjoint_pair_kernel(
    winds, winds_above, upper_edge, mine, after_own, after_extended, own, extended
):
    across = upper_winds(winds, winds_above, upper_edge)
    high = 2 * ROWS + 2
    current, high = adjoint_steps(upper_state(after_own, after_extended, high), across, high, 6)
    listed = [current[row] + mine[row] for row in range(ROWS + EXTRA)]
    encode(listed[:ROWS], own)
    encode(listed, extended)


def adjoint_final_kernel(
    source, unpacked, winds, winds_above, upper_edge,
    after_own, after_extended, pair_own, pair_extended, gradient,
):
    across = upper_winds(winds, winds_above, upper_edge)
    high = 2 * ROWS + EXTRA
    current, high = adjoint_steps(upper_state(pair_own, pair_extended, high), across, high, 6)
    after = upper_state(after_own, after_extended, high)
    current = {row: current[row] + after[row] for row in current}

    def source_row(sub):
        return lambda row: source[sub, row] if row < ROWS else unpacked[sub * ROWS + row - ROWS]

    for sub in reversed(range(SUBS)):
        current = add_rows(current, source_row(sub), 0, high)
        current, high = adjoint_steps(current, across, high, 2)
        gradient[sub] = jnp.swapaxes(jnp.stack([current[row] for row in range(ROWS)]), 0, 1)


def run(kernel, outputs, arguments, scratch=(), name=None, flops=2_000_000, far=False):
    size = sum(a.size * a.dtype.itemsize for a in arguments)
    place = pltpu.HBM if far else pltpu.VMEM
    if far:
        arguments = [pltpu.with_memory_space_constraint(a, pltpu.HBM) for a in arguments]
    return pl.pallas_call(
        kernel,
        out_shape=outputs,
        in_specs=[pl.BlockSpec(memory_space=place)] * len(arguments),
        scratch_shapes=scratch,
        compiler_params=pltpu.CompilerParams(vmem_limit_bytes=40 * 1024 * 1024),
        cost_estimate=pl.CostEstimate(flops=flops, bytes_accessed=size, transcendentals=0),
        name=name,
    )(*arguments)


def moved(array, parts, tiles):
    pairs = []
    for part in range(PARTS):
        for tile in range(TILES):
            to_part, to_tile = part + parts, tile + tiles
            if 0 <= to_part < PARTS and 0 <= to_tile < TILES:
                pairs.append((part * TILES + tile, to_part * TILES + to_tile))
    return lax.ppermute(array, ("tm", "space"), pairs)


def shards(
    forcing, courant, innovation, obs_cells, obs_weight, obs_owner, channel_weight, channel_rinv
):
    message = functools.partial(struct, dtype=jnp.int32)
    winds, forces, below, down_edge = run(
        rows_kernel,
        (
            struct(WINDS * ROWS, LEVELS, WIDTH),
            struct(SUBS * ROWS, LEVELS, WIDTH),
            message(ROWS + FORCE_MESSAGE, LEVELS, WIDTH),
            message(DOWN_EDGE + 2, LEVELS, WIDTH),
        ),
        (forcing, courant),
        scratch=(
            pltpu.VMEM(forcing.shape, f32),
            pltpu.VMEM(courant.shape, f32),
            pltpu.SemaphoreType.DMA((FIELDS,)),
        ),
        name="rows",
        far=True,
    )
    below = moved(below, 0, 1)
    down_edge = moved(down_edge, 0, 2)
    records = (
        innovation, obs_cells, obs_weight, jnp.swapaxes(obs_owner, 1, 2),
        channel_weight.T, channel_rinv.reshape(1, -1),
    )
    chosen, target, mixing = run(
        choose_kernel,
        (
            struct(2 * SUBS, RECORDS, LANES),
            struct(SUBS, TILES, RECORDS),
            struct(LEVELS, LEVELS, LANES),
        ),
        records,
        scratch=(
            *[pltpu.VMEM(array.shape, array.dtype) for array in records],
            pltpu.SemaphoreType.DMA((len(records) + SUBS - 1,)),
        ),
        name="choose",
        far=True,
    )
    below, down_edge, chosen, target = lax.optimization_barrier(
        (below, down_edge, chosen, target)
    )
    pair_shapes = (
        message(OWN_MESSAGE, LEVELS, WIDTH), message(EXTENDED_MESSAGE, LEVELS, WIDTH)
    )
    own, extended, mine, winds_below, lower_edge, forces_below = run(
        forward_local_kernel,
        (
            *pair_shapes,
            struct(ROWS + EXTRA, LEVELS, WIDTH),
            struct(WINDS * ROWS, LEVELS, WIDTH),
            struct(WINDS * DOWN_EDGE, LEVELS, WIDTH),
            struct(SUBS * ROWS, LEVELS, WIDTH),
        ),
        (winds, forces, below, down_edge),
        name="forward_local",
    )
    before = (moved(own, 1, 0), moved(extended, 1, 1))
    send = run(
        place_kernel,
        struct(TILES * 8, LANES),
        (chosen, target, lower_edge),
        name="place",
    )
    received = lax.all_to_all(
        send.reshape(TILES, 8, LANES), "space", split_axis=0, concat_axis=0, tiled=True
    ).reshape(TILES * 8, LANES)
    own, extended = run(
        forward_pair_kernel,
        pair_shapes,
        (winds, winds_below, lower_edge, mine, *before),
        name="forward_pair",
    )
    pair = (moved(own, 2, 0), moved(extended, 2, 1))
    slots, stencil = run(
        stencil_kernel,
        (
            struct(SUBS, LANES, LANES),
            struct(SUBS, CHUNKS, HALF, CORNERS * LANES, dtype=bf16),
        ),
        (received,),
        scratch=(pltpu.VMEM((LANES, LANES), f32),),
        name="stencil",
    )
    size = PIECES * LEVELS
    source, source_above, source_edge = run(
        forward_final_kernel,
        (
            struct(SUBS, ROWS, LEVELS, WIDTH),
            message(FORCE_MESSAGE + ROWS, LEVELS, WIDTH),
            message(2 + UP_EDGE, LEVELS, WIDTH),
        ),
        (
            winds, forces, winds_below, lower_edge, forces_below,
            *before, *pair, slots, stencil, mixing,
        ),
        scratch=(
            pltpu.VMEM((SUBS, size, HALF), f32),
            pltpu.VMEM((CHUNKS, 2 * size, CORNERS * LANES), f32),
            pltpu.VMEM((CHUNKS, 2 * size, CORNERS * LANES), bf16),
        ),
        name="forward_final",
    )

    source_above = moved(source_above, 0, -1)
    source_edge = moved(source_edge, 0, -2)
    own, extended, mine, unpacked, winds_above, upper_edge = run(
        adjoint_local_kernel,
        (
            *pair_shapes,
            struct(ROWS + EXTRA, LEVELS, WIDTH),
            struct(SUBS * ROWS, LEVELS, WIDTH),
            struct(WINDS * ROWS, LEVELS, WIDTH),
            struct(WINDS * UP_EDGE, LEVELS, WIDTH),
        ),
        (source, source_above, source_edge, winds),
        name="adjoint_local",
    )
    after = (moved(own, -1, 0), moved(extended, -1, -1))
    own, extended = run(
        adjoint_pair_kernel,
        pair_shapes,
        (winds, winds_above, upper_edge, mine, *after),
        name="adjoint_pair",
    )
    pair = (moved(own, -2, 0), moved(extended, -2, -1))
    return run(
        adjoint_final_kernel,
        struct(SUBS, LEVELS, ROWS, WIDTH),
        (source, unpacked, winds, winds_above, upper_edge, *after, *pair),
        name="adjoint_final",
    )


def solution(mesh):
    return jax.shard_map(
        shards,
        mesh=mesh,
        in_specs=(
            P("tm", None, "space", None),
            P(None, None, "space", None),
            P("tm", None, "space"),
            P("tm", None, "space"),
            P("tm", None, "space"),
            P("tm", "space", None),
            P(),
            P(),
        ),
        out_specs=P("tm", None, "space", None),
        check_vma=False,
    )
```

time: 108 us -> 93.6 us (0.87)
  starting transfers between devices: 49.2 us -> 41.1 us
  local copies, waits for them, and re-layouts: 2.94 us -> 0 us
  waiting for transfers between devices: 33.3 us -> 31.7 us
  Pallas kernels: 21.5 us -> 20.1 us
    ppermute x14 -> x12, starting transfers between devices: 37.5 us -> 31 us  [moved(): return lax.ppermute(array, ('tm', 'space'), pairs)]
    unnamed x18 -> x0, local copies, waits for them, and re-layouts: 2.94 us -> none
    ppermute x14 -> x12, waiting for transfers between devices: 33.3 us -> 31.7 us  [moved(): return lax.ppermute(array, ('tm', 'space'), pairs)]
    all_to_all x1, starting transfers between devices: 11.6 us -> 10 us  [shards(): lax.all_to_all(send.reshape(TILES, 8, LANES), 'space', split_axis=0, conc...]
    pallas_call x8 -> x10, Pallas kernels: 21.5 us -> 20.1 us  [run(): pl.pallas_call(kernel, out_shape=outputs, in_specs=[pl.BlockSpec(memory_s...]
  transfers between devices with their start and end apart: 15 -> 13, of which waited for: 6 -> 6; matrix products, arithmetic and copies ran while one was open for 0% -> 0% of each run, Pallas kernels for 4% -> 6%
where the time goes in v2:
time: 93.6 us; the launch traced here: 93 us
  starting transfers between devices  41.1 us (44%)
  waiting for transfers between devices  31.7 us (34%)
  Pallas kernels  20.1 us (21%)
    ppermute x12, waiting for transfers between devices, moved(): return lax.ppermute(array, ('tm', 'space'), pairs)  31.7 us
    ppermute x12, starting transfers between devices, moved(): return lax.ppermute(array, ('tm', 'space'), pairs)  31 us
    pallas_call x10, Pallas kernels, run(): pl.pallas_call(kernel, out_shape=outputs, in_specs=[pl.BlockSpec(memory_s...  20.1 us
    all_to_all x1, starting transfers between devices, shards(): lax.all_to_all(send.reshape(TILES, 8, LANES), 'space', split_axis=0, conc...  10 us
  transfers between devices with their start and end apart: 13, of which 6 were waited for; matrix products, arithmetic and copies ran while one was open for 0% of the time, Pallas kernels for 6%

profile of v2, /device:TPU:4, one launch (start us, length us, event | category | flops | bytes accessed | tf_op | source)
XLA Modules:
  0.0 93.0 jit_solution(7301234988709182735)
XLA Ops:
  0.0 1.5 %rows.1 = (f32[16,8,512]{2,1,0:T(8,128)S(1)}, f32[24,8,512]{2,1,0:T(8,128)S(1)}, s32[21,8,512]{2,1,0:T(8,128)S(1)}, s32[5,8,512]{2,1,0:T(8,128)S(1)}) custom-call(f32[3,8,8,512]{3,2,1,0:T(8,128)} %forcing_far.1, f32[2,8,8,512]{3,2,1,0:T(8,128)} %courant_far.1), custom_call_target="tpu_custom_call" | custom-call | flops 2000000 | bytes 655360 | tf_op jit(solution)/shard_map/rows/pallas_call | solution.py:538
  1.5 1.9 %collective-permute-start = (s32[21,8,512]{2,1,0:T(8,128)S(1)}, s32[21,8,512]{2,1,0:T(8,128)S(1)}, u32[]{:S(2)}, u32[]{:S(2)}) collective-permute-start(s32[21,8,512]{2,1,0:T(8,128)S(1)} %get-tuple-element.39), channel_id=1, source_target_pairs={{0,1},{1,2},{2,3},{3,4},{4,5},{5,6},{6,7},{7,8},{8,9},{9,10},{10,1... | collective-permute-start | bytes 1032200 | tf_op jit(solution)/shard_map/ppermute | solution.py:556
  3.5 3.8 %collective-permute-start.1 = (s32[5,8,512]{2,1,0:T(8,128)S(1)}, s32[5,8,512]{2,1,0:T(8,128)S(1)}, u32[]{:S(2)}, u32[]{:S(2)}) collective-permute-start(s32[5,8,512]{2,1,0:T(8,128)S(1)} %get-tuple-element.40), channel_id=1, source_target_pairs={{0,2},{1,3},{2,4},{3,5},{4,6},{5,7},{6,8},{7,9},{8,10},{9,11},{10,... | collective-permute-start | bytes 245768 | tf_op jit(solution)/shard_map/ppermute | solution.py:556
  7.3 2.4 %choose.1 = (f32[6,256,128]{2,1,0:T(8,128)S(1)}, f32[3,64,256]{2,1,0:T(8,128)S(1)}, f32[8,8,128]{2,1,0:T(8,128)S(1)}) custom-call(bf16[3,256,256]{2,1,0:T(8,128)(2,1)} %innovation_far.1, s32[3,4,256]{2,1,0:T(4,128)} %cells_far.1, bf16[3,4,256]{2,1,0:T(4,128)(2,1)} %weight_far.1, s32[3,1,256]{2,1,0:T(1,128)} %bitcast.7, f32[8,256]{1,0:T(8,128)} %bitcast.6, ...), custom_call_target="tpu_custom_call" | custom-call | flops 2000000 | bytes 423936 | tf_op jit(solution)/shard_map/choose/pallas_call | solution.py:538
  9.7 4.9 %collective-permute-done.1.down_edge = s32[5,8,512]{2,1,0:T(8,128)S(1)} collective-permute-done((s32[5,8,512]{2,1,0:T(8,128)S(1)}, s32[5,8,512]{2,1,0:T(8,128)S(1)}, u32[]{:S(2)}, u32[]{:S(2)}) %collective-permute-start.1) | collective-permute-done | bytes 81952 | tf_op jit(solution)/shard_map/ppermute | solution.py:556
  16.8 10.0 %all-to-all-start = ((f32[64,8,128]{2,1,0:T(8,128)}), f32[64,8,128]{2,1,0:T(8,128)S(1)}, u32[]{:S(2)}, u32[]{:S(2)}) async-start(f32[64,8,128]{2,1,0:T(8,128)} %bitcast.3), calls=%async_computation | async-start | bytes 524288 | tf_op jit(solution)/shard_map/all_to_all | solution.py:626
  26.8 3.2 %collective-permute-start.3 = (s32[7,8,512]{2,1,0:T(8,128)S(1)}, s32[7,8,512]{2,1,0:T(8,128)S(1)}, u32[]{:S(2)}, u32[]{:S(2)}) collective-permute-start(s32[7,8,512]{2,1,0:T(8,128)S(1)} %get-tuple-element.49), channel_id=1, source_target_pairs={{0,65},{1,66},{2,67},{3,68},{4,69},{5,70},{6,71},{7,72},{8,73},{9,... | collective-permute-start | bytes 344072 | tf_op jit(solution)/shard_map/ppermute | solution.py:556
  30.1 3.5 %collective-permute-start.2 = (s32[5,8,512]{2,1,0:T(8,128)S(1)}, s32[5,8,512]{2,1,0:T(8,128)S(1)}, u32[]{:S(2)}, u32[]{:S(2)}) collective-permute-start(s32[5,8,512]{2,1,0:T(8,128)S(1)} %get-tuple-element.48), channel_id=1, source_target_pairs={{0,64},{1,65},{2,66},{3,67},{4,68},{5,69},{6,70},{7,71},{8,72},{9,... | collective-permute-start | bytes 245768 | tf_op jit(solution)/shard_map/ppermute | solution.py:556
  33.6 3.5 %collective-permute-done.2.before_own = s32[5,8,512]{2,1,0:T(8,128)S(1)} collective-permute-done((s32[5,8,512]{2,1,0:T(8,128)S(1)}, s32[5,8,512]{2,1,0:T(8,128)S(1)}, u32[]{:S(2)}, u32[]{:S(2)}) %collective-permute-start.2) | collective-permute-done | bytes 81952 | tf_op jit(solution)/shard_map/ppermute | solution.py:556
  38.0 5.8 %collective-permute-start.5 = (s32[7,8,512]{2,1,0:T(8,128)S(1)}, s32[7,8,512]{2,1,0:T(8,128)S(1)}, u32[]{:S(2)}, u32[]{:S(2)}) collective-permute-start(s32[7,8,512]{2,1,0:T(8,128)S(1)} %get-tuple-element.52), channel_id=1, source_target_pairs={{0,129},{1,130},{2,131},{3,132},{4,133},{5,134},{6,135},{7,136},{8... | collective-permute-start | bytes 344072 | tf_op jit(solution)/shard_map/ppermute | solution.py:556
  43.8 1.4 %collective-permute-start.4 = (s32[5,8,512]{2,1,0:T(8,128)S(1)}, s32[5,8,512]{2,1,0:T(8,128)S(1)}, u32[]{:S(2)}, u32[]{:S(2)}) collective-permute-start(s32[5,8,512]{2,1,0:T(8,128)S(1)} %get-tuple-element.51), channel_id=1, source_target_pairs={{0,128},{1,129},{2,130},{3,131},{4,132},{5,133},{6,134},{7,135},{8... | collective-permute-start | bytes 245768 | tf_op jit(solution)/shard_map/ppermute | solution.py:556
  45.2 2.4 %stencil.1 = (f32[3,128,128]{2,1,0:T(8,128)S(1)}, bf16[3,8,256,512]{3,2,1,0:T(8,128)(2,1)S(1)}) custom-call(f32[512,128]{1,0:T(8,128)S(1)} %bitcast.5), custom_call_target="tpu_custom_call" | custom-call | flops 2000000 | bytes 262144 | tf_op jit(solution)/shard_map/stencil/pallas_call | solution.py:538
  47.6 1.5 %collective-permute-done.4.pair_own = s32[5,8,512]{2,1,0:T(8,128)S(1)} collective-permute-done((s32[5,8,512]{2,1,0:T(8,128)S(1)}, s32[5,8,512]{2,1,0:T(8,128)S(1)}, u32[]{:S(2)}, u32[]{:S(2)}) %collective-permute-start.4) | collective-permute-done | bytes 81952 | tf_op jit(solution)/shard_map/ppermute | solution.py:556
  49.1 7.2 %forward_final.1 = (f32[3,8,8,512]{3,2,1,0:T(8,128)S(1)}, s32[21,8,512]{2,1,0:T(8,128)S(1)}, s32[6,8,512]{2,1,0:T(8,128)S(1)}) custom-call(f32[16,8,512]{2,1,0:T(8,128)S(1)} %get-tuple-element.37.winds, f32[24,8,512]{2,1,0:T(8,128)S(1)} %get-tuple-element.38.forces, f32[16,8,512]{2,1,0:T(8,128)S(1)} %get-tuple-element.45.winds_below, ...), custom_call_target="tpu_custom_call" | custom-call | flops 2000000 | bytes 8323072 | tf_op jit(solution)/shard_map/forward_final/pallas_call | solution.py:538
  56.3 3.7 %collective-permute-start.6 = (s32[21,8,512]{2,1,0:T(8,128)S(1)}, s32[21,8,512]{2,1,0:T(8,128)S(1)}, u32[]{:S(2)}, u32[]{:S(2)}) collective-permute-start(s32[21,8,512]{2,1,0:T(8,128)S(1)} %get-tuple-element.59), channel_id=1, source_target_pairs={{1,0},{2,1},{3,2},{4,3},{5,4},{6,5},{7,6},{8,7},{9,8},{10,9},{11,1... | collective-permute-start | bytes 1032200 | tf_op jit(solution)/shard_map/ppermute | solution.py:556
  60.0 2.5 %collective-permute-start.7 = (s32[6,8,512]{2,1,0:T(8,128)S(1)}, s32[6,8,512]{2,1,0:T(8,128)S(1)}, u32[]{:S(2)}, u32[]{:S(2)}) collective-permute-start(s32[6,8,512]{2,1,0:T(8,128)S(1)} %get-tuple-element.60), channel_id=1, source_target_pairs={{2,0},{3,1},{4,2},{5,3},{6,4},{7,5},{8,6},{9,7},{10,8},{11,9},{12,... | collective-permute-start | bytes 294920 | tf_op jit(solution)/shard_map/ppermute | solution.py:556
  62.5 4.4 %collective-permute-done.7.source_edge = s32[6,8,512]{2,1,0:T(8,128)S(1)} collective-permute-done((s32[6,8,512]{2,1,0:T(8,128)S(1)}, s32[6,8,512]{2,1,0:T(8,128)S(1)}, u32[]{:S(2)}, u32[]{:S(2)}) %collective-permute-start.7) | collective-permute-done | bytes 98336 | tf_op jit(solution)/shard_map/ppermute | solution.py:556
  67.7 1.3 %collective-permute-start.9 = (s32[7,8,512]{2,1,0:T(8,128)S(1)}, s32[7,8,512]{2,1,0:T(8,128)S(1)}, u32[]{:S(2)}, u32[]{:S(2)}) collective-permute-start(s32[7,8,512]{2,1,0:T(8,128)S(1)} %get-tuple-element.65), channel_id=1, source_target_pairs={{65,0},{66,1},{67,2},{68,3},{69,4},{70,5},{71,6},{72,7},{73,8},{74... | collective-permute-start | bytes 344072 | tf_op jit(solution)/shard_map/ppermute | solution.py:556
  69.0 1.3 %collective-permute-start.8 = (s32[5,8,512]{2,1,0:T(8,128)S(1)}, s32[5,8,512]{2,1,0:T(8,128)S(1)}, u32[]{:S(2)}, u32[]{:S(2)}) collective-permute-start(s32[5,8,512]{2,1,0:T(8,128)S(1)} %get-tuple-element.64), channel_id=1, source_target_pairs={{64,0},{65,1},{66,2},{67,3},{68,4},{69,5},{70,6},{71,7},{72,8},{73... | collective-permute-start | bytes 245768 | tf_op jit(solution)/shard_map/ppermute | solution.py:556
  70.3 8.1 %collective-permute-done.8.after_own = s32[5,8,512]{2,1,0:T(8,128)S(1)} collective-permute-done((s32[5,8,512]{2,1,0:T(8,128)S(1)}, s32[5,8,512]{2,1,0:T(8,128)S(1)}, u32[]{:S(2)}, u32[]{:S(2)}) %collective-permute-start.8) | collective-permute-done | bytes 81952 | tf_op jit(solution)/shard_map/ppermute | solution.py:556
  79.2 1.3 %collective-permute-start.11 = (s32[7,8,512]{2,1,0:T(8,128)S(1)}, s32[7,8,512]{2,1,0:T(8,128)S(1)}, u32[]{:S(2)}, u32[]{:S(2)}) collective-permute-start(s32[7,8,512]{2,1,0:T(8,128)S(1)} %get-tuple-element.68), channel_id=1, source_target_pairs={{129,0},{130,1},{131,2},{132,3},{133,4},{134,5},{135,6},{136,7},{1... | collective-permute-start | bytes 344072 | tf_op jit(solution)/shard_map/ppermute | solution.py:556
  80.5 1.3 %collective-permute-start.10 = (s32[5,8,512]{2,1,0:T(8,128)S(1)}, s32[5,8,512]{2,1,0:T(8,128)S(1)}, u32[]{:S(2)}, u32[]{:S(2)}) collective-permute-start(s32[5,8,512]{2,1,0:T(8,128)S(1)} %get-tuple-element.67), channel_id=1, source_target_pairs={{128,0},{129,1},{130,2},{131,3},{132,4},{133,5},{134,6},{135,7},{1... | collective-permute-start | bytes 245768 | tf_op jit(solution)/shard_map/ppermute | solution.py:556
  81.8 9.3 %collective-permute-done.10.pair_own = s32[5,8,512]{2,1,0:T(8,128)S(1)} collective-permute-done((s32[5,8,512]{2,1,0:T(8,128)S(1)}, s32[5,8,512]{2,1,0:T(8,128)S(1)}, u32[]{:S(2)}, u32[]{:S(2)}) %collective-permute-start.10) | collective-permute-done | bytes 81952 | tf_op jit(solution)/shard_map/ppermute | solution.py:556
  91.1 1.9 %adjoint_final.1 = f32[3,8,8,512]{3,2,1,0:T(8,128)} custom-call(f32[3,8,8,512]{3,2,1,0:T(8,128)S(1)} %get-tuple-element.58.source, f32[24,8,512]{2,1,0:T(8,128)S(1)} %get-tuple-element.61.unpacked, f32[16,8,512]{2,1,0:T(8,128)S(1)} %get-tuple-element.37.winds, f32[16,8,512]{2,1,0:T(8,128)S(1)} %get-tuple-element.62.winds_above, ...), custom_call_target="tpu_custom_call" | custom-call | flops 2000000 | bytes 1835008 | tf_op jit(solution)/shard_map/adjoint_final/pallas_call | solution.py:538
  (12 shorter events, 4.8 us)
Async XLA Ops:
  1.5 13.0 %collective-permute-start = (s32[21,8,512]{2,1,0:T(8,128)S(1)}, s32[21,8,512]{2,1,0:T(8,128)S(1)}, u32[]{:S(2)}, u32[]{:S(2)}) collective-permute-start(s32[21,8,512]{2,1,0:T(8,128)S(1)} %get-tuple-element.39), channel_id=1, source_target_pairs={{0,1},{1,2},{2,3},{3,4},{4,5},{5,6},{6,7},{7,8},{8,9},{9,10},{10,1... | collective-permute-start | bytes 1032200 | tf_op jit(solution)/shard_map/ppermute | solution.py:556
  3.5 11.1 %collective-permute-start.1 = (s32[5,8,512]{2,1,0:T(8,128)S(1)}, s32[5,8,512]{2,1,0:T(8,128)S(1)}, u32[]{:S(2)}, u32[]{:S(2)}) collective-permute-start(s32[5,8,512]{2,1,0:T(8,128)S(1)} %get-tuple-element.40), channel_id=1, source_target_pairs={{0,2},{1,3},{2,4},{3,5},{4,6},{5,7},{6,8},{7,9},{8,10},{9,11},{10,... | collective-permute-start | bytes 245768 | tf_op jit(solution)/shard_map/ppermute | solution.py:556
  16.8 28.4 %all-to-all-start = ((f32[64,8,128]{2,1,0:T(8,128)}), f32[64,8,128]{2,1,0:T(8,128)S(1)}, u32[]{:S(2)}, u32[]{:S(2)}) async-start(f32[64,8,128]{2,1,0:T(8,128)} %bitcast.3), calls=%async_computation | async-start | bytes 524288 | tf_op jit(solution)/shard_map/all_to_all | solution.py:626
  26.8 10.3 %collective-permute-start.3 = (s32[7,8,512]{2,1,0:T(8,128)S(1)}, s32[7,8,512]{2,1,0:T(8,128)S(1)}, u32[]{:S(2)}, u32[]{:S(2)}) collective-permute-start(s32[7,8,512]{2,1,0:T(8,128)S(1)} %get-tuple-element.49), channel_id=1, source_target_pairs={{0,65},{1,66},{2,67},{3,68},{4,69},{5,70},{6,71},{7,72},{8,73},{9,... | collective-permute-start | bytes 344072 | tf_op jit(solution)/shard_map/ppermute | solution.py:556
  30.1 7.0 %collective-permute-start.2 = (s32[5,8,512]{2,1,0:T(8,128)S(1)}, s32[5,8,512]{2,1,0:T(8,128)S(1)}, u32[]{:S(2)}, u32[]{:S(2)}) collective-permute-start(s32[5,8,512]{2,1,0:T(8,128)S(1)} %get-tuple-element.48), channel_id=1, source_target_pairs={{0,64},{1,65},{2,66},{3,67},{4,68},{5,69},{6,70},{7,71},{8,72},{9,... | collective-permute-start | bytes 245768 | tf_op jit(solution)/shard_map/ppermute | solution.py:556
  38.0 11.1 %collective-permute-start.5 = (s32[7,8,512]{2,1,0:T(8,128)S(1)}, s32[7,8,512]{2,1,0:T(8,128)S(1)}, u32[]{:S(2)}, u32[]{:S(2)}) collective-permute-start(s32[7,8,512]{2,1,0:T(8,128)S(1)} %get-tuple-element.52), channel_id=1, source_target_pairs={{0,129},{1,130},{2,131},{3,132},{4,133},{5,134},{6,135},{7,136},{8... | collective-permute-start | bytes 344072 | tf_op jit(solution)/shard_map/ppermute | solution.py:556
  43.8 5.3 %collective-permute-start.4 = (s32[5,8,512]{2,1,0:T(8,128)S(1)}, s32[5,8,512]{2,1,0:T(8,128)S(1)}, u32[]{:S(2)}, u32[]{:S(2)}) collective-permute-start(s32[5,8,512]{2,1,0:T(8,128)S(1)} %get-tuple-element.51), channel_id=1, source_target_pairs={{0,128},{1,129},{2,130},{3,131},{4,132},{5,133},{6,134},{7,135},{8... | collective-permute-start | bytes 245768 | tf_op jit(solution)/shard_map/ppermute | solution.py:556
  56.3 10.6 %collective-permute-start.6 = (s32[21,8,512]{2,1,0:T(8,128)S(1)}, s32[21,8,512]{2,1,0:T(8,128)S(1)}, u32[]{:S(2)}, u32[]{:S(2)}) collective-permute-start(s32[21,8,512]{2,1,0:T(8,128)S(1)} %get-tuple-element.59), channel_id=1, source_target_pairs={{1,0},{2,1},{3,2},{4,3},{5,4},{6,5},{7,6},{8,7},{9,8},{10,9},{11,1... | collective-permute-start | bytes 1032200 | tf_op jit(solution)/shard_map/ppermute | solution.py:556
  60.0 6.9 %collective-permute-start.7 = (s32[6,8,512]{2,1,0:T(8,128)S(1)}, s32[6,8,512]{2,1,0:T(8,128)S(1)}, u32[]{:S(2)}, u32[]{:S(2)}) collective-permute-start(s32[6,8,512]{2,1,0:T(8,128)S(1)} %get-tuple-element.60), channel_id=1, source_target_pairs={{2,0},{3,1},{4,2},{5,3},{6,4},{7,5},{8,6},{9,7},{10,8},{11,9},{12,... | collective-permute-start | bytes 294920 | tf_op jit(solution)/shard_map/ppermute | solution.py:556
  67.7 10.7 %collective-permute-start.9 = (s32[7,8,512]{2,1,0:T(8,128)S(1)}, s32[7,8,512]{2,1,0:T(8,128)S(1)}, u32[]{:S(2)}, u32[]{:S(2)}) collective-permute-start(s32[7,8,512]{2,1,0:T(8,128)S(1)} %get-tuple-element.65), channel_id=1, source_target_pairs={{65,0},{66,1},{67,2},{68,3},{69,4},{70,5},{71,6},{72,7},{73,8},{74... | collective-permute-start | bytes 344072 | tf_op jit(solution)/shard_map/ppermute | solution.py:556
  69.0 9.4 %collective-permute-start.8 = (s32[5,8,512]{2,1,0:T(8,128)S(1)}, s32[5,8,512]{2,1,0:T(8,128)S(1)}, u32[]{:S(2)}, u32[]{:S(2)}) collective-permute-start(s32[5,8,512]{2,1,0:T(8,128)S(1)} %get-tuple-element.64), channel_id=1, source_target_pairs={{64,0},{65,1},{66,2},{67,3},{68,4},{69,5},{70,6},{71,7},{72,8},{73... | collective-permute-start | bytes 245768 | tf_op jit(solution)/shard_map/ppermute | solution.py:556
  79.2 11.9 %collective-permute-start.11 = (s32[7,8,512]{2,1,0:T(8,128)S(1)}, s32[7,8,512]{2,1,0:T(8,128)S(1)}, u32[]{:S(2)}, u32[]{:S(2)}) collective-permute-start(s32[7,8,512]{2,1,0:T(8,128)S(1)} %get-tuple-element.68), channel_id=1, source_target_pairs={{129,0},{130,1},{131,2},{132,3},{133,4},{134,5},{135,6},{136,7},{1... | collective-permute-start | bytes 344072 | tf_op jit(solution)/shard_map/ppermute | solution.py:556
  80.5 10.6 %collective-permute-start.10 = (s32[5,8,512]{2,1,0:T(8,128)S(1)}, s32[5,8,512]{2,1,0:T(8,128)S(1)}, u32[]{:S(2)}, u32[]{:S(2)}) collective-permute-start(s32[5,8,512]{2,1,0:T(8,128)S(1)} %get-tuple-element.67), channel_id=1, source_target_pairs={{128,0},{129,1},{130,2},{131,3},{132,4},{133,5},{134,6},{135,7},{1... | collective-permute-start | bytes 245768 | tf_op jit(solution)/shard_map/ppermute | solution.py:556

commit v3 on v2

--- a/solution.py
+++ b/solution.py
@@ -1,5 +1,3 @@
-import functools
-
 import jax
 import jax.numpy as jnp
 from jax import lax
@@ -59,7 +57,23 @@
     return mantissa * jnp.exp2(exponent)
 
 
-def encode(values, message):
+TILE_COLUMNS = WIDTH // LANES
+
+
+def message_tiles(count):
+    return count // 2 * TILE_COLUMNS + 1
+
+
+def put_row(message, start, value):
+    for part in range(TILE_COLUMNS):
+        message[start + part] = value[:, part * LANES : (part + 1) * LANES]
+
+
+def get_row(message, start):
+    return jnp.concatenate([message[start + part] for part in range(TILE_COLUMNS)], axis=1)
+
+
+def encode(values, message, start=0):
     count = len(values)
     lane = lax.broadcasted_iota(jnp.int32, (LEVELS, LANES), 1)
     largest = jnp.full((LEVELS, LANES), 1e-30, f32)
@@ -73,16 +87,16 @@
     half = count // 2
     whole = [nearest(value * factor[:, n : n + 1]) for n, value in enumerate(values)]
     for number in range(half):
-        message[number] = join(whole[number], whole[number + half])
-    message[half] = jnp.concatenate([code] * (WIDTH // LANES), axis=1)
-
-
-def decode(message, count):
+        put_row(message, start + number * TILE_COLUMNS, join(whole[number], whole[number + half]))
+    message[start + half * TILE_COLUMNS] = code
+
+
+def decode(message, count, start=0):
     half = count // 2
-    factor = scale_of(message[half][:, :LANES]) * (1.0 / LEVEL_TOP)
+    factor = scale_of(message[start + half * TILE_COLUMNS]) * (1.0 / LEVEL_TOP)
     values = [None] * count
     for number in range(half):
-        pair = parted(message[number])
+        pair = parted(get_row(message, start + number * TILE_COLUMNS))
         for place, value in zip((number, number + half), pair):
             values[place] = value.astype(f32) * factor[:, place : place + 1]
     return values
@@ -138,12 +152,13 @@
 
 WINDS = 2
 FIELDS = WINDS + SUBS
-DOWN_EDGE = 3
 UP_EDGE = 4
 EXTRA = 4
-OWN_MESSAGE = ROWS // 2 + 1
-EXTENDED_MESSAGE = (ROWS + EXTRA) // 2 + 1
-FORCE_MESSAGE = SUBS * ROWS // 2 + 1
+REACH = 10
+DOWN_ROWS = [(sub, row) for sub in range(SUBS) for row in range(2 * sub, ROWS)]
+WIND_TILES = ROWS * TILE_COLUMNS
+FORCE_TILES = message_tiles(SUBS * ROWS)
+EDGE_TILES = message_tiles(2)
 
 
 def lower_winds(winds, winds_below, edge):
@@ -153,7 +168,7 @@
                 return winds[field * ROWS + row]
             if row >= -ROWS:
                 return winds_below[field * ROWS + row + ROWS]
-            return edge[field * DOWN_EDGE + row + ROWS + DOWN_EDGE]
+            return edge[field * ROWS + row + 2 * ROWS]
 
         return read
 
@@ -174,12 +189,14 @@
     return [reader(field) for field in range(WINDS)]
 
 
-def lower_forces(forces, forces_below):
+def lower_forces(forces, forces_below, edge=None):
     def reader(sub):
         def read(row):
             if row >= 0:
                 return forces[sub * ROWS + row]
-            return forces_below[sub * ROWS + row + ROWS]
+            if row >= -ROWS:
+                return forces_below[sub * ROWS + row + ROWS]
+            return edge[sub, row + 2 * ROWS]
 
         return read
 
@@ -213,25 +230,26 @@
     for field in range(WINDS):
         winds[pl.ds(field * ROWS, ROWS)] = jnp.swapaxes(courant[field], 0, 1)
     encode_winds(winds, range(ROWS), below, 0)
-    encode_winds(winds, range(ROWS - DOWN_EDGE, ROWS), down_edge, 0)
+    encode_winds(winds, range(ROWS), down_edge, 0)
     rows = []
     for sub in range(SUBS):
         copies[WINDS + sub].wait()
         turned = jnp.swapaxes(forcing[sub], 0, 1)
         forces[pl.ds(sub * ROWS, ROWS)] = turned
         rows += [turned[row] for row in range(ROWS)]
-    encode(rows, below.at[pl.ds(ROWS, FORCE_MESSAGE)])
-    encode(rows[ROWS - 2 : ROWS], down_edge.at[pl.ds(DOWN_EDGE, 2)])
+    encode(rows, below, WIND_TILES)
+    encode([rows[sub * ROWS + row] for sub, row in DOWN_ROWS], down_edge, WIND_TILES)
 
 
 def encode_winds(winds, rows, message, start):
     for number, row in enumerate(rows):
-        message[start + number] = encode_wind(winds[row], winds[ROWS + row])
+        both = encode_wind(winds[row], winds[ROWS + row])
+        put_row(message, start + number * TILE_COLUMNS, both)
 
 
 def unpack_winds(message, rows, result, start=0):
     for row in range(rows):
-        first, second = decode_wind(message[start + row])
+        first, second = decode_wind(get_row(message, start + row * TILE_COLUMNS))
         result[row] = first
         result[rows + row] = second
 
@@ -299,8 +317,7 @@
             chosen[2 * sub + half] = jnp.where(rank == slot_rank + half, repeated, 0.0)
 
 
-def place_kernel(chosen, target, after, send):
-    del after
+def place_kernel(chosen, target, send):
     for sub in range(SUBS):
         for half in range(2):
             send[pl.ds(2 * sub + half, TILES, stride=8), :] = jnp.dot(
@@ -384,30 +401,30 @@
 
 
 def forward_local_kernel(
-    winds, forces, below, down_edge,
-    own, extended, mine, winds_below, lower_edge, forces_below,
+    winds, forces, below, down_edge, own, mine, winds_below, lower_edge, forces_below
 ):
     unpack_winds(below, ROWS, winds_below)
-    unpack_winds(down_edge, DOWN_EDGE, lower_edge)
-    rows = decode(below.at[pl.ds(ROWS, FORCE_MESSAGE)], SUBS * ROWS)
-    for number, row in enumerate(rows):
+    unpack_winds(down_edge, ROWS, lower_edge)
+    for number, row in enumerate(decode(below, SUBS * ROWS, WIND_TILES)):
         forces_below[number] = row
-    edge = decode(down_edge.at[pl.ds(DOWN_EDGE, 2)], 2)
+    edge = dict(zip(DOWN_ROWS, decode(down_edge, len(DOWN_ROWS), WIND_TILES)))
     across = lower_winds(winds, winds_below, lower_edge)
-    forced = lower_forces(forces, forces_below)
-    low = -(ROWS + 2)
-    current = {row: edge[row - low] for row in (low, low + 1)}
-    for row in range(-ROWS, ROWS):
-        current[row] = forced[0](row)
+    forced = lower_forces(forces, forces_below, edge)
+    low = -2 * ROWS
+    current = {row: forced[0](row) for row in range(low, ROWS)}
     current, low = forward_steps(current, across, low, 2)
     for sub in range(1, SUBS):
         current = add_rows(current, forced[sub], low, ROWS)
         current, low = forward_steps(current, across, low, 2)
-    listed = [current[row] for row in range(-EXTRA, ROWS)]
-    for number, row in enumerate(listed):
+    listed = [current[row] for row in range(-REACH, ROWS)]
+    for number, row in enumerate(listed[REACH - EXTRA :]):
         mine[number] = row
-    encode(listed[EXTRA:], own)
-    encode(listed, extended)
+    encode(listed, own)
+
+
+def before_state(message, low):
+    rows = decode(message, REACH + ROWS)
+    return {row: rows[row + REACH] for row in range(low, ROWS)}
 
 
 def lower_state(own, extended, low):
@@ -416,12 +433,9 @@
     return {row: here[row] if row >= 0 else under[row + ROWS + EXTRA] for row in range(low, ROWS)}
 
 
-def forward_pair_kernel(
-    winds, winds_below, lower_edge, mine, before_own, before_extended, own, extended
-):
+def forward_pair_kernel(winds, winds_below, lower_edge, mine, before, own, extended):
     across = lower_winds(winds, winds_below, lower_edge)
-    low = -(ROWS + 2)
-    current, low = forward_steps(lower_state(before_own, before_extended, low), across, low, 6)
+    current, low = forward_steps(before_state(before, -REACH), across, -REACH, 6)
     listed = [current[row] + mine[row + EXTRA] for row in range(-EXTRA, ROWS)]
     encode(listed[EXTRA:], own)
     encode(listed, extended)
@@ -429,7 +443,7 @@
 
 def forward_final_kernel(
     winds, forces, winds_below, lower_edge, forces_below,
-    before_own, before_extended, pair_own, pair_extended, slots, stencil, mixing,
+    before, pair_own, pair_extended, slots, stencil, mixing,
     result, result_above, result_edge,
     states, found, spread,
 ):
@@ -437,7 +451,7 @@
     forced = lower_forces(forces, forces_below)
     low = -(ROWS + EXTRA)
     current, low = forward_steps(lower_state(pair_own, pair_extended, low), across, low, 6)
-    before = lower_state(before_own, before_extended, low)
+    before = before_state(before, low)
     current = {row: current[row] + before[row] for row in current}
     for sub in range(SUBS):
         current = add_rows(current, forced[sub], low, ROWS)
@@ -458,22 +472,22 @@
             )
             result[sub, row] = value
             listed.append(value)
-    encode(listed, result_above.at[pl.ds(0, FORCE_MESSAGE)])
-    encode_winds(winds, range(ROWS), result_above, FORCE_MESSAGE)
-    encode(listed[-ROWS : 2 - ROWS], result_edge.at[pl.ds(0, 2)])
-    encode_winds(winds, range(UP_EDGE), result_edge, 2)
+    encode(listed, result_above)
+    encode_winds(winds, range(ROWS), result_above, FORCE_TILES)
+    encode(listed[-ROWS : 2 - ROWS], result_edge)
+    encode_winds(winds, range(UP_EDGE), result_edge, EDGE_TILES)
 
 
 def adjoint_local_kernel(
     source, source_above, source_edge, winds,
     own, extended, mine, unpacked, winds_above, upper_edge,
 ):
-    unpack_winds(source_above, ROWS, winds_above, FORCE_MESSAGE)
-    unpack_winds(source_edge, UP_EDGE, upper_edge, 2)
+    unpack_winds(source_above, ROWS, winds_above, FORCE_TILES)
+    unpack_winds(source_edge, UP_EDGE, upper_edge, EDGE_TILES)
     across = upper_winds(winds, winds_above, upper_edge)
     high = 2 * ROWS + 2
-    above = decode(source_above.at[pl.ds(0, FORCE_MESSAGE)], SUBS * ROWS)
-    edge = decode(source_edge.at[pl.ds(0, 2)], 2)
+    above = decode(source_above, SUBS * ROWS)
+    edge = decode(source_edge, 2)
     for number, row in enumerate(above):
         unpacked[number] = row
 
@@ -491,12 +505,12 @@
     for number, row in enumerate(listed):
         mine[number] = row
     encode(listed[:ROWS], own)
-    encode(listed, extended)
-
-
-def upper_state(own, extended, high):
+    encode(listed[:REACH], extended)
+
+
+def upper_state(own, extended, high, count):
     here = decode(own, ROWS)
-    over = decode(extended, ROWS + EXTRA)
+    over = decode(extended, count)
     return {row: here[row] if row < ROWS else over[row - ROWS] for row in range(high)}
 
 
@@ -505,7 +519,7 @@
 ):
     across = upper_winds(winds, winds_above, upper_edge)
     high = 2 * ROWS + 2
-    current, high = adjoint_steps(upper_state(after_own, after_extended, high), across, high, 6)
+    current, high = adjoint_steps(upper_state(after_own, after_extended, high, REACH), across, high, 6)
     listed = [current[row] + mine[row] for row in range(ROWS + EXTRA)]
     encode(listed[:ROWS], own)
     encode(listed, extended)
@@ -513,24 +527,31 @@
 
 def adjoint_final_kernel(
     source, unpacked, winds, winds_above, upper_edge,
-    after_own, after_extended, pair_own, pair_extended, gradient,
+    after_own, after_extended, pair_own, pair_extended, gradient_far, gradient, sems,
 ):
     across = upper_winds(winds, winds_above, upper_edge)
     high = 2 * ROWS + EXTRA
-    current, high = adjoint_steps(upper_state(pair_own, pair_extended, high), across, high, 6)
-    after = upper_state(after_own, after_extended, high)
+    current, high = adjoint_steps(upper_state(pair_own, pair_extended, high, ROWS + EXTRA), across, high, 6)
+    after = upper_state(after_own, after_extended, high, REACH)
     current = {row: current[row] + after[row] for row in current}
 
     def source_row(sub):
         return lambda row: source[sub, row] if row < ROWS else unpacked[sub * ROWS + row - ROWS]
 
+    copies = []
     for sub in reversed(range(SUBS)):
         current = add_rows(current, source_row(sub), 0, high)
         current, high = adjoint_steps(current, across, high, 2)
         gradient[sub] = jnp.swapaxes(jnp.stack([current[row] for row in range(ROWS)]), 0, 1)
-
-
-def run(kernel, outputs, arguments, scratch=(), name=None, flops=2_000_000, far=False):
+        copies.append(
+            pltpu.make_async_copy(gradient.at[sub], gradient_far.at[sub], sems.at[sub])
+        )
+        copies[-1].start()
+    for copy in copies:
+        copy.wait()
+
+
+def run(kernel, outputs, arguments, scratch=(), name=None, flops=2_000_000, far=False, far_out=False):
     size = sum(a.size * a.dtype.itemsize for a in arguments)
     place = pltpu.HBM if far else pltpu.VMEM
     if far:
@@ -539,6 +560,7 @@
         kernel,
         out_shape=outputs,
         in_specs=[pl.BlockSpec(memory_space=place)] * len(arguments),
+        **({"out_specs": pl.BlockSpec(memory_space=pltpu.HBM)} if far_out else {}),
         scratch_shapes=scratch,
         compiler_params=pltpu.CompilerParams(vmem_limit_bytes=40 * 1024 * 1024),
         cost_estimate=pl.CostEstimate(flops=flops, bytes_accessed=size, transcendentals=0),
@@ -559,14 +581,16 @@
 def shards(
     forcing, courant, innovation, obs_cells, obs_weight, obs_owner, channel_weight, channel_rinv
 ):
-    message = functools.partial(struct, dtype=jnp.int32)
+    def message(tiles):
+        return struct(tiles, LEVELS, LANES, dtype=jnp.int32)
+
     winds, forces, below, down_edge = run(
         rows_kernel,
         (
             struct(WINDS * ROWS, LEVELS, WIDTH),
             struct(SUBS * ROWS, LEVELS, WIDTH),
-            message(ROWS + FORCE_MESSAGE, LEVELS, WIDTH),
-            message(DOWN_EDGE + 2, LEVELS, WIDTH),
+            message(WIND_TILES + FORCE_TILES),
+            message(WIND_TILES + message_tiles(len(DOWN_ROWS))),
         ),
         (forcing, courant),
         scratch=(
@@ -598,38 +622,29 @@
         name="choose",
         far=True,
     )
-    below, down_edge, chosen, target = lax.optimization_barrier(
-        (below, down_edge, chosen, target)
-    )
-    pair_shapes = (
-        message(OWN_MESSAGE, LEVELS, WIDTH), message(EXTENDED_MESSAGE, LEVELS, WIDTH)
-    )
-    own, extended, mine, winds_below, lower_edge, forces_below = run(
-        forward_local_kernel,
-        (
-            *pair_shapes,
-            struct(ROWS + EXTRA, LEVELS, WIDTH),
-            struct(WINDS * ROWS, LEVELS, WIDTH),
-            struct(WINDS * DOWN_EDGE, LEVELS, WIDTH),
-            struct(SUBS * ROWS, LEVELS, WIDTH),
-        ),
-        (winds, forces, below, down_edge),
-        name="forward_local",
-    )
-    before = (moved(own, 1, 0), moved(extended, 1, 1))
-    send = run(
-        place_kernel,
-        struct(TILES * 8, LANES),
-        (chosen, target, lower_edge),
-        name="place",
-    )
+    send = run(place_kernel, struct(TILES * 8, LANES), (chosen, target), name="place")
     received = lax.all_to_all(
         send.reshape(TILES, 8, LANES), "space", split_axis=0, concat_axis=0, tiled=True
     ).reshape(TILES * 8, LANES)
+    below, down_edge, _ = lax.optimization_barrier((below, down_edge, send))
+    own, mine, winds_below, lower_edge, forces_below = run(
+        forward_local_kernel,
+        (
+            message(message_tiles(REACH + ROWS)),
+            struct(ROWS + EXTRA, LEVELS, WIDTH),
+            struct(WINDS * ROWS, LEVELS, WIDTH),
+            struct(WINDS * ROWS, LEVELS, WIDTH),
+            struct(SUBS * ROWS, LEVELS, WIDTH),
+        ),
+        (winds, forces, below, down_edge),
+        name="forward_local",
+    )
+    before = moved(own, 1, 0)
+    pair_shapes = (message(message_tiles(ROWS)), message(message_tiles(ROWS + EXTRA)))
     own, extended = run(
         forward_pair_kernel,
         pair_shapes,
-        (winds, winds_below, lower_edge, mine, *before),
+        (winds, winds_below, lower_edge, mine, before),
         name="forward_pair",
     )
     pair = (moved(own, 2, 0), moved(extended, 2, 1))
@@ -648,12 +663,12 @@
         forward_final_kernel,
         (
             struct(SUBS, ROWS, LEVELS, WIDTH),
-            message(FORCE_MESSAGE + ROWS, LEVELS, WIDTH),
-            message(2 + UP_EDGE, LEVELS, WIDTH),
+            message(FORCE_TILES + WIND_TILES),
+            message(EDGE_TILES + UP_EDGE * TILE_COLUMNS),
         ),
         (
             winds, forces, winds_below, lower_edge, forces_below,
-            *before, *pair, slots, stencil, mixing,
+            before, *pair, slots, stencil, mixing,
         ),
         scratch=(
             pltpu.VMEM((SUBS, size, HALF), f32),
@@ -668,7 +683,8 @@
     own, extended, mine, unpacked, winds_above, upper_edge = run(
         adjoint_local_kernel,
         (
-            *pair_shapes,
+            message(message_tiles(ROWS)),
+            message(message_tiles(REACH)),
             struct(ROWS + EXTRA, LEVELS, WIDTH),
             struct(SUBS * ROWS, LEVELS, WIDTH),
             struct(WINDS * ROWS, LEVELS, WIDTH),
@@ -689,7 +705,12 @@
         adjoint_final_kernel,
         struct(SUBS, LEVELS, ROWS, WIDTH),
         (source, unpacked, winds, winds_above, upper_edge, *after, *pair),
+        scratch=(
+            pltpu.VMEM((SUBS, LEVELS, ROWS, WIDTH), f32),
+            pltpu.SemaphoreType.DMA((SUBS,)),
+        ),
         name="adjoint_final",
+        far_out=True,
     )
 
 

time: 93.6 us -> 86.2 us (0.921)
  waiting for transfers between devices: 31.7 us -> 24 us
    ppermute x12 -> x11, waiting for transfers between devices: 31.7 us -> 24 us  [moved(): return lax.ppermute(array, ('tm', 'space'), pairs)]
    all_to_all x1, starting transfers between devices: 10 us -> 11.6 us  [shards(): lax.all_to_all(send.reshape(TILES, 8, LANES), 'space', split_axis=0, conc...]
    ppermute x12 -> x11, starting transfers between devices: 31 us -> 29.6 us  [moved(): return lax.ppermute(array, ('tm', 'space'), pairs)]
  transfers between devices with their start and end apart: 13 -> 12, of which waited for: 6 -> 4; matrix products, arithmetic and copies ran while one was open for 0% -> 0% of each run, Pallas kernels for 6% -> 9%
where the time goes in v3:
time: 86.2 us; the launch traced here: 85.7 us
  starting transfers between devices  41.2 us (48%)
  waiting for transfers between devices  24 us (28%)
  Pallas kernels  20.3 us (24%)
    ppermute x11, starting transfers between devices, moved(): return lax.ppermute(array, ('tm', 'space'), pairs)  29.6 us
    ppermute x11, waiting for transfers between devices, moved(): return lax.ppermute(array, ('tm', 'space'), pairs)  24 us
    pallas_call x10, Pallas kernels, run(): pl.pallas_call(kernel, out_shape=outputs, in_specs=[pl.BlockSpec(memory_s...  20.3 us
    all_to_all x1, starting transfers between devices, shards(): lax.all_to_all(send.reshape(TILES, 8, LANES), 'space', split_axis=0, conc...  11.6 us
  transfers between devices with their start and end apart: 12, of which 4 were waited for; matrix products, arithmetic and copies ran while one was open for 0% of the time, Pallas kernels for 9%

profile of v3, /device:TPU:4, one launch (start us, length us, event | category | flops | bytes accessed | tf_op | source)
XLA Modules:
  0.0 85.7 jit_solution(11235097199075115276)
XLA Ops:
  0.0 1.6 %rows.1 = (f32[16,8,512]{2,1,0:T(8,128)S(1)}, f32[24,8,512]{2,1,0:T(8,128)S(1)}, s32[81,8,128]{2,1,0:T(8,128)S(1)}, s32[69,8,128]{2,1,0:T(8,128)S(1)}) custom-call(f32[3,8,8,512]{3,2,1,0:T(8,128)} %forcing_far.1, f32[2,8,8,512]{3,2,1,0:T(8,128)} %courant_far.1), custom_call_target="tpu_custom_call" | custom-call | flops 2000000 | bytes 655360 | tf_op jit(solution)/shard_map/rows/pallas_call | solution.py:559
  1.6 1.9 %collective-permute-start = (s32[81,8,128]{2,1,0:T(8,128)S(1)}, s32[81,8,128]{2,1,0:T(8,128)S(1)}, u32[]{:S(2)}, u32[]{:S(2)}) collective-permute-start(s32[81,8,128]{2,1,0:T(8,128)S(1)} %get-tuple-element.36), channel_id=1, source_target_pairs={{0,1},{1,2},{2,3},{3,4},{4,5},{5,6},{6,7},{7,8},{8,9},{9,10},{10,1... | collective-permute-start | bytes 995336 | tf_op jit(solution)/shard_map/ppermute | solution.py:578
  3.6 3.8 %collective-permute-start.1 = (s32[69,8,128]{2,1,0:T(8,128)S(1)}, s32[69,8,128]{2,1,0:T(8,128)S(1)}, u32[]{:S(2)}, u32[]{:S(2)}) collective-permute-start(s32[69,8,128]{2,1,0:T(8,128)S(1)} %get-tuple-element.37), channel_id=1, source_target_pairs={{0,2},{1,3},{2,4},{3,5},{4,6},{5,7},{6,8},{7,9},{8,10},{9,11},{10,... | collective-permute-start | bytes 847880 | tf_op jit(solution)/shard_map/ppermute | solution.py:578
  7.4 2.4 %choose.1 = (f32[6,256,128]{2,1,0:T(8,128)S(1)}, f32[3,64,256]{2,1,0:T(8,128)S(1)}, f32[8,8,128]{2,1,0:T(8,128)S(1)}) custom-call(bf16[3,256,256]{2,1,0:T(8,128)(2,1)} %innovation_far.1, s32[3,4,256]{2,1,0:T(4,128)} %cells_far.1, bf16[3,4,256]{2,1,0:T(4,128)(2,1)} %weight_far.1, s32[3,1,256]{2,1,0:T(1,128)} %bitcast.7, f32[8,256]{1,0:T(8,128)} %bitcast.6, ...), custom_call_target="tpu_custom_call" | custom-call | flops 2000000 | bytes 423936 | tf_op jit(solution)/shard_map/choose/pallas_call | solution.py:559
  9.8 1.2 %place.1 = f32[512,128]{1,0:T(8,128)} custom-call(f32[6,256,128]{2,1,0:T(8,128)S(1)} %get-tuple-element.38.chosen, f32[3,64,256]{2,1,0:T(8,128)S(1)} %get-tuple-element.39.target), custom_call_target="tpu_custom_call" | custom-call | flops 2000000 | bytes 983040 | tf_op jit(solution)/shard_map/place/pallas_call | solution.py:559
  11.0 11.6 %all-to-all-start = ((f32[64,8,128]{2,1,0:T(8,128)}), f32[64,8,128]{2,1,0:T(8,128)S(1)}, u32[]{:S(2)}, u32[]{:S(2)}) async-start(f32[64,8,128]{2,1,0:T(8,128)} %bitcast.3), calls=%async_computation | async-start | bytes 524288 | tf_op jit(solution)/shard_map/all_to_all | solution.py:626
  22.7 1.0 %forward_local.1 = (s32[37,8,128]{2,1,0:T(8,128)S(1)}, f32[12,8,512]{2,1,0:T(8,128)S(1)}, f32[16,8,512]{2,1,0:T(8,128)S(1)}, f32[16,8,512]{2,1,0:T(8,128)S(1)}, f32[24,8,512]{2,1,0:T(8,128)S(1)}) custom-call(f32[16,8,512]{2,1,0:T(8,128)S(1)} %get-tuple-element.34.winds, f32[24,8,512]{2,1,0:T(8,128)S(1)} %get-tuple-element.35.forces, ...), custom_call_target="tpu_custom_call" | custom-call | flops 2000000 | bytes 1269760 | tf_op jit(solution)/shard_map/forward_local/pallas_call | solution.py:559
  23.7 3.5 %collective-permute-start.2 = (s32[37,8,128]{2,1,0:T(8,128)S(1)}, s32[37,8,128]{2,1,0:T(8,128)S(1)}, u32[]{:S(2)}, u32[]{:S(2)}) collective-permute-start(s32[37,8,128]{2,1,0:T(8,128)S(1)} %get-tuple-element.45), channel_id=1, source_target_pairs={{0,64},{1,65},{2,66},{3,67},{4,68},{5,69},{6,70},{7,71},{8,72},{9,... | collective-permute-start | bytes 454664 | tf_op jit(solution)/shard_map/ppermute | solution.py:578
  27.2 3.5 %collective-permute-done.2.before = s32[37,8,128]{2,1,0:T(8,128)S(1)} collective-permute-done((s32[37,8,128]{2,1,0:T(8,128)S(1)}, s32[37,8,128]{2,1,0:T(8,128)S(1)}, u32[]{:S(2)}, u32[]{:S(2)}) %collective-permute-start.2) | collective-permute-done | bytes 151584 | tf_op jit(solution)/shard_map/ppermute | solution.py:578
  30.7 0.9 %forward_pair.1 = (s32[17,8,128]{2,1,0:T(8,128)S(1)}, s32[25,8,128]{2,1,0:T(8,128)S(1)}) custom-call(f32[16,8,512]{2,1,0:T(8,128)S(1)} %get-tuple-element.34.winds, f32[16,8,512]{2,1,0:T(8,128)S(1)} %get-tuple-element.42.winds_below, f32[16,8,512]{2,1,0:T(8,128)S(1)} %get-tuple-element.43.lower_edge, f32[12,8,512]{2,1,0:T(8,128)S(1)} %get-tuple-element.46.mine, ...), custom_call_target="tpu_custom_call" | custom-call | flops 2000000 | bytes 1134592 | tf_op jit(solution)/shard_map/forward_pair/pallas_call | solution.py:559
  31.5 4.9 %collective-permute-start.4 = (s32[25,8,128]{2,1,0:T(8,128)S(1)}, s32[25,8,128]{2,1,0:T(8,128)S(1)}, u32[]{:S(2)}, u32[]{:S(2)}) collective-permute-start(s32[25,8,128]{2,1,0:T(8,128)S(1)} %get-tuple-element.48), channel_id=1, source_target_pairs={{0,129},{1,130},{2,131},{3,132},{4,133},{5,134},{6,135},{7,136},{8... | collective-permute-start | bytes 307208 | tf_op jit(solution)/shard_map/ppermute | solution.py:578
  36.5 2.4 %collective-permute-start.3 = (s32[17,8,128]{2,1,0:T(8,128)S(1)}, s32[17,8,128]{2,1,0:T(8,128)S(1)}, u32[]{:S(2)}, u32[]{:S(2)}) collective-permute-start(s32[17,8,128]{2,1,0:T(8,128)S(1)} %get-tuple-element.47), channel_id=1, source_target_pairs={{0,128},{1,129},{2,130},{3,131},{4,132},{5,133},{6,134},{7,135},{8... | collective-permute-start | bytes 208904 | tf_op jit(solution)/shard_map/ppermute | solution.py:578
  38.9 2.4 %stencil.1 = (f32[3,128,128]{2,1,0:T(8,128)S(1)}, bf16[3,8,256,512]{3,2,1,0:T(8,128)(2,1)S(1)}) custom-call(f32[512,128]{1,0:T(8,128)S(1)} %bitcast.5), custom_call_target="tpu_custom_call" | custom-call | flops 2000000 | bytes 262144 | tf_op jit(solution)/shard_map/stencil/pallas_call | solution.py:559
  41.3 7.4 %forward_final.1 = (f32[3,8,8,512]{3,2,1,0:T(8,128)S(1)}, s32[81,8,128]{2,1,0:T(8,128)S(1)}, s32[21,8,128]{2,1,0:T(8,128)S(1)}) custom-call(f32[16,8,512]{2,1,0:T(8,128)S(1)} %get-tuple-element.34.winds, f32[24,8,512]{2,1,0:T(8,128)S(1)} %get-tuple-element.35.forces, f32[16,8,512]{2,1,0:T(8,128)S(1)} %get-tuple-element.42.winds_below, ...), custom_call_target="tpu_custom_call" | custom-call | flops 2000000 | bytes 8417280 | tf_op jit(solution)/shard_map/forward_final/pallas_call | solution.py:559
  48.6 5.2 %collective-permute-start.5 = (s32[81,8,128]{2,1,0:T(8,128)S(1)}, s32[81,8,128]{2,1,0:T(8,128)S(1)}, u32[]{:S(2)}, u32[]{:S(2)}) collective-permute-start(s32[81,8,128]{2,1,0:T(8,128)S(1)} %get-tuple-element.53), channel_id=1, source_target_pairs={{1,0},{2,1},{3,2},{4,3},{5,4},{6,5},{7,6},{8,7},{9,8},{10,9},{11,1... | collective-permute-start | bytes 995336 | tf_op jit(solution)/shard_map/ppermute | solution.py:578
  53.8 2.7 %collective-permute-start.6 = (s32[21,8,128]{2,1,0:T(8,128)S(1)}, s32[21,8,128]{2,1,0:T(8,128)S(1)}, u32[]{:S(2)}, u32[]{:S(2)}) collective-permute-start(s32[21,8,128]{2,1,0:T(8,128)S(1)} %get-tuple-element.54), channel_id=1, source_target_pairs={{2,0},{3,1},{4,2},{5,3},{6,4},{7,5},{8,6},{9,7},{10,8},{11,9},{12,... | collective-permute-start | bytes 258056 | tf_op jit(solution)/shard_map/ppermute | solution.py:578
  56.5 3.9 %collective-permute-done.6.source_edge = s32[21,8,128]{2,1,0:T(8,128)S(1)} collective-permute-done((s32[21,8,128]{2,1,0:T(8,128)S(1)}, s32[21,8,128]{2,1,0:T(8,128)S(1)}, u32[]{:S(2)}, u32[]{:S(2)}) %collective-permute-start.6) | collective-permute-done | bytes 86048 | tf_op jit(solution)/shard_map/ppermute | solution.py:578
  61.3 1.3 %collective-permute-start.8 = (s32[21,8,128]{2,1,0:T(8,128)S(1)}, s32[21,8,128]{2,1,0:T(8,128)S(1)}, u32[]{:S(2)}, u32[]{:S(2)}) collective-permute-start(s32[21,8,128]{2,1,0:T(8,128)S(1)} %get-tuple-element.59), channel_id=1, source_target_pairs={{65,0},{66,1},{67,2},{68,3},{69,4},{70,5},{71,6},{72,7},{73,8},{74... | collective-permute-start | bytes 258056 | tf_op jit(solution)/shard_map/ppermute | solution.py:578
  62.6 1.3 %collective-permute-start.7 = (s32[17,8,128]{2,1,0:T(8,128)S(1)}, s32[17,8,128]{2,1,0:T(8,128)S(1)}, u32[]{:S(2)}, u32[]{:S(2)}) collective-permute-start(s32[17,8,128]{2,1,0:T(8,128)S(1)} %get-tuple-element.58), channel_id=1, source_target_pairs={{64,0},{65,1},{66,2},{67,3},{68,4},{69,5},{70,6},{71,7},{72,8},{73... | collective-permute-start | bytes 208904 | tf_op jit(solution)/shard_map/ppermute | solution.py:578
  63.9 7.9 %collective-permute-done.7.after_own = s32[17,8,128]{2,1,0:T(8,128)S(1)} collective-permute-done((s32[17,8,128]{2,1,0:T(8,128)S(1)}, s32[17,8,128]{2,1,0:T(8,128)S(1)}, u32[]{:S(2)}, u32[]{:S(2)}) %collective-permute-start.7) | collective-permute-done | bytes 69664 | tf_op jit(solution)/shard_map/ppermute | solution.py:578
  72.6 1.3 %collective-permute-start.10 = (s32[25,8,128]{2,1,0:T(8,128)S(1)}, s32[25,8,128]{2,1,0:T(8,128)S(1)}, u32[]{:S(2)}, u32[]{:S(2)}) collective-permute-start(s32[25,8,128]{2,1,0:T(8,128)S(1)} %get-tuple-element.62), channel_id=1, source_target_pairs={{129,0},{130,1},{131,2},{132,3},{133,4},{134,5},{135,6},{136,7},{1... | collective-permute-start | bytes 307208 | tf_op jit(solution)/shard_map/ppermute | solution.py:578
  73.9 1.3 %collective-permute-start.9 = (s32[17,8,128]{2,1,0:T(8,128)S(1)}, s32[17,8,128]{2,1,0:T(8,128)S(1)}, u32[]{:S(2)}, u32[]{:S(2)}) collective-permute-start(s32[17,8,128]{2,1,0:T(8,128)S(1)} %get-tuple-element.61), channel_id=1, source_target_pairs={{128,0},{129,1},{130,2},{131,3},{132,4},{133,5},{134,6},{135,7},{1... | collective-permute-start | bytes 208904 | tf_op jit(solution)/shard_map/ppermute | solution.py:578
  75.2 8.6 %collective-permute-done.9.pair_own = s32[17,8,128]{2,1,0:T(8,128)S(1)} collective-permute-done((s32[17,8,128]{2,1,0:T(8,128)S(1)}, s32[17,8,128]{2,1,0:T(8,128)S(1)}, u32[]{:S(2)}, u32[]{:S(2)}) %collective-permute-start.9) | collective-permute-done | bytes 69664 | tf_op jit(solution)/shard_map/ppermute | solution.py:578
  83.9 1.8 %adjoint_final.1 = f32[3,8,8,512]{3,2,1,0:T(8,128)} custom-call(f32[3,8,8,512]{3,2,1,0:T(8,128)S(1)} %get-tuple-element.52.source, f32[24,8,512]{2,1,0:T(8,128)S(1)} %get-tuple-element.55.unpacked, f32[16,8,512]{2,1,0:T(8,128)S(1)} %get-tuple-element.34.winds, f32[16,8,512]{2,1,0:T(8,128)S(1)} %get-tuple-element.56.winds_above, ...), custom_call_target="tpu_custom_call" | custom-call | flops 2000000 | bytes 1769472 | tf_op jit(solution)/shard_map/adjoint_final/pallas_call | solution.py:559
  (10 shorter events, 1.7 us)
Async XLA Ops:
  1.6 21.0 %collective-permute-start = (s32[81,8,128]{2,1,0:T(8,128)S(1)}, s32[81,8,128]{2,1,0:T(8,128)S(1)}, u32[]{:S(2)}, u32[]{:S(2)}) collective-permute-start(s32[81,8,128]{2,1,0:T(8,128)S(1)} %get-tuple-element.36), channel_id=1, source_target_pairs={{0,1},{1,2},{2,3},{3,4},{4,5},{5,6},{6,7},{7,8},{8,9},{9,10},{10,1... | collective-permute-start | bytes 995336 | tf_op jit(solution)/shard_map/ppermute | solution.py:578
  3.6 19.1 %collective-permute-start.1 = (s32[69,8,128]{2,1,0:T(8,128)S(1)}, s32[69,8,128]{2,1,0:T(8,128)S(1)}, u32[]{:S(2)}, u32[]{:S(2)}) collective-permute-start(s32[69,8,128]{2,1,0:T(8,128)S(1)} %get-tuple-element.37), channel_id=1, source_target_pairs={{0,2},{1,3},{2,4},{3,5},{4,6},{5,7},{6,8},{7,9},{8,10},{9,11},{10,... | collective-permute-start | bytes 847880 | tf_op jit(solution)/shard_map/ppermute | solution.py:578
  11.0 27.9 %all-to-all-start = ((f32[64,8,128]{2,1,0:T(8,128)}), f32[64,8,128]{2,1,0:T(8,128)S(1)}, u32[]{:S(2)}, u32[]{:S(2)}) async-start(f32[64,8,128]{2,1,0:T(8,128)} %bitcast.3), calls=%async_computation | async-start | bytes 524288 | tf_op jit(solution)/shard_map/all_to_all | solution.py:626
  23.7 7.0 %collective-permute-start.2 = (s32[37,8,128]{2,1,0:T(8,128)S(1)}, s32[37,8,128]{2,1,0:T(8,128)S(1)}, u32[]{:S(2)}, u32[]{:S(2)}) collective-permute-start(s32[37,8,128]{2,1,0:T(8,128)S(1)} %get-tuple-element.45), channel_id=1, source_target_pairs={{0,64},{1,65},{2,66},{3,67},{4,68},{5,69},{6,70},{7,71},{8,72},{9,... | collective-permute-start | bytes 454664 | tf_op jit(solution)/shard_map/ppermute | solution.py:578
  31.5 9.7 %collective-permute-start.4 = (s32[25,8,128]{2,1,0:T(8,128)S(1)}, s32[25,8,128]{2,1,0:T(8,128)S(1)}, u32[]{:S(2)}, u32[]{:S(2)}) collective-permute-start(s32[25,8,128]{2,1,0:T(8,128)S(1)} %get-tuple-element.48), channel_id=1, source_target_pairs={{0,129},{1,130},{2,131},{3,132},{4,133},{5,134},{6,135},{7,136},{8... | collective-permute-start | bytes 307208 | tf_op jit(solution)/shard_map/ppermute | solution.py:578
  36.5 4.8 %collective-permute-start.3 = (s32[17,8,128]{2,1,0:T(8,128)S(1)}, s32[17,8,128]{2,1,0:T(8,128)S(1)}, u32[]{:S(2)}, u32[]{:S(2)}) collective-permute-start(s32[17,8,128]{2,1,0:T(8,128)S(1)} %get-tuple-element.47), channel_id=1, source_target_pairs={{0,128},{1,129},{2,130},{3,131},{4,132},{5,133},{6,134},{7,135},{8... | collective-permute-start | bytes 208904 | tf_op jit(solution)/shard_map/ppermute | solution.py:578
  48.6 11.8 %collective-permute-start.5 = (s32[81,8,128]{2,1,0:T(8,128)S(1)}, s32[81,8,128]{2,1,0:T(8,128)S(1)}, u32[]{:S(2)}, u32[]{:S(2)}) collective-permute-start(s32[81,8,128]{2,1,0:T(8,128)S(1)} %get-tuple-element.53), channel_id=1, source_target_pairs={{1,0},{2,1},{3,2},{4,3},{5,4},{6,5},{7,6},{8,7},{9,8},{10,9},{11,1... | collective-permute-start | bytes 995336 | tf_op jit(solution)/shard_map/ppermute | solution.py:578
  53.8 6.6 %collective-permute-start.6 = (s32[21,8,128]{2,1,0:T(8,128)S(1)}, s32[21,8,128]{2,1,0:T(8,128)S(1)}, u32[]{:S(2)}, u32[]{:S(2)}) collective-permute-start(s32[21,8,128]{2,1,0:T(8,128)S(1)} %get-tuple-element.54), channel_id=1, source_target_pairs={{2,0},{3,1},{4,2},{5,3},{6,4},{7,5},{8,6},{9,7},{10,8},{11,9},{12,... | collective-permute-start | bytes 258056 | tf_op jit(solution)/shard_map/ppermute | solution.py:578
  61.3 10.5 %collective-permute-start.8 = (s32[21,8,128]{2,1,0:T(8,128)S(1)}, s32[21,8,128]{2,1,0:T(8,128)S(1)}, u32[]{:S(2)}, u32[]{:S(2)}) collective-permute-start(s32[21,8,128]{2,1,0:T(8,128)S(1)} %get-tuple-element.59), channel_id=1, source_target_pairs={{65,0},{66,1},{67,2},{68,3},{69,4},{70,5},{71,6},{72,7},{73,8},{74... | collective-permute-start | bytes 258056 | tf_op jit(solution)/shard_map/ppermute | solution.py:578
  62.6 9.2 %collective-permute-start.7 = (s32[17,8,128]{2,1,0:T(8,128)S(1)}, s32[17,8,128]{2,1,0:T(8,128)S(1)}, u32[]{:S(2)}, u32[]{:S(2)}) collective-permute-start(s32[17,8,128]{2,1,0:T(8,128)S(1)} %get-tuple-element.58), channel_id=1, source_target_pairs={{64,0},{65,1},{66,2},{67,3},{68,4},{69,5},{70,6},{71,7},{72,8},{73... | collective-permute-start | bytes 208904 | tf_op jit(solution)/shard_map/ppermute | solution.py:578
  72.6 11.2 %collective-permute-start.10 = (s32[25,8,128]{2,1,0:T(8,128)S(1)}, s32[25,8,128]{2,1,0:T(8,128)S(1)}, u32[]{:S(2)}, u32[]{:S(2)}) collective-permute-start(s32[25,8,128]{2,1,0:T(8,128)S(1)} %get-tuple-element.62), channel_id=1, source_target_pairs={{129,0},{130,1},{131,2},{132,3},{133,4},{134,5},{135,6},{136,7},{1... | collective-permute-start | bytes 307208 | tf_op jit(solution)/shard_map/ppermute | solution.py:578
  73.9 9.9 %collective-permute-start.9 = (s32[17,8,128]{2,1,0:T(8,128)S(1)}, s32[17,8,128]{2,1,0:T(8,128)S(1)}, u32[]{:S(2)}, u32[]{:S(2)}) collective-permute-start(s32[17,8,128]{2,1,0:T(8,128)S(1)} %get-tuple-element.61), channel_id=1, source_target_pairs={{128,0},{129,1},{130,2},{131,3},{132,4},{133,5},{134,6},{135,7},{1... | collective-permute-start | bytes 208904 | tf_op jit(solution)/shard_map/ppermute | solution.py:578

commit v4 on v3

--- a/solution.py
+++ b/solution.py
@@ -123,16 +123,15 @@
     return result
 
 
-def adjoint_step(current, wind_x, wind_y, high):
-    result = {}
-    for row in range(high - 1):
+def adjoint_step(current, wind_x, wind_y, low):
+    result = {low - 1: wind_y(low) * current[low]}
+    for row in range(low, ROWS):
         here = current[row]
-        along, across = wind_x(row), wind_y(row)
-        result[row] = (
-            here * (1.0 - along - across)
-            + pltpu.roll(along * here, WIDTH - 1, 1)
-            + wind_y(row + 1) * current[row + 1]
-        )
+        along = wind_x(row)
+        value = here * (1.0 - along - wind_y(row)) + pltpu.roll(along * here, WIDTH - 1, 1)
+        if row + 1 < ROWS:
+            value = value + wind_y(row + 1) * current[row + 1]
+        result[row] = value
     return result
 
 
@@ -143,22 +142,20 @@
     return current, low
 
 
-def adjoint_steps(current, winds, high, count):
+def adjoint_steps(current, winds, low, count):
     for _ in range(count):
-        current = adjoint_step(current, winds[0], winds[1], high)
-        high -= 1
-    return current, high
+        current = adjoint_step(current, winds[0], winds[1], low)
+        low -= 1
+    return current, low
 
 
 WINDS = 2
 FIELDS = WINDS + SUBS
-UP_EDGE = 4
 EXTRA = 4
 REACH = 10
+DROP = 6
 DOWN_ROWS = [(sub, row) for sub in range(SUBS) for row in range(2 * sub, ROWS)]
 WIND_TILES = ROWS * TILE_COLUMNS
-FORCE_TILES = message_tiles(SUBS * ROWS)
-EDGE_TILES = message_tiles(2)
 
 
 def lower_winds(winds, winds_below, edge):
@@ -169,20 +166,6 @@
             if row >= -ROWS:
                 return winds_below[field * ROWS + row + ROWS]
             return edge[field * ROWS + row + 2 * ROWS]
-
-        return read
-
-    return [reader(field) for field in range(WINDS)]
-
-
-def upper_winds(winds, winds_above, edge):
-    def reader(field):
-        def read(row):
-            if row < ROWS:
-                return winds[field * ROWS + row]
-            if row < 2 * ROWS:
-                return winds_above[field * ROWS + row - ROWS]
-            return edge[field * UP_EDGE + row - 2 * ROWS]
 
         return read
 
@@ -351,53 +334,55 @@
     lax.fori_loop(0, SUBS, one_sub, 0)
 
 
+def respond(slots, mixing, sub, chunk, found, spread):
+    size = PIECES * LEVELS
+    record = slots[sub, pl.ds(chunk * LEVELS, LEVELS), :]
+    adjoint = -slots[sub, pl.ds(TILES + chunk * LEVELS, LEVELS), :]
+    piece = jnp.right_shift(record.astype(jnp.int32), 8)
+    sums = []
+    wanted = []
+    for corner in range(CORNERS):
+        wanted.append(jnp.broadcast_to(piece[corner : corner + 1], (LEVELS, LANES)))
+        part = pl.ds(corner * LANES, LANES)
+        value = None
+        for number in range(PIECES):
+            both = (
+                found[sub, chunk, pl.ds(number * LEVELS, LEVELS), part]
+                + found[sub, chunk, pl.ds(size + number * LEVELS, LEVELS), part]
+            )
+            value = both if value is None else jnp.where(wanted[corner] == number, both, value)
+        sums.append(value)
+    values = (sums[0] + sums[1]) + (sums[2] + sums[3])
+    for level in range(LEVELS):
+        adjoint = adjoint + mixing[level] * values[level : level + 1]
+    sources = [part.astype(f32) for part in split(adjoint)]
+    for corner in range(CORNERS):
+        part = pl.ds(corner * LANES, LANES)
+        for place, source in enumerate(sources):
+            spread[sub, chunk, pl.ds(place * size, size), part] = jnp.concatenate(
+                [jnp.where(wanted[corner] == number, source, 0.0) for number in range(PIECES)],
+                axis=0,
+            ).astype(bf16)
+
+
 def observe(slots, stencil, mixing, states, found, spread):
     size = PIECES * LEVELS
-
-    def one_sub(sub, _):
-        top, low = split(states[sub])
-        left = jnp.concatenate([top, low], axis=0)
+    for sub in range(SUBS):
+        left = jnp.concatenate(split(states[sub]), axis=0)
         for chunk in range(CHUNKS):
-            found[chunk] = jnp.dot(left, stencil[sub, chunk], preferred_element_type=f32)
+            found[sub, chunk] = jnp.dot(left, stencil[sub, chunk], preferred_element_type=f32)
+    results = []
+    for sub in range(SUBS):
         for chunk in range(CHUNKS):
-            record = slots[sub, pl.ds(chunk * LEVELS, LEVELS), :]
-            adjoint = -slots[sub, pl.ds(TILES + chunk * LEVELS, LEVELS), :]
-            piece = jnp.right_shift(record.astype(jnp.int32), 8)
-            sums = []
-            wanted = []
-            for corner in range(CORNERS):
-                wanted.append(jnp.broadcast_to(piece[corner : corner + 1], (LEVELS, LANES)))
-                part = pl.ds(corner * LANES, LANES)
-                value = None
-                for number in range(PIECES):
-                    both = (
-                        found[chunk, pl.ds(number * LEVELS, LEVELS), part]
-                        + found[chunk, pl.ds(size + number * LEVELS, LEVELS), part]
-                    )
-                    value = both if value is None else jnp.where(wanted[corner] == number, both, value)
-                sums.append(value)
-            values = (sums[0] + sums[1]) + (sums[2] + sums[3])
-            for level in range(LEVELS):
-                adjoint = adjoint + mixing[level] * values[level : level + 1]
-            first, second = split(adjoint)
-            sources = first.astype(f32), second.astype(f32)
-            for corner in range(CORNERS):
-                part = pl.ds(corner * LANES, LANES)
-                for place, source in enumerate(sources):
-                    spread[chunk, pl.ds(place * size, size), part] = jnp.concatenate(
-                        [jnp.where(wanted[corner] == number, source, 0.0) for number in range(PIECES)],
-                        axis=0,
-                    ).astype(bf16)
+            respond(slots, mixing, sub, chunk, found, spread)
         total = jnp.zeros((2 * size, HALF), f32)
         for chunk in range(CHUNKS):
             total = total + lax.dot_general(
-                spread[chunk], stencil[sub, chunk], (((1,), (1,)), ((), ())),
+                spread[sub, chunk], stencil[sub, chunk], (((1,), (1,)), ((), ())),
                 preferred_element_type=f32,
             )
-        states[sub] = total[:size] + total[size:]
-        return 0
-
-    lax.fori_loop(0, SUBS, one_sub, 0)
+        results.append(total[:size] + total[size:])
+    return results
 
 
 def forward_local_kernel(
@@ -444,7 +429,7 @@
 def forward_final_kernel(
     winds, forces, winds_below, lower_edge, forces_below,
     before, pair_own, pair_extended, slots, stencil, mixing,
-    result, result_above, result_edge,
+    sources, mine, response,
     states, found, spread,
 ):
     across = lower_winds(winds, winds_below, lower_edge)
@@ -462,87 +447,86 @@
                 states[sub, place : place + LEVELS, :] = current[row][
                     :, half * HALF : (half + 1) * HALF
                 ]
-    observe(slots, stencil, mixing, states, found, spread)
-    listed = []
-    for sub in range(SUBS):
+    for sub, stack in enumerate(observe(slots, stencil, mixing, states, found, spread)):
         for row in range(ROWS):
-            places = [(2 * row + half) * LEVELS for half in range(2)]
-            value = jnp.concatenate(
-                [states[sub, place : place + LEVELS, :] for place in places], axis=1
-            )
-            result[sub, row] = value
-            listed.append(value)
-    encode(listed, result_above)
-    encode_winds(winds, range(ROWS), result_above, FORCE_TILES)
-    encode(listed[-ROWS : 2 - ROWS], result_edge)
-    encode_winds(winds, range(UP_EDGE), result_edge, EDGE_TILES)
-
-
-def adjoint_local_kernel(
-    source, source_above, source_edge, winds,
-    own, extended, mine, unpacked, winds_above, upper_edge,
-):
-    unpack_winds(source_above, ROWS, winds_above, FORCE_TILES)
-    unpack_winds(source_edge, UP_EDGE, upper_edge, EDGE_TILES)
-    across = upper_winds(winds, winds_above, upper_edge)
-    high = 2 * ROWS + 2
-    above = decode(source_above, SUBS * ROWS)
-    edge = decode(source_edge, 2)
-    for number, row in enumerate(above):
-        unpacked[number] = row
-
-    def source_row(sub):
-        return lambda row: source[sub, row] if row < ROWS else unpacked[sub * ROWS + row - ROWS]
-
-    current = {row: source_row(SUBS - 1)(row) for row in range(2 * ROWS)}
-    for number, row in enumerate(edge):
-        current[2 * ROWS + number] = row
-    current, high = adjoint_steps(current, across, high, 2)
+            for half in range(2):
+                place = (2 * row + half) * LEVELS
+                sources[sub * ROWS + row, :, half * HALF : (half + 1) * HALF] = stack[
+                    place : place + LEVELS
+                ]
+    current = {row: sources[(SUBS - 1) * ROWS + row] for row in range(ROWS)}
+    current, low = adjoint_steps(current, across, 0, 2)
     for sub in reversed(range(SUBS - 1)):
-        current = add_rows(current, source_row(sub), 0, high)
-        current, high = adjoint_steps(current, across, high, 2)
-    listed = [current[row] for row in range(ROWS + EXTRA)]
+        current = add_sources(current, sources, sub)
+        current, low = adjoint_steps(current, across, low, 2)
+    listed = [current[row] for row in range(low, ROWS)]
     for number, row in enumerate(listed):
         mine[number] = row
-    encode(listed[:ROWS], own)
-    encode(listed[:REACH], extended)
-
-
-def upper_state(own, extended, high, count):
-    here = decode(own, ROWS)
-    over = decode(extended, count)
-    return {row: here[row] if row < ROWS else over[row - ROWS] for row in range(high)}
-
-
-def adjoint_pair_kernel(
-    winds, winds_above, upper_edge, mine, after_own, after_extended, own, extended
+    encode(listed, response)
+
+
+def add_sources(current, sources, sub):
+    return {
+        row: value + sources[sub * ROWS + row] if row >= 0 else value
+        for row, value in current.items()
+    }
+
+
+def after_state(message):
+    rows = decode(message, DROP + ROWS)
+    return {row: rows[row + DROP] for row in range(-DROP, ROWS)}
+
+
+def adjoint_pair_kernel(winds, winds_below, lower_edge, mine, after, own, extended):
+    across = lower_winds(winds, winds_below, lower_edge)
+    current, low = adjoint_steps(after_state(after), across, -DROP, 6)
+    for row in range(-DROP, ROWS):
+        current[row] = current[row] + mine[row + DROP]
+    encode([current[row] for row in range(ROWS)], own)
+    encode([current[row] for row in range(low, 0)], extended)
+
+
+PUSHED = [(sub, row) for sub in range(SUBS) for row in range(ROWS)]
+PUSHED_FAR = [(sub, row) for sub in range(SUBS) for row in range(2 * sub, ROWS)]
+
+
+def adjoint_final_kernel(
+    sources, winds, winds_below, lower_edge, after, pair_own, pair_extended,
+    gradient, pushed, pushed_far,
 ):
-    across = upper_winds(winds, winds_above, upper_edge)
-    high = 2 * ROWS + 2
-    current, high = adjoint_steps(upper_state(after_own, after_extended, high, REACH), across, high, 6)
-    listed = [current[row] + mine[row] for row in range(ROWS + EXTRA)]
-    encode(listed[:ROWS], own)
-    encode(listed, extended)
-
-
-def adjoint_final_kernel(
-    source, unpacked, winds, winds_above, upper_edge,
-    after_own, after_extended, pair_own, pair_extended, gradient_far, gradient, sems,
-):
-    across = upper_winds(winds, winds_above, upper_edge)
-    high = 2 * ROWS + EXTRA
-    current, high = adjoint_steps(upper_state(pair_own, pair_extended, high, ROWS + EXTRA), across, high, 6)
-    after = upper_state(after_own, after_extended, high, REACH)
-    current = {row: current[row] + after[row] for row in current}
-
-    def source_row(sub):
-        return lambda row: source[sub, row] if row < ROWS else unpacked[sub * ROWS + row - ROWS]
-
+    across = lower_winds(winds, winds_below, lower_edge)
+    own = decode(pair_own, ROWS)
+    above = decode(pair_extended, ROWS + EXTRA)
+    low = -EXTRA
+    current = {
+        row: above[row + EXTRA] + own[row] if row >= 0 else above[row + EXTRA]
+        for row in range(low, ROWS)
+    }
+    current, low = adjoint_steps(current, across, low, 6)
+    after = after_state(after)
+    for row in after:
+        current[row] = current[row] + after[row]
+    results = [None] * SUBS
+    for sub in reversed(range(SUBS)):
+        current = add_sources(current, sources, sub)
+        current, low = adjoint_steps(current, across, low, 2)
+        results[sub] = current
+        for row in range(ROWS):
+            gradient[sub * ROWS + row] = current[row]
+    encode([results[sub][row - ROWS] for sub, row in PUSHED], pushed)
+    encode([results[sub][row - 2 * ROWS] for sub, row in PUSHED_FAR], pushed_far)
+
+
+def finish_kernel(part, pushed, pushed_far, gradient_far, gradient, sems):
+    near = dict(zip(PUSHED, decode(pushed, len(PUSHED))))
+    far = dict(zip(PUSHED_FAR, decode(pushed_far, len(PUSHED_FAR))))
     copies = []
-    for sub in reversed(range(SUBS)):
-        current = add_rows(current, source_row(sub), 0, high)
-        current, high = adjoint_steps(current, across, high, 2)
-        gradient[sub] = jnp.swapaxes(jnp.stack([current[row] for row in range(ROWS)]), 0, 1)
+    for sub in range(SUBS):
+        rows = []
+        for row in range(ROWS):
+            value = part[sub * ROWS + row] + near[sub, row]
+            rows.append(value + far[sub, row] if (sub, row) in far else value)
+        gradient[sub] = jnp.swapaxes(jnp.stack(rows), 0, 1)
         copies.append(
             pltpu.make_async_copy(gradient.at[sub], gradient_far.at[sub], sems.at[sub])
         )
@@ -589,7 +573,7 @@
         (
             struct(WINDS * ROWS, LEVELS, WIDTH),
             struct(SUBS * ROWS, LEVELS, WIDTH),
-            message(WIND_TILES + FORCE_TILES),
+            message(WIND_TILES + message_tiles(SUBS * ROWS)),
             message(WIND_TILES + message_tiles(len(DOWN_ROWS))),
         ),
         (forcing, courant),
@@ -659,12 +643,12 @@
         name="stencil",
     )
     size = PIECES * LEVELS
-    source, source_above, source_edge = run(
+    sources, mine, response = run(
         forward_final_kernel,
         (
-            struct(SUBS, ROWS, LEVELS, WIDTH),
-            message(FORCE_TILES + WIND_TILES),
-            message(EDGE_TILES + UP_EDGE * TILE_COLUMNS),
+            struct(SUBS * ROWS, LEVELS, WIDTH),
+            struct(DROP + ROWS, LEVELS, WIDTH),
+            message(message_tiles(DROP + ROWS)),
         ),
         (
             winds, forces, winds_below, lower_edge, forces_below,
@@ -672,44 +656,41 @@
         ),
         scratch=(
             pltpu.VMEM((SUBS, size, HALF), f32),
-            pltpu.VMEM((CHUNKS, 2 * size, CORNERS * LANES), f32),
-            pltpu.VMEM((CHUNKS, 2 * size, CORNERS * LANES), bf16),
+            pltpu.VMEM((SUBS, CHUNKS, 2 * size, CORNERS * LANES), f32),
+            pltpu.VMEM((SUBS, CHUNKS, 2 * size, CORNERS * LANES), bf16),
         ),
         name="forward_final",
     )
 
-    source_above = moved(source_above, 0, -1)
-    source_edge = moved(source_edge, 0, -2)
-    own, extended, mine, unpacked, winds_above, upper_edge = run(
-        adjoint_local_kernel,
-        (
-            message(message_tiles(ROWS)),
-            message(message_tiles(REACH)),
-            struct(ROWS + EXTRA, LEVELS, WIDTH),
-            struct(SUBS * ROWS, LEVELS, WIDTH),
-            struct(WINDS * ROWS, LEVELS, WIDTH),
-            struct(WINDS * UP_EDGE, LEVELS, WIDTH),
-        ),
-        (source, source_above, source_edge, winds),
-        name="adjoint_local",
-    )
-    after = (moved(own, -1, 0), moved(extended, -1, -1))
+    after = moved(response, -1, 0)
     own, extended = run(
         adjoint_pair_kernel,
         pair_shapes,
-        (winds, winds_above, upper_edge, mine, *after),
+        (winds, winds_below, lower_edge, mine, after),
         name="adjoint_pair",
     )
     pair = (moved(own, -2, 0), moved(extended, -2, -1))
+    part, pushed, pushed_far = run(
+        adjoint_final_kernel,
+        (
+            struct(SUBS * ROWS, LEVELS, WIDTH),
+            message(message_tiles(len(PUSHED))),
+            message(message_tiles(len(PUSHED_FAR))),
+        ),
+        (sources, winds, winds_below, lower_edge, after, *pair),
+        name="adjoint_final",
+    )
+    pushed = moved(pushed, 0, -1)
+    pushed_far = moved(pushed_far, 0, -2)
     return run(
-        adjoint_final_kernel,
+        finish_kernel,
         struct(SUBS, LEVELS, ROWS, WIDTH),
-        (source, unpacked, winds, winds_above, upper_edge, *after, *pair),
+        (part, pushed, pushed_far),
         scratch=(
             pltpu.VMEM((SUBS, LEVELS, ROWS, WIDTH), f32),
             pltpu.SemaphoreType.DMA((SUBS,)),
         ),
-        name="adjoint_final",
+        name="finish",
         far_out=True,
     )
 

time: 86.2 us -> 81.3 us (0.943)
  starting transfers between devices: 41.2 us -> 38 us
  Pallas kernels: 20.3 us -> 19.2 us
    ppermute x11 -> x10, starting transfers between devices: 29.6 us -> 26.4 us  [moved(): return lax.ppermute(array, ('tm', 'space'), pairs)]
    pallas_call x10, Pallas kernels: 20.3 us -> 19.2 us  [run(): pl.pallas_call(kernel, out_shape=outputs, in_specs=[pl.BlockSpec(memory_s...]
    ppermute x11 -> x10, waiting for transfers between devices: 24 us -> 23.5 us  [moved(): return lax.ppermute(array, ('tm', 'space'), pairs)]
  transfers between devices with their start and end apart: 12 -> 11, of which waited for: 4 -> 4; matrix products, arithmetic and copies ran while one was open for 0% -> 0% of each run, Pallas kernels for 9% -> 10%
where the time goes in v4:
time: 81.3 us; the launch traced here: 80.9 us
  starting transfers between devices  38 us (47%)
  waiting for transfers between devices  23.5 us (29%)
  Pallas kernels  19.2 us (24%)
    ppermute x10, starting transfers between devices, moved(): return lax.ppermute(array, ('tm', 'space'), pairs)  26.4 us
    ppermute x10, waiting for transfers between devices, moved(): return lax.ppermute(array, ('tm', 'space'), pairs)  23.5 us
    pallas_call x10, Pallas kernels, run(): pl.pallas_call(kernel, out_shape=outputs, in_specs=[pl.BlockSpec(memory_s...  19.2 us
    all_to_all x1, starting transfers between devices, shards(): lax.all_to_all(send.reshape(TILES, 8, LANES), 'space', split_axis=0, conc...  11.6 us
  transfers between devices with their start and end apart: 11, of which 4 were waited for; matrix products, arithmetic and copies ran while one was open for 0% of the time, Pallas kernels for 10%

profile of v4, /device:TPU:4, one launch (start us, length us, event | category | flops | bytes accessed | tf_op | source)
XLA Modules:
  0.0 80.9 jit_solution(1843564850109979202)
XLA Ops:
  0.0 1.6 %rows.1 = (f32[16,8,512]{2,1,0:T(8,128)S(1)}, f32[24,8,512]{2,1,0:T(8,128)S(1)}, s32[81,8,128]{2,1,0:T(8,128)S(1)}, s32[69,8,128]{2,1,0:T(8,128)S(1)}) custom-call(f32[3,8,8,512]{3,2,1,0:T(8,128)} %forcing_far.1, f32[2,8,8,512]{3,2,1,0:T(8,128)} %courant_far.1), custom_call_target="tpu_custom_call" | custom-call | flops 2000000 | bytes 655360 | tf_op jit(solution)/shard_map/rows/pallas_call | solution.py:543
  1.6 1.9 %collective-permute-start = (s32[81,8,128]{2,1,0:T(8,128)S(1)}, s32[81,8,128]{2,1,0:T(8,128)S(1)}, u32[]{:S(2)}, u32[]{:S(2)}) collective-permute-start(s32[81,8,128]{2,1,0:T(8,128)S(1)} %get-tuple-element.33), channel_id=1, source_target_pairs={{0,1},{1,2},{2,3},{3,4},{4,5},{5,6},{6,7},{7,8},{8,9},{9,10},{10,1... | collective-permute-start | bytes 995336 | tf_op jit(solution)/shard_map/ppermute | solution.py:562
  3.6 3.8 %collective-permute-start.1 = (s32[69,8,128]{2,1,0:T(8,128)S(1)}, s32[69,8,128]{2,1,0:T(8,128)S(1)}, u32[]{:S(2)}, u32[]{:S(2)}) collective-permute-start(s32[69,8,128]{2,1,0:T(8,128)S(1)} %get-tuple-element.34), channel_id=1, source_target_pairs={{0,2},{1,3},{2,4},{3,5},{4,6},{5,7},{6,8},{7,9},{8,10},{9,11},{10,... | collective-permute-start | bytes 847880 | tf_op jit(solution)/shard_map/ppermute | solution.py:562
  7.4 2.4 %choose.1 = (f32[6,256,128]{2,1,0:T(8,128)S(1)}, f32[3,64,256]{2,1,0:T(8,128)S(1)}, f32[8,8,128]{2,1,0:T(8,128)S(1)}) custom-call(bf16[3,256,256]{2,1,0:T(8,128)(2,1)} %innovation_far.1, s32[3,4,256]{2,1,0:T(4,128)} %cells_far.1, bf16[3,4,256]{2,1,0:T(4,128)(2,1)} %weight_far.1, s32[3,1,256]{2,1,0:T(1,128)} %bitcast.7, f32[8,256]{1,0:T(8,128)} %bitcast.6, ...), custom_call_target="tpu_custom_call" | custom-call | flops 2000000 | bytes 423936 | tf_op jit(solution)/shard_map/choose/pallas_call | solution.py:543
  9.8 1.2 %place.1 = f32[512,128]{1,0:T(8,128)} custom-call(f32[6,256,128]{2,1,0:T(8,128)S(1)} %get-tuple-element.35.chosen, f32[3,64,256]{2,1,0:T(8,128)S(1)} %get-tuple-element.36.target), custom_call_target="tpu_custom_call" | custom-call | flops 2000000 | bytes 983040 | tf_op jit(solution)/shard_map/place/pallas_call | solution.py:543
  11.0 11.6 %all-to-all-start = ((f32[64,8,128]{2,1,0:T(8,128)}), f32[64,8,128]{2,1,0:T(8,128)S(1)}, u32[]{:S(2)}, u32[]{:S(2)}) async-start(f32[64,8,128]{2,1,0:T(8,128)} %bitcast.3), calls=%async_computation | async-start | bytes 524288 | tf_op jit(solution)/shard_map/all_to_all | solution.py:610
  22.7 1.0 %forward_local.1 = (s32[37,8,128]{2,1,0:T(8,128)S(1)}, f32[12,8,512]{2,1,0:T(8,128)S(1)}, f32[16,8,512]{2,1,0:T(8,128)S(1)}, f32[16,8,512]{2,1,0:T(8,128)S(1)}, f32[24,8,512]{2,1,0:T(8,128)S(1)}) custom-call(f32[16,8,512]{2,1,0:T(8,128)S(1)} %get-tuple-element.31.winds, f32[24,8,512]{2,1,0:T(8,128)S(1)} %get-tuple-element.32.forces, ...), custom_call_target="tpu_custom_call" | custom-call | flops 2000000 | bytes 1269760 | tf_op jit(solution)/shard_map/forward_local/pallas_call | solution.py:543
  23.7 3.5 %collective-permute-start.2 = (s32[37,8,128]{2,1,0:T(8,128)S(1)}, s32[37,8,128]{2,1,0:T(8,128)S(1)}, u32[]{:S(2)}, u32[]{:S(2)}) collective-permute-start(s32[37,8,128]{2,1,0:T(8,128)S(1)} %get-tuple-element.42), channel_id=1, source_target_pairs={{0,64},{1,65},{2,66},{3,67},{4,68},{5,69},{6,70},{7,71},{8,72},{9,... | collective-permute-start | bytes 454664 | tf_op jit(solution)/shard_map/ppermute | solution.py:562
  27.2 3.5 %collective-permute-done.2.before = s32[37,8,128]{2,1,0:T(8,128)S(1)} collective-permute-done((s32[37,8,128]{2,1,0:T(8,128)S(1)}, s32[37,8,128]{2,1,0:T(8,128)S(1)}, u32[]{:S(2)}, u32[]{:S(2)}) %collective-permute-start.2) | collective-permute-done | bytes 151584 | tf_op jit(solution)/shard_map/ppermute | solution.py:562
  31.5 4.9 %collective-permute-start.4 = (s32[25,8,128]{2,1,0:T(8,128)S(1)}, s32[25,8,128]{2,1,0:T(8,128)S(1)}, u32[]{:S(2)}, u32[]{:S(2)}) collective-permute-start(s32[25,8,128]{2,1,0:T(8,128)S(1)} %get-tuple-element.45), channel_id=1, source_target_pairs={{0,129},{1,130},{2,131},{3,132},{4,133},{5,134},{6,135},{7,136},{8... | collective-permute-start | bytes 307208 | tf_op jit(solution)/shard_map/ppermute | solution.py:562
  36.5 2.4 %collective-permute-start.3 = (s32[17,8,128]{2,1,0:T(8,128)S(1)}, s32[17,8,128]{2,1,0:T(8,128)S(1)}, u32[]{:S(2)}, u32[]{:S(2)}) collective-permute-start(s32[17,8,128]{2,1,0:T(8,128)S(1)} %get-tuple-element.44), channel_id=1, source_target_pairs={{0,128},{1,129},{2,130},{3,131},{4,132},{5,133},{6,134},{7,135},{8... | collective-permute-start | bytes 208904 | tf_op jit(solution)/shard_map/ppermute | solution.py:562
  38.9 2.4 %stencil.1 = (f32[3,128,128]{2,1,0:T(8,128)S(1)}, bf16[3,8,256,512]{3,2,1,0:T(8,128)(2,1)S(1)}) custom-call(f32[512,128]{1,0:T(8,128)S(1)} %bitcast.5), custom_call_target="tpu_custom_call" | custom-call | flops 2000000 | bytes 262144 | tf_op jit(solution)/shard_map/stencil/pallas_call | solution.py:543
  41.3 6.4 %forward_final.1 = (f32[24,8,512]{2,1,0:T(8,128)S(1)}, f32[14,8,512]{2,1,0:T(8,128)S(1)}, s32[29,8,128]{2,1,0:T(8,128)S(1)}) custom-call(f32[16,8,512]{2,1,0:T(8,128)S(1)} %get-tuple-element.31.winds, f32[24,8,512]{2,1,0:T(8,128)S(1)} %get-tuple-element.32.forces, f32[16,8,512]{2,1,0:T(8,128)S(1)} %get-tuple-element.39.winds_below, ...), custom_call_target="tpu_custom_call" | custom-call | flops 2000000 | bytes 8417280 | tf_op jit(solution)/shard_map/forward_final/pallas_call | solution.py:543
  47.6 1.3 %collective-permute-start.5 = (s32[29,8,128]{2,1,0:T(8,128)S(1)}, s32[29,8,128]{2,1,0:T(8,128)S(1)}, u32[]{:S(2)}, u32[]{:S(2)}) collective-permute-start(s32[29,8,128]{2,1,0:T(8,128)S(1)} %get-tuple-element.50), channel_id=1, source_target_pairs={{64,0},{65,1},{66,2},{67,3},{68,4},{69,5},{70,6},{71,7},{72,8},{73... | collective-permute-start | bytes 356360 | tf_op jit(solution)/shard_map/ppermute | solution.py:562
  48.9 6.4 %collective-permute-done.5.after = s32[29,8,128]{2,1,0:T(8,128)S(1)} collective-permute-done((s32[29,8,128]{2,1,0:T(8,128)S(1)}, s32[29,8,128]{2,1,0:T(8,128)S(1)}, u32[]{:S(2)}, u32[]{:S(2)}) %collective-permute-start.5) | collective-permute-done | bytes 118816 | tf_op jit(solution)/shard_map/ppermute | solution.py:562
  55.3 0.9 %adjoint_pair.1 = (s32[17,8,128]{2,1,0:T(8,128)S(1)}, s32[25,8,128]{2,1,0:T(8,128)S(1)}) custom-call(f32[16,8,512]{2,1,0:T(8,128)S(1)} %get-tuple-element.31.winds, f32[16,8,512]{2,1,0:T(8,128)S(1)} %get-tuple-element.39.winds_below, f32[16,8,512]{2,1,0:T(8,128)S(1)} %get-tuple-element.40.lower_edge, f32[14,8,512]{2,1,0:T(8,128)S(1)} %get-tuple-element.51.mine, ...), custom_call_target="tpu_custom_call" | custom-call | flops 2000000 | bytes 1134592 | tf_op jit(solution)/shard_map/adjoint_pair/pallas_call | solution.py:543
  56.2 1.3 %collective-permute-start.7 = (s32[25,8,128]{2,1,0:T(8,128)S(1)}, s32[25,8,128]{2,1,0:T(8,128)S(1)}, u32[]{:S(2)}, u32[]{:S(2)}) collective-permute-start(s32[25,8,128]{2,1,0:T(8,128)S(1)} %get-tuple-element.53), channel_id=1, source_target_pairs={{129,0},{130,1},{131,2},{132,3},{133,4},{134,5},{135,6},{136,7},{1... | collective-permute-start | bytes 307208 | tf_op jit(solution)/shard_map/ppermute | solution.py:562
  57.5 1.3 %collective-permute-start.6 = (s32[17,8,128]{2,1,0:T(8,128)S(1)}, s32[17,8,128]{2,1,0:T(8,128)S(1)}, u32[]{:S(2)}, u32[]{:S(2)}) collective-permute-start(s32[17,8,128]{2,1,0:T(8,128)S(1)} %get-tuple-element.52), channel_id=1, source_target_pairs={{128,0},{129,1},{130,2},{131,3},{132,4},{133,5},{134,6},{135,7},{1... | collective-permute-start | bytes 208904 | tf_op jit(solution)/shard_map/ppermute | solution.py:562
  58.8 8.6 %collective-permute-done.6.pair_own = s32[17,8,128]{2,1,0:T(8,128)S(1)} collective-permute-done((s32[17,8,128]{2,1,0:T(8,128)S(1)}, s32[17,8,128]{2,1,0:T(8,128)S(1)}, u32[]{:S(2)}, u32[]{:S(2)}) %collective-permute-start.6) | collective-permute-done | bytes 69664 | tf_op jit(solution)/shard_map/ppermute | solution.py:562
  67.4 1.5 %adjoint_final.1 = (f32[24,8,512]{2,1,0:T(8,128)S(1)}, s32[49,8,128]{2,1,0:T(8,128)S(1)}, s32[37,8,128]{2,1,0:T(8,128)S(1)}) custom-call(f32[24,8,512]{2,1,0:T(8,128)S(1)} %get-tuple-element.49.sources, f32[16,8,512]{2,1,0:T(8,128)S(1)} %get-tuple-element.31.winds, f32[16,8,512]{2,1,0:T(8,128)S(1)} %get-tuple-element.39.winds_below, ...), custom_call_target="tpu_custom_call" | custom-call | flops 2000000 | bytes 1470464 | tf_op jit(solution)/shard_map/adjoint_final/pallas_call | solution.py:543
  68.9 3.9 %collective-permute-start.8 = (s32[49,8,128]{2,1,0:T(8,128)S(1)}, s32[49,8,128]{2,1,0:T(8,128)S(1)}, u32[]{:S(2)}, u32[]{:S(2)}) collective-permute-start(s32[49,8,128]{2,1,0:T(8,128)S(1)} %get-tuple-element.55), channel_id=1, source_target_pairs={{1,0},{2,1},{3,2},{4,3},{5,4},{6,5},{7,6},{8,7},{9,8},{10,9},{11,1... | collective-permute-start | bytes 602120 | tf_op jit(solution)/shard_map/ppermute | solution.py:562
  72.9 2.0 %collective-permute-start.9 = (s32[37,8,128]{2,1,0:T(8,128)S(1)}, s32[37,8,128]{2,1,0:T(8,128)S(1)}, u32[]{:S(2)}, u32[]{:S(2)}) collective-permute-start(s32[37,8,128]{2,1,0:T(8,128)S(1)} %get-tuple-element.56), channel_id=1, source_target_pairs={{2,0},{3,1},{4,2},{5,3},{6,4},{7,5},{8,6},{9,7},{10,8},{11,9},{12,... | collective-permute-start | bytes 454664 | tf_op jit(solution)/shard_map/ppermute | solution.py:562
  74.9 5.1 %collective-permute-done.9.pushed_far = s32[37,8,128]{2,1,0:T(8,128)S(1)} collective-permute-done((s32[37,8,128]{2,1,0:T(8,128)S(1)}, s32[37,8,128]{2,1,0:T(8,128)S(1)}, u32[]{:S(2)}, u32[]{:S(2)}) %collective-permute-start.9) | collective-permute-done | bytes 151584 | tf_op jit(solution)/shard_map/ppermute | solution.py:562
  80.0 0.9 %finish.1 = f32[3,8,8,512]{3,2,1,0:T(8,128)} custom-call(f32[24,8,512]{2,1,0:T(8,128)S(1)} %get-tuple-element.54.part, s32[49,8,128]{2,1,0:T(8,128)S(1)} %collective-permute-done.8.pushed, s32[37,8,128]{2,1,0:T(8,128)S(1)} %collective-permute-done.9.pushed_far), custom_call_target="tpu_custom_call" | custom-call | flops 2000000 | bytes 745472 | tf_op jit(solution)/shard_map/finish/pallas_call | solution.py:543
  (8 shorter events, 0.9 us)
Async XLA Ops:
  1.6 21.0 %collective-permute-start = (s32[81,8,128]{2,1,0:T(8,128)S(1)}, s32[81,8,128]{2,1,0:T(8,128)S(1)}, u32[]{:S(2)}, u32[]{:S(2)}) collective-permute-start(s32[81,8,128]{2,1,0:T(8,128)S(1)} %get-tuple-element.33), channel_id=1, source_target_pairs={{0,1},{1,2},{2,3},{3,4},{4,5},{5,6},{6,7},{7,8},{8,9},{9,10},{10,1... | collective-permute-start | bytes 995336 | tf_op jit(solution)/shard_map/ppermute | solution.py:562
  3.6 19.1 %collective-permute-start.1 = (s32[69,8,128]{2,1,0:T(8,128)S(1)}, s32[69,8,128]{2,1,0:T(8,128)S(1)}, u32[]{:S(2)}, u32[]{:S(2)}) collective-permute-start(s32[69,8,128]{2,1,0:T(8,128)S(1)} %get-tuple-element.34), channel_id=1, source_target_pairs={{0,2},{1,3},{2,4},{3,5},{4,6},{5,7},{6,8},{7,9},{8,10},{9,11},{10,... | collective-permute-start | bytes 847880 | tf_op jit(solution)/shard_map/ppermute | solution.py:562
  11.0 27.9 %all-to-all-start = ((f32[64,8,128]{2,1,0:T(8,128)}), f32[64,8,128]{2,1,0:T(8,128)S(1)}, u32[]{:S(2)}, u32[]{:S(2)}) async-start(f32[64,8,128]{2,1,0:T(8,128)} %bitcast.3), calls=%async_computation | async-start | bytes 524288 | tf_op jit(solution)/shard_map/all_to_all | solution.py:610
  23.7 7.0 %collective-permute-start.2 = (s32[37,8,128]{2,1,0:T(8,128)S(1)}, s32[37,8,128]{2,1,0:T(8,128)S(1)}, u32[]{:S(2)}, u32[]{:S(2)}) collective-permute-start(s32[37,8,128]{2,1,0:T(8,128)S(1)} %get-tuple-element.42), channel_id=1, source_target_pairs={{0,64},{1,65},{2,66},{3,67},{4,68},{5,69},{6,70},{7,71},{8,72},{9,... | collective-permute-start | bytes 454664 | tf_op jit(solution)/shard_map/ppermute | solution.py:562
  31.5 9.7 %collective-permute-start.4 = (s32[25,8,128]{2,1,0:T(8,128)S(1)}, s32[25,8,128]{2,1,0:T(8,128)S(1)}, u32[]{:S(2)}, u32[]{:S(2)}) collective-permute-start(s32[25,8,128]{2,1,0:T(8,128)S(1)} %get-tuple-element.45), channel_id=1, source_target_pairs={{0,129},{1,130},{2,131},{3,132},{4,133},{5,134},{6,135},{7,136},{8... | collective-permute-start | bytes 307208 | tf_op jit(solution)/shard_map/ppermute | solution.py:562
  36.5 4.8 %collective-permute-start.3 = (s32[17,8,128]{2,1,0:T(8,128)S(1)}, s32[17,8,128]{2,1,0:T(8,128)S(1)}, u32[]{:S(2)}, u32[]{:S(2)}) collective-permute-start(s32[17,8,128]{2,1,0:T(8,128)S(1)} %get-tuple-element.44), channel_id=1, source_target_pairs={{0,128},{1,129},{2,130},{3,131},{4,132},{5,133},{6,134},{7,135},{8... | collective-permute-start | bytes 208904 | tf_op jit(solution)/shard_map/ppermute | solution.py:562
  47.6 7.7 %collective-permute-start.5 = (s32[29,8,128]{2,1,0:T(8,128)S(1)}, s32[29,8,128]{2,1,0:T(8,128)S(1)}, u32[]{:S(2)}, u32[]{:S(2)}) collective-permute-start(s32[29,8,128]{2,1,0:T(8,128)S(1)} %get-tuple-element.50), channel_id=1, source_target_pairs={{64,0},{65,1},{66,2},{67,3},{68,4},{69,5},{70,6},{71,7},{72,8},{73... | collective-permute-start | bytes 356360 | tf_op jit(solution)/shard_map/ppermute | solution.py:562
  56.2 11.2 %collective-permute-start.7 = (s32[25,8,128]{2,1,0:T(8,128)S(1)}, s32[25,8,128]{2,1,0:T(8,128)S(1)}, u32[]{:S(2)}, u32[]{:S(2)}) collective-permute-start(s32[25,8,128]{2,1,0:T(8,128)S(1)} %get-tuple-element.53), channel_id=1, source_target_pairs={{129,0},{130,1},{131,2},{132,3},{133,4},{134,5},{135,6},{136,7},{1... | collective-permute-start | bytes 307208 | tf_op jit(solution)/shard_map/ppermute | solution.py:562
  57.5 9.9 %collective-permute-start.6 = (s32[17,8,128]{2,1,0:T(8,128)S(1)}, s32[17,8,128]{2,1,0:T(8,128)S(1)}, u32[]{:S(2)}, u32[]{:S(2)}) collective-permute-start(s32[17,8,128]{2,1,0:T(8,128)S(1)} %get-tuple-element.52), channel_id=1, source_target_pairs={{128,0},{129,1},{130,2},{131,3},{132,4},{133,5},{134,6},{135,7},{1... | collective-permute-start | bytes 208904 | tf_op jit(solution)/shard_map/ppermute | solution.py:562
  68.9 11.0 %collective-permute-start.8 = (s32[49,8,128]{2,1,0:T(8,128)S(1)}, s32[49,8,128]{2,1,0:T(8,128)S(1)}, u32[]{:S(2)}, u32[]{:S(2)}) collective-permute-start(s32[49,8,128]{2,1,0:T(8,128)S(1)} %get-tuple-element.55), channel_id=1, source_target_pairs={{1,0},{2,1},{3,2},{4,3},{5,4},{6,5},{7,6},{8,7},{9,8},{10,9},{11,1... | collective-permute-start | bytes 602120 | tf_op jit(solution)/shard_map/ppermute | solution.py:562
  72.9 7.1 %collective-permute-start.9 = (s32[37,8,128]{2,1,0:T(8,128)S(1)}, s32[37,8,128]{2,1,0:T(8,128)S(1)}, u32[]{:S(2)}, u32[]{:S(2)}) collective-permute-start(s32[37,8,128]{2,1,0:T(8,128)S(1)} %get-tuple-element.56), channel_id=1, source_target_pairs={{2,0},{3,1},{4,2},{5,3},{6,4},{7,5},{8,6},{9,7},{10,8},{11,9},{12,... | collective-permute-start | bytes 454664 | tf_op jit(solution)/shard_map/ppermute | solution.py:562

commit v5 on v4

--- a/solution.py
+++ b/solution.py
@@ -151,6 +151,7 @@
 
 WINDS = 2
 FIELDS = WINDS + SUBS
+RECORD_ARRAYS = 6
 EXTRA = 4
 REACH = 10
 DROP = 6
@@ -200,12 +201,14 @@
     return copies
 
 
-def rows_kernel(
-    forcing_far, courant_far, winds, forces, below, down_edge, forcing, courant, sems
-):
+def rows_kernel(*refs):
+    forcing_far, courant_far, *records_far = refs[: 2 + RECORD_ARRAYS]
+    winds, forces, below, down_edge, *records = refs[2 + RECORD_ARRAYS : 6 + 2 * RECORD_ARRAYS]
+    forcing, courant, sems = refs[6 + 2 * RECORD_ARRAYS :]
     copies = fetch(
         [(courant_far.at[field], courant.at[field]) for field in range(WINDS)]
-        + [(forcing_far.at[sub], forcing.at[sub]) for sub in range(SUBS)],
+        + [(forcing_far.at[sub], forcing.at[sub]) for sub in range(SUBS)]
+        + list(zip(records_far, records)),
         sems,
     )
     for copy in copies[:WINDS]:
@@ -222,6 +225,8 @@
         rows += [turned[row] for row in range(ROWS)]
     encode(rows, below, WIND_TILES)
     encode([rows[sub * ROWS + row] for sub, row in DOWN_ROWS], down_edge, WIND_TILES)
+    for copy in copies[FIELDS:]:
+        copy.wait()
 
 
 def encode_winds(winds, rows, message, start):
@@ -237,21 +242,14 @@
         result[rows + row] = second
 
 
-def choose_kernel(
-    innovation_far, cells_far, weight_far, owner_far, channel_far, rinv_far,
-    chosen, target, mixing,
-    innovation, cells, weight, owner, channel_weight, rinv, sems,
-):
-    copies = fetch(
-        [
-            (channel_far, channel_weight), (rinv_far, rinv), (owner_far, owner),
-            (cells_far, cells), (weight_far, weight),
-        ]
-        + [(innovation_far.at[sub], innovation.at[sub]) for sub in range(SUBS)],
-        sems,
-    )
-    for copy in copies:
-        copy.wait()
+def three(value):
+    top = value.astype(bf16)
+    rest = value - top.astype(f32)
+    middle = rest.astype(bf16)
+    return top, middle, (rest - middle.astype(f32)).astype(bf16)
+
+
+def pack_kernel(innovation, cells, weight, owner, channel_weight, rinv, send, mixing):
     sub_id = lax.broadcasted_iota(jnp.int32, (RECORDS, RECORDS), 0)
     lane_id = lax.broadcasted_iota(jnp.int32, (RECORDS, RECORDS), 1)
     not_later = lane_id <= sub_id
@@ -263,27 +261,22 @@
     )
     for level in range(LEVELS):
         mixing[level] = jnp.broadcast_to(matrix[:, level : level + 1], (LEVELS, LANES))
-    top = scaled.astype(bf16)
-    rest = scaled - top.astype(f32)
-    middle = rest.astype(bf16)
-    low = (rest - middle.astype(f32)).astype(bf16)
+    scaled = jnp.concatenate(three(scaled), axis=0)
 
     spread_row = lax.broadcasted_iota(jnp.int32, (2 * LEVELS, LANES), 0)
     spread_lane = lax.broadcasted_iota(jnp.int32, (2 * LEVELS, LANES), 1)
-    repeat = (
-        (spread_lane // 64 == spread_row // LEVELS) & (spread_lane % LEVELS == spread_row % LEVELS)
-    ).astype(f32)
+    repeat = jnp.where(
+        (spread_lane // 64 == spread_row // LEVELS) & (spread_lane % LEVELS == spread_row % LEVELS),
+        1.0,
+        0.0,
+    ).astype(bf16)
     slot_lane = lax.broadcasted_iota(jnp.int32, (RECORDS, LANES), 1)
     slot_rank = ((slot_lane % 64) // LEVELS) * 2
     tile_id = lax.broadcasted_iota(jnp.int32, (TILES, RECORDS), 0)
     ones = jnp.ones((RECORDS, LANES), bf16)
     for sub in range(SUBS):
-        data = innovation[sub]
-        projected = (
-            jnp.dot(top, data, preferred_element_type=f32)
-            + jnp.dot(middle, data, preferred_element_type=f32)
-            + jnp.dot(low, data, preferred_element_type=f32)
-        )
+        parts = jnp.dot(scaled, innovation[sub], preferred_element_type=f32)
+        projected = (parts[:LEVELS] + parts[LEVELS : 2 * LEVELS]) + parts[2 * LEVELS :]
         payload = jnp.concatenate(
             [cells[sub].astype(f32), weight[sub].astype(f32), projected], axis=0
         )
@@ -291,22 +284,20 @@
         owner_rows = jnp.broadcast_to(owner_row, (RECORDS, RECORDS))
         earlier = jnp.where((owner_rows.T == owner_rows) & not_later, 1.0, 0.0).astype(bf16)
         rank = jnp.dot(earlier, ones, preferred_element_type=f32).astype(jnp.int32) - 1
-        repeated = lax.dot_general(
-            payload, repeat, (((0,), (0,)), ((), ())),
-            precision=highest, preferred_element_type=f32,
-        )
-        target[sub] = (tile_id == owner_row).astype(f32)
+        target = jnp.where(tile_id == owner_row, 1.0, 0.0).astype(bf16)
+        repeated = [
+            lax.dot_general(part, repeat, (((0,), (0,)), ((), ())), preferred_element_type=f32)
+            for part in three(payload)
+        ]
         for half in range(2):
-            chosen[2 * sub + half] = jnp.where(rank == slot_rank + half, repeated, 0.0)
-
-
-def place_kernel(chosen, target, send):
-    for sub in range(SUBS):
-        for half in range(2):
-            send[pl.ds(2 * sub + half, TILES, stride=8), :] = jnp.dot(
-                target[sub], chosen[2 * sub + half],
-                precision=highest, preferred_element_type=f32,
-            )
+            chosen = rank == slot_rank + half
+            placed = [
+                jnp.dot(
+                    target, jnp.where(chosen, part, 0.0).astype(bf16), preferred_element_type=f32
+                )
+                for part in repeated
+            ]
+            send[pl.ds(2 * sub + half, TILES, stride=8), :] = (placed[0] + placed[1]) + placed[2]
     for spare in range(2 * SUBS, 8):
         send[pl.ds(spare, TILES, stride=8), :] = jnp.zeros((TILES, LANES), f32)
 
@@ -365,24 +356,35 @@
             ).astype(bf16)
 
 
-def observe(slots, stencil, mixing, states, found, spread):
+def interpolate(state, stencil, sub, found):
+    left = jnp.concatenate(split(state), axis=0)
+    for chunk in range(CHUNKS):
+        found[sub, chunk] = jnp.dot(left, stencil[sub, chunk], preferred_element_type=f32)
+
+
+def scatter(slots, stencil, mixing, sub, found, spread):
     size = PIECES * LEVELS
-    for sub in range(SUBS):
-        left = jnp.concatenate(split(states[sub]), axis=0)
-        for chunk in range(CHUNKS):
-            found[sub, chunk] = jnp.dot(left, stencil[sub, chunk], preferred_element_type=f32)
-    results = []
-    for sub in range(SUBS):
-        for chunk in range(CHUNKS):
-            respond(slots, mixing, sub, chunk, found, spread)
-        total = jnp.zeros((2 * size, HALF), f32)
-        for chunk in range(CHUNKS):
-            total = total + lax.dot_general(
-                spread[sub, chunk], stencil[sub, chunk], (((1,), (1,)), ((), ())),
-                preferred_element_type=f32,
-            )
-        results.append(total[:size] + total[size:])
-    return results
+    for chunk in range(CHUNKS):
+        respond(slots, mixing, sub, chunk, found, spread)
+    total = jnp.zeros((2 * size, HALF), f32)
+    for chunk in range(CHUNKS):
+        total = total + lax.dot_general(
+            spread[sub, chunk], stencil[sub, chunk], (((1,), (1,)), ((), ())),
+            preferred_element_type=f32,
+        )
+    return total[:size] + total[size:]
+
+
+def stacked(rows):
+    return jnp.concatenate(
+        [rows[row][:, half * HALF : (half + 1) * HALF] for row in range(ROWS) for half in range(2)],
+        axis=0,
+    )
+
+
+def unstacked(stack, row):
+    places = [(2 * row + half) * LEVELS for half in range(2)]
+    return jnp.concatenate([stack[place : place + LEVELS] for place in places], axis=1)
 
 
 def forward_local_kernel(
@@ -402,62 +404,72 @@
         current = add_rows(current, forced[sub], low, ROWS)
         current, low = forward_steps(current, across, low, 2)
     listed = [current[row] for row in range(-REACH, ROWS)]
-    for number, row in enumerate(listed[REACH - EXTRA :]):
+    for number, row in enumerate(listed):
         mine[number] = row
     encode(listed, own)
 
 
-def before_state(message, low):
-    rows = decode(message, REACH + ROWS)
-    return {row: rows[row + REACH] for row in range(low, ROWS)}
-
-
-def lower_state(own, extended, low):
+def time_is(condition):
+    index = jnp.full((LEVELS, WIDTH), lax.axis_index("tm"), jnp.int32)
+    return condition(index)
+
+
+def lower_state(own, extended):
     here = decode(own, ROWS)
     under = decode(extended, ROWS + EXTRA)
-    return {row: here[row] if row >= 0 else under[row + ROWS + EXTRA] for row in range(low, ROWS)}
-
-
-def forward_pair_kernel(winds, winds_below, lower_edge, mine, before, own, extended):
-    across = lower_winds(winds, winds_below, lower_edge)
-    current, low = forward_steps(before_state(before, -REACH), across, -REACH, 6)
-    listed = [current[row] + mine[row + EXTRA] for row in range(-EXTRA, ROWS)]
-    encode(listed[EXTRA:], own)
-    encode(listed, extended)
+    return {
+        row: here[row] if row >= 0 else under[row + ROWS + EXTRA]
+        for row in range(-(ROWS + EXTRA), ROWS)
+    }
+
+
+def forward_pair_kernel(winds, winds_below, lower_edge, mine, other, own, extended):
+    @pl.when(lax.axis_index("tm") < 2)
+    def _():
+        across = lower_winds(winds, winds_below, lower_edge)
+        first = time_is(lambda index: index == 0)
+        rows = decode(other, REACH + ROWS)
+        current = {
+            row: jnp.where(first, mine[row + REACH], rows[row + REACH])
+            for row in range(-REACH, ROWS)
+        }
+        current, low = forward_steps(current, across, -REACH, 6)
+        listed = [
+            current[row] + jnp.where(first, rows[row + REACH], mine[row + REACH])
+            for row in range(-EXTRA, ROWS)
+        ]
+        encode(listed[EXTRA:], own)
+        encode(listed, extended)
 
 
 def forward_final_kernel(
     winds, forces, winds_below, lower_edge, forces_below,
     before, pair_own, pair_extended, slots, stencil, mixing,
     sources, mine, response,
-    states, found, spread,
+    found, spread,
 ):
     across = lower_winds(winds, winds_below, lower_edge)
     forced = lower_forces(forces, forces_below)
-    low = -(ROWS + EXTRA)
-    current, low = forward_steps(lower_state(pair_own, pair_extended, low), across, low, 6)
-    before = before_state(before, low)
-    current = {row: current[row] + before[row] for row in current}
+    half_way = lower_state(pair_own, pair_extended)
+    current, low = forward_steps(half_way, across, -(ROWS + EXTRA), 6)
+    before = decode(before, REACH + ROWS)
+    third = time_is(lambda index: index == 2)
+    odd = time_is(lambda index: (index & 1) == 1)
+    current = {
+        row: jnp.where(third, half_way[row], value) + jnp.where(odd, before[row + REACH], 0.0)
+        for row, value in current.items()
+    }
     for sub in range(SUBS):
         current = add_rows(current, forced[sub], low, ROWS)
         current, low = forward_steps(current, across, low, 2)
+        interpolate(stacked(current), stencil, sub, found)
+    current, low = {}, 0
+    for sub in reversed(range(SUBS)):
+        stack = scatter(slots, stencil, mixing, sub, found, spread)
         for row in range(ROWS):
-            for half in range(2):
-                place = (2 * row + half) * LEVELS
-                states[sub, place : place + LEVELS, :] = current[row][
-                    :, half * HALF : (half + 1) * HALF
-                ]
-    for sub, stack in enumerate(observe(slots, stencil, mixing, states, found, spread)):
-        for row in range(ROWS):
-            for half in range(2):
-                place = (2 * row + half) * LEVELS
-                sources[sub * ROWS + row, :, half * HALF : (half + 1) * HALF] = stack[
-                    place : place + LEVELS
-                ]
-    current = {row: sources[(SUBS - 1) * ROWS + row] for row in range(ROWS)}
-    current, low = adjoint_steps(current, across, 0, 2)
-    for sub in reversed(range(SUBS - 1)):
-        current = add_sources(current, sources, sub)
+            value = unstacked(stack, row)
+            sources[sub * ROWS + row] = value
+            current[row] = current[row] + value if row in current else value
         current, low = adjoint_steps(current, across, low, 2)
     listed = [current[row] for row in range(low, ROWS)]
     for number, row in enumerate(listed):
@@ -472,18 +484,20 @@
     }
 
 
-def after_state(message):
-    rows = decode(message, DROP + ROWS)
-    return {row: rows[row + DROP] for row in range(-DROP, ROWS)}
-
-
-def adjoint_pair_kernel(winds, winds_below, lower_edge, mine, after, own, extended):
-    across = lower_winds(winds, winds_below, lower_edge)
-    current, low = adjoint_steps(after_state(after), across, -DROP, 6)
-    for row in range(-DROP, ROWS):
-        current[row] = current[row] + mine[row + DROP]
-    encode([current[row] for row in range(ROWS)], own)
-    encode([current[row] for row in range(low, 0)], extended)
+def adjoint_pair_kernel(winds, winds_below, lower_edge, mine, other, own, extended):
+    @pl.when(lax.axis_index("tm") >= 2)
+    def _():
+        across = lower_winds(winds, winds_below, lower_edge)
+        last = time_is(lambda index: index == 3)
+        rows = decode(other, DROP + ROWS)
+        current = {
+            row: jnp.where(last, mine[row + DROP], rows[row + DROP]) for row in range(-DROP, ROWS)
+        }
+        current, low = adjoint_steps(current, across, -DROP, 6)
+        for row in range(-DROP, ROWS):
+            current[row] = current[row] + jnp.where(last, rows[row + DROP], mine[row + DROP])
+        encode([current[row] for row in range(ROWS)], own)
+        encode([current[row] for row in range(low, 0)], extended)
 
 
 PUSHED = [(sub, row) for sub in range(SUBS) for row in range(ROWS)]
@@ -498,14 +512,18 @@
     own = decode(pair_own, ROWS)
     above = decode(pair_extended, ROWS + EXTRA)
     low = -EXTRA
-    current = {
+    half_way = {
         row: above[row + EXTRA] + own[row] if row >= 0 else above[row + EXTRA]
         for row in range(low, ROWS)
     }
-    current, low = adjoint_steps(current, across, low, 6)
-    after = after_state(after)
-    for row in after:
-        current[row] = current[row] + after[row]
+    current, low = adjoint_steps(half_way, across, low, 6)
+    after = decode(after, DROP + ROWS)
+    second = time_is(lambda index: index == 1)
+    even = time_is(lambda index: (index & 1) == 0)
+    for row in current:
+        current[row] = jnp.where(second, half_way.get(row, 0.0), current[row])
+        if row >= -DROP:
+            current[row] = current[row] + jnp.where(even, after[row + DROP], 0.0)
     results = [None] * SUBS
     for sub in reversed(range(SUBS)):
         current = add_sources(current, sources, sub)
@@ -552,13 +570,18 @@
     )(*arguments)
 
 
+STAY = {part: part for part in range(PARTS)}
+FORWARD_FIRST, FORWARD_SECOND = {0: 1, 1: 0, 2: 3}, {1: 2, 0: 3}
+ADJOINT_FIRST, ADJOINT_SECOND = {3: 2, 2: 3, 1: 0}, {2: 1, 3: 0}
+
+
 def moved(array, parts, tiles):
-    pairs = []
-    for part in range(PARTS):
-        for tile in range(TILES):
-            to_part, to_tile = part + parts, tile + tiles
-            if 0 <= to_part < PARTS and 0 <= to_tile < TILES:
-                pairs.append((part * TILES + tile, to_part * TILES + to_tile))
+    pairs = [
+        (part * TILES + tile, to_part * TILES + tile + tiles)
+        for part, to_part in parts.items()
+        for tile in range(TILES)
+        if 0 <= tile + tiles < TILES
+    ]
     return lax.ppermute(array, ("tm", "space"), pairs)
 
 
@@ -568,45 +591,36 @@
     def message(tiles):
         return struct(tiles, LEVELS, LANES, dtype=jnp.int32)
 
-    winds, forces, below, down_edge = run(
+    records = (
+        innovation, obs_cells, obs_weight, jnp.swapaxes(obs_owner, 1, 2),
+        channel_weight.T, channel_rinv.reshape(1, -1),
+    )
+    winds, forces, below, down_edge, *records = run(
         rows_kernel,
         (
             struct(WINDS * ROWS, LEVELS, WIDTH),
             struct(SUBS * ROWS, LEVELS, WIDTH),
             message(WIND_TILES + message_tiles(SUBS * ROWS)),
             message(WIND_TILES + message_tiles(len(DOWN_ROWS))),
-        ),
-        (forcing, courant),
+            *[struct(*array.shape, dtype=array.dtype) for array in records],
+        ),
+        (forcing, courant, *records),
         scratch=(
             pltpu.VMEM(forcing.shape, f32),
             pltpu.VMEM(courant.shape, f32),
-            pltpu.SemaphoreType.DMA((FIELDS,)),
+            pltpu.SemaphoreType.DMA((FIELDS + RECORD_ARRAYS,)),
         ),
         name="rows",
         far=True,
     )
-    below = moved(below, 0, 1)
-    down_edge = moved(down_edge, 0, 2)
-    records = (
-        innovation, obs_cells, obs_weight, jnp.swapaxes(obs_owner, 1, 2),
-        channel_weight.T, channel_rinv.reshape(1, -1),
-    )
-    chosen, target, mixing = run(
-        choose_kernel,
-        (
-            struct(2 * SUBS, RECORDS, LANES),
-            struct(SUBS, TILES, RECORDS),
-            struct(LEVELS, LEVELS, LANES),
-        ),
+    below = moved(below, STAY, 1)
+    down_edge = moved(down_edge, STAY, 2)
+    send, mixing = run(
+        pack_kernel,
+        (struct(TILES * 8, LANES), struct(LEVELS, LEVELS, LANES)),
         records,
-        scratch=(
-            *[pltpu.VMEM(array.shape, array.dtype) for array in records],
-            pltpu.SemaphoreType.DMA((len(records) + SUBS - 1,)),
-        ),
-        name="choose",
-        far=True,
-    )
-    send = run(place_kernel, struct(TILES * 8, LANES), (chosen, target), name="place")
+        name="pack",
+    )
     received = lax.all_to_all(
         send.reshape(TILES, 8, LANES), "space", split_axis=0, concat_axis=0, tiled=True
     ).reshape(TILES * 8, LANES)
@@ -615,7 +629,7 @@
         forward_local_kernel,
         (
             message(message_tiles(REACH + ROWS)),
-            struct(ROWS + EXTRA, LEVELS, WIDTH),
+            struct(REACH + ROWS, LEVELS, WIDTH),
             struct(WINDS * ROWS, LEVELS, WIDTH),
             struct(WINDS * ROWS, LEVELS, WIDTH),
             struct(SUBS * ROWS, LEVELS, WIDTH),
@@ -623,7 +637,7 @@
         (winds, forces, below, down_edge),
         name="forward_local",
     )
-    before = moved(own, 1, 0)
+    before = moved(own, FORWARD_FIRST, 0)
     pair_shapes = (message(message_tiles(ROWS)), message(message_tiles(ROWS + EXTRA)))
     own, extended = run(
         forward_pair_kernel,
@@ -631,7 +645,7 @@
         (winds, winds_below, lower_edge, mine, before),
         name="forward_pair",
     )
-    pair = (moved(own, 2, 0), moved(extended, 2, 1))
+    pair = (moved(own, FORWARD_SECOND, 0), moved(extended, FORWARD_SECOND, 1))
     slots, stencil = run(
         stencil_kernel,
         (
@@ -655,21 +669,20 @@
             before, *pair, slots, stencil, mixing,
         ),
         scratch=(
-            pltpu.VMEM((SUBS, size, HALF), f32),
             pltpu.VMEM((SUBS, CHUNKS, 2 * size, CORNERS * LANES), f32),
             pltpu.VMEM((SUBS, CHUNKS, 2 * size, CORNERS * LANES), bf16),
         ),
         name="forward_final",
     )
 
-    after = moved(response, -1, 0)
+    after = moved(response, ADJOINT_FIRST, 0)
     own, extended = run(
         adjoint_pair_kernel,
         pair_shapes,
         (winds, winds_below, lower_edge, mine, after),
         name="adjoint_pair",
     )
-    pair = (moved(own, -2, 0), moved(extended, -2, -1))
+    pair = (moved(own, ADJOINT_SECOND, 0), moved(extended, ADJOINT_SECOND, -1))
     part, pushed, pushed_far = run(
         adjoint_final_kernel,
         (
@@ -680,8 +693,8 @@
         (sources, winds, winds_below, lower_edge, after, *pair),
         name="adjoint_final",
     )
-    pushed = moved(pushed, 0, -1)
-    pushed_far = moved(pushed_far, 0, -2)
+    pushed = moved(pushed, STAY, -1)
+    pushed_far = moved(pushed_far, STAY, -2)
     return run(
         finish_kernel,
         struct(SUBS, LEVELS, ROWS, WIDTH),

time: 81.3 us -> 77.7 us (0.956)
  Pallas kernels: 19.2 us -> 17.1 us
  starting transfers between devices: 38 us -> 36 us
    pallas_call x10 -> x9, Pallas kernels: 19.2 us -> 17.1 us  [run(): pl.pallas_call(kernel, out_shape=outputs, in_specs=[pl.BlockSpec(memory_s...]
    ppermute x10, starting transfers between devices: 26.4 us -> 24.4 us  [moved(): return lax.ppermute(array, ('tm', 'space'), pairs)]
  transfers between devices with their start and end apart: 11 -> 11, of which waited for: 4 -> 4; matrix products, arithmetic and copies ran while one was open for 0% -> 0% of each run, Pallas kernels for 10% -> 8%
where the time goes in v5:
time: 77.7 us; the launch traced here: 77.3 us
  starting transfers between devices  36 us (46%)
  waiting for transfers between devices  24 us (31%)
  Pallas kernels  17.1 us (22%)
    ppermute x10, starting transfers between devices, moved(): return lax.ppermute(array, ('tm', 'space'), pairs)  24.4 us
    ppermute x10, waiting for transfers between devices, moved(): return lax.ppermute(array, ('tm', 'space'), pairs)  24 us
    pallas_call x9, Pallas kernels, run(): pl.pallas_call(kernel, out_shape=outputs, in_specs=[pl.BlockSpec(memory_s...  17.1 us
    all_to_all x1, starting transfers between devices, shards(): lax.all_to_all(send.reshape(TILES, 8, LANES), 'space', split_axis=0, conc...  11.6 us
  transfers between devices with their start and end apart: 11, of which 4 were waited for; matrix products, arithmetic and copies ran while one was open for 0% of the time, Pallas kernels for 8%

profile of v5, /device:TPU:4, one launch (start us, length us, event | category | flops | bytes accessed | tf_op | source)
XLA Modules:
  0.0 77.3 jit_solution(12174978136357359326)
XLA Ops:
  0.0 1.7 %rows.1 = (f32[16,8,512]{2,1,0:T(8,128)S(1)}, f32[24,8,512]{2,1,0:T(8,128)S(1)}, s32[81,8,128]{2,1,0:T(8,128)S(1)}, s32[69,8,128]{2,1,0:T(8,128)S(1)}, bf16[3,25...) custom-call(f32[3,8,8,512]{3,2,1,0:T(8,128)} %refs_0_.1, ...), custom_call_target="tpu_custom_call" | custom-call | flops 2000000 | bytes 1079296 | tf_op jit(solution)/shard_map/rows/pallas_call | solution.py:561
  1.7 1.9 %collective-permute-start = (s32[81,8,128]{2,1,0:T(8,128)S(1)}, s32[81,8,128]{2,1,0:T(8,128)S(1)}, u32[]{:S(2)}, u32[]{:S(2)}) collective-permute-start(s32[81,8,128]{2,1,0:T(8,128)S(1)} %get-tuple-element.38), channel_id=1, source_target_pairs={{0,1},{1,2},{2,3},{3,4},{4,5},{5,6},{6,7},{7,8},{8,9},{9,10},{10,1... | collective-permute-start | bytes 995336 | tf_op jit(solution)/shard_map/ppermute | solution.py:585
  3.6 3.8 %collective-permute-start.1 = (s32[69,8,128]{2,1,0:T(8,128)S(1)}, s32[69,8,128]{2,1,0:T(8,128)S(1)}, u32[]{:S(2)}, u32[]{:S(2)}) collective-permute-start(s32[69,8,128]{2,1,0:T(8,128)S(1)} %get-tuple-element.39), channel_id=1, source_target_pairs={{0,2},{1,3},{2,4},{3,5},{4,6},{5,7},{6,8},{7,9},{8,10},{9,11},{10,... | collective-permute-start | bytes 847880 | tf_op jit(solution)/shard_map/ppermute | solution.py:585
  7.5 2.2 %pack.1 = (f32[512,128]{1,0:T(8,128)}, f32[8,8,128]{2,1,0:T(8,128)S(1)}) custom-call(bf16[3,256,256]{2,1,0:T(8,128)(2,1)S(1)} %get-tuple-element.40.innovation, s32[3,4,256]{2,1,0:T(4,128)S(1)} %get-tuple-element.41.cells, bf16[3,4,256]{2,1,0:T(4,128)(2,1)S(1)} %get-tuple-element.42.weight, s32[3,1,256]{2,1,0:T(1,128)S(1)} %get-tuple-element.43.owner, ...), custom_call_target="tpu_custom_call" | custom-call | flops 2000000 | bytes 423936 | tf_op jit(solution)/shard_map/pack/pallas_call | solution.py:561
  9.6 11.6 %all-to-all-start = ((f32[64,8,128]{2,1,0:T(8,128)}), f32[64,8,128]{2,1,0:T(8,128)S(1)}, u32[]{:S(2)}, u32[]{:S(2)}) async-start(f32[64,8,128]{2,1,0:T(8,128)} %bitcast.3), calls=%async_computation | async-start | bytes 524288 | tf_op jit(solution)/shard_map/all_to_all | solution.py:624
  21.3 0.0 collective-permute-done.1.down_edge
  21.3 1.0 %forward_local.1 = (s32[37,8,128]{2,1,0:T(8,128)S(1)}, f32[18,8,512]{2,1,0:T(8,128)S(1)}, f32[16,8,512]{2,1,0:T(8,128)S(1)}, f32[16,8,512]{2,1,0:T(8,128)S(1)}, f32[24,8,512]{2,1,0:T(8,128)S(1)}) custom-call(f32[16,8,512]{2,1,0:T(8,128)S(1)} %get-tuple-element.36.winds, f32[24,8,512]{2,1,0:T(8,128)S(1)} %get-tuple-element.37.forces, ...), custom_call_target="tpu_custom_call" | custom-call | flops 2000000 | bytes 1269760 | tf_op jit(solution)/shard_map/forward_local/pallas_call | solution.py:561
  22.3 3.5 %collective-permute-start.2 = (s32[37,8,128]{2,1,0:T(8,128)S(1)}, s32[37,8,128]{2,1,0:T(8,128)S(1)}, u32[]{:S(2)}, u32[]{:S(2)}) collective-permute-start(s32[37,8,128]{2,1,0:T(8,128)S(1)} %get-tuple-element.52), channel_id=1, source_target_pairs={{0,64},{1,65},{2,66},{3,67},{4,68},{5,69},{6,70},{7,71},{8,72},{9,... | collective-permute-start | bytes 454664 | tf_op jit(solution)/shard_map/ppermute | solution.py:585
  25.8 4.4 %collective-permute-done.2.other.before = s32[37,8,128]{2,1,0:T(8,128)S(1)} collective-permute-done((s32[37,8,128]{2,1,0:T(8,128)S(1)}, s32[37,8,128]{2,1,0:T(8,128)S(1)}, u32[]{:S(2)}, u32[]{:S(2)}) %collective-permute-start.2) | collective-permute-done | bytes 151584 | tf_op jit(solution)/shard_map/ppermute | solution.py:585
  30.2 0.9 %forward_pair.1 = (s32[17,8,128]{2,1,0:T(8,128)S(1)}, s32[25,8,128]{2,1,0:T(8,128)S(1)}) custom-call(f32[16,8,512]{2,1,0:T(8,128)S(1)} %get-tuple-element.36.winds, f32[16,8,512]{2,1,0:T(8,128)S(1)} %get-tuple-element.49.winds_below, f32[16,8,512]{2,1,0:T(8,128)S(1)} %get-tuple-element.50.lower_edge, f32[18,8,512]{2,1,0:T(8,128)S(1)} %get-tuple-element.53.mine, ...), custom_call_target="tpu_custom_call" | custom-call | flops 2000000 | bytes 1232896 | tf_op jit(solution)/shard_map/forward_pair/pallas_call | solution.py:561
  31.1 3.0 %collective-permute-start.4 = (s32[25,8,128]{2,1,0:T(8,128)S(1)}, s32[25,8,128]{2,1,0:T(8,128)S(1)}, u32[]{:S(2)}, u32[]{:S(2)}) collective-permute-start(s32[25,8,128]{2,1,0:T(8,128)S(1)} %get-tuple-element.55), channel_id=1, source_target_pairs={{64,129},{65,130},{66,131},{67,132},{68,133},{69,134},{70,135},{71... | collective-permute-start | bytes 307208 | tf_op jit(solution)/shard_map/ppermute | solution.py:585
  34.0 2.4 %collective-permute-start.3 = (s32[17,8,128]{2,1,0:T(8,128)S(1)}, s32[17,8,128]{2,1,0:T(8,128)S(1)}, u32[]{:S(2)}, u32[]{:S(2)}) collective-permute-start(s32[17,8,128]{2,1,0:T(8,128)S(1)} %get-tuple-element.54), channel_id=1, source_target_pairs={{64,128},{65,129},{66,130},{67,131},{68,132},{69,133},{70,134},{71... | collective-permute-start | bytes 208904 | tf_op jit(solution)/shard_map/ppermute | solution.py:585
  36.4 2.4 %stencil.1 = (f32[3,128,128]{2,1,0:T(8,128)S(1)}, bf16[3,8,256,512]{3,2,1,0:T(8,128)(2,1)S(1)}) custom-call(f32[512,128]{1,0:T(8,128)S(1)} %bitcast.5), custom_call_target="tpu_custom_call" | custom-call | flops 2000000 | bytes 262144 | tf_op jit(solution)/shard_map/stencil/pallas_call | solution.py:561
  38.8 6.5 %forward_final.1 = (f32[24,8,512]{2,1,0:T(8,128)S(1)}, f32[14,8,512]{2,1,0:T(8,128)S(1)}, s32[29,8,128]{2,1,0:T(8,128)S(1)}) custom-call(f32[16,8,512]{2,1,0:T(8,128)S(1)} %get-tuple-element.36.winds, f32[24,8,512]{2,1,0:T(8,128)S(1)} %get-tuple-element.37.forces, f32[16,8,512]{2,1,0:T(8,128)S(1)} %get-tuple-element.49.winds_below, ...), custom_call_target="tpu_custom_call" | custom-call | flops 2000000 | bytes 8417280 | tf_op jit(solution)/shard_map/forward_final/pallas_call | solution.py:561
  45.4 1.3 %collective-permute-start.5 = (s32[29,8,128]{2,1,0:T(8,128)S(1)}, s32[29,8,128]{2,1,0:T(8,128)S(1)}, u32[]{:S(2)}, u32[]{:S(2)}) collective-permute-start(s32[29,8,128]{2,1,0:T(8,128)S(1)} %get-tuple-element.60), channel_id=1, source_target_pairs={{192,128},{193,129},{194,130},{195,131},{196,132},{197,133},{198,1... | collective-permute-start | bytes 356360 | tf_op jit(solution)/shard_map/ppermute | solution.py:585
  46.7 6.4 %collective-permute-done.5.other.after = s32[29,8,128]{2,1,0:T(8,128)S(1)} collective-permute-done((s32[29,8,128]{2,1,0:T(8,128)S(1)}, s32[29,8,128]{2,1,0:T(8,128)S(1)}, u32[]{:S(2)}, u32[]{:S(2)}) %collective-permute-start.5) | collective-permute-done | bytes 118816 | tf_op jit(solution)/shard_map/ppermute | solution.py:585
  53.0 1.3 %collective-permute-start.7 = (s32[25,8,128]{2,1,0:T(8,128)S(1)}, s32[25,8,128]{2,1,0:T(8,128)S(1)}, u32[]{:S(2)}, u32[]{:S(2)}) collective-permute-start(s32[25,8,128]{2,1,0:T(8,128)S(1)} %get-tuple-element.63), channel_id=1, source_target_pairs={{129,64},{130,65},{131,66},{132,67},{133,68},{134,69},{135,70},{13... | collective-permute-start | bytes 307208 | tf_op jit(solution)/shard_map/ppermute | solution.py:585
  54.3 1.3 %collective-permute-start.6 = (s32[17,8,128]{2,1,0:T(8,128)S(1)}, s32[17,8,128]{2,1,0:T(8,128)S(1)}, u32[]{:S(2)}, u32[]{:S(2)}) collective-permute-start(s32[17,8,128]{2,1,0:T(8,128)S(1)} %get-tuple-element.62), channel_id=1, source_target_pairs={{128,64},{129,65},{130,66},{131,67},{132,68},{133,69},{134,70},{13... | collective-permute-start | bytes 208904 | tf_op jit(solution)/shard_map/ppermute | solution.py:585
  55.6 8.2 %collective-permute-done.6.pair_own = s32[17,8,128]{2,1,0:T(8,128)S(1)} collective-permute-done((s32[17,8,128]{2,1,0:T(8,128)S(1)}, s32[17,8,128]{2,1,0:T(8,128)S(1)}, u32[]{:S(2)}, u32[]{:S(2)}) %collective-permute-start.6) | collective-permute-done | bytes 69664 | tf_op jit(solution)/shard_map/ppermute | solution.py:585
  63.8 1.5 %adjoint_final.1 = (f32[24,8,512]{2,1,0:T(8,128)S(1)}, s32[49,8,128]{2,1,0:T(8,128)S(1)}, s32[37,8,128]{2,1,0:T(8,128)S(1)}) custom-call(f32[24,8,512]{2,1,0:T(8,128)S(1)} %get-tuple-element.59.sources, f32[16,8,512]{2,1,0:T(8,128)S(1)} %get-tuple-element.36.winds, f32[16,8,512]{2,1,0:T(8,128)S(1)} %get-tuple-element.49.winds_below, ...), custom_call_target="tpu_custom_call" | custom-call | flops 2000000 | bytes 1470464 | tf_op jit(solution)/shard_map/adjoint_final/pallas_call | solution.py:561
  65.4 3.9 %collective-permute-start.8 = (s32[49,8,128]{2,1,0:T(8,128)S(1)}, s32[49,8,128]{2,1,0:T(8,128)S(1)}, u32[]{:S(2)}, u32[]{:S(2)}) collective-permute-start(s32[49,8,128]{2,1,0:T(8,128)S(1)} %get-tuple-element.65), channel_id=1, source_target_pairs={{1,0},{2,1},{3,2},{4,3},{5,4},{6,5},{7,6},{8,7},{9,8},{10,9},{11,1... | collective-permute-start | bytes 602120 | tf_op jit(solution)/shard_map/ppermute | solution.py:585
  69.3 2.0 %collective-permute-start.9 = (s32[37,8,128]{2,1,0:T(8,128)S(1)}, s32[37,8,128]{2,1,0:T(8,128)S(1)}, u32[]{:S(2)}, u32[]{:S(2)}) collective-permute-start(s32[37,8,128]{2,1,0:T(8,128)S(1)} %get-tuple-element.66), channel_id=1, source_target_pairs={{2,0},{3,1},{4,2},{5,3},{6,4},{7,5},{8,6},{9,7},{10,8},{11,9},{12,... | collective-permute-start | bytes 454664 | tf_op jit(solution)/shard_map/ppermute | solution.py:585
  71.3 5.1 %collective-permute-done.9.pushed_far = s32[37,8,128]{2,1,0:T(8,128)S(1)} collective-permute-done((s32[37,8,128]{2,1,0:T(8,128)S(1)}, s32[37,8,128]{2,1,0:T(8,128)S(1)}, u32[]{:S(2)}, u32[]{:S(2)}) %collective-permute-start.9) | collective-permute-done | bytes 151584 | tf_op jit(solution)/shard_map/ppermute | solution.py:585
  76.4 0.9 %finish.1 = f32[3,8,8,512]{3,2,1,0:T(8,128)} custom-call(f32[24,8,512]{2,1,0:T(8,128)S(1)} %get-tuple-element.64.part, s32[49,8,128]{2,1,0:T(8,128)S(1)} %collective-permute-done.8.pushed, s32[37,8,128]{2,1,0:T(8,128)S(1)} %collective-permute-done.9.pushed_far), custom_call_target="tpu_custom_call" | custom-call | flops 2000000 | bytes 745472 | tf_op jit(solution)/shard_map/finish/pallas_call | solution.py:561
  (7 shorter events, 0.0 us)
Async XLA Ops:
  1.7 19.6 %collective-permute-start = (s32[81,8,128]{2,1,0:T(8,128)S(1)}, s32[81,8,128]{2,1,0:T(8,128)S(1)}, u32[]{:S(2)}, u32[]{:S(2)}) collective-permute-start(s32[81,8,128]{2,1,0:T(8,128)S(1)} %get-tuple-element.38), channel_id=1, source_target_pairs={{0,1},{1,2},{2,3},{3,4},{4,5},{5,6},{6,7},{7,8},{8,9},{9,10},{10,1... | collective-permute-start | bytes 995336 | tf_op jit(solution)/shard_map/ppermute | solution.py:585
  3.6 17.6 %collective-permute-start.1 = (s32[69,8,128]{2,1,0:T(8,128)S(1)}, s32[69,8,128]{2,1,0:T(8,128)S(1)}, u32[]{:S(2)}, u32[]{:S(2)}) collective-permute-start(s32[69,8,128]{2,1,0:T(8,128)S(1)} %get-tuple-element.39), channel_id=1, source_target_pairs={{0,2},{1,3},{2,4},{3,5},{4,6},{5,7},{6,8},{7,9},{8,10},{9,11},{10,... | collective-permute-start | bytes 847880 | tf_op jit(solution)/shard_map/ppermute | solution.py:585
  9.6 26.8 %all-to-all-start = ((f32[64,8,128]{2,1,0:T(8,128)}), f32[64,8,128]{2,1,0:T(8,128)S(1)}, u32[]{:S(2)}, u32[]{:S(2)}) async-start(f32[64,8,128]{2,1,0:T(8,128)} %bitcast.3), calls=%async_computation | async-start | bytes 524288 | tf_op jit(solution)/shard_map/all_to_all | solution.py:624
  22.3 7.9 %collective-permute-start.2 = (s32[37,8,128]{2,1,0:T(8,128)S(1)}, s32[37,8,128]{2,1,0:T(8,128)S(1)}, u32[]{:S(2)}, u32[]{:S(2)}) collective-permute-start(s32[37,8,128]{2,1,0:T(8,128)S(1)} %get-tuple-element.52), channel_id=1, source_target_pairs={{0,64},{1,65},{2,66},{3,67},{4,68},{5,69},{6,70},{7,71},{8,72},{9,... | collective-permute-start | bytes 454664 | tf_op jit(solution)/shard_map/ppermute | solution.py:585
  31.1 7.7 %collective-permute-start.4 = (s32[25,8,128]{2,1,0:T(8,128)S(1)}, s32[25,8,128]{2,1,0:T(8,128)S(1)}, u32[]{:S(2)}, u32[]{:S(2)}) collective-permute-start(s32[25,8,128]{2,1,0:T(8,128)S(1)} %get-tuple-element.55), channel_id=1, source_target_pairs={{64,129},{65,130},{66,131},{67,132},{68,133},{69,134},{70,135},{71... | collective-permute-start | bytes 307208 | tf_op jit(solution)/shard_map/ppermute | solution.py:585
  34.0 4.8 %collective-permute-start.3 = (s32[17,8,128]{2,1,0:T(8,128)S(1)}, s32[17,8,128]{2,1,0:T(8,128)S(1)}, u32[]{:S(2)}, u32[]{:S(2)}) collective-permute-start(s32[17,8,128]{2,1,0:T(8,128)S(1)} %get-tuple-element.54), channel_id=1, source_target_pairs={{64,128},{65,129},{66,130},{67,131},{68,132},{69,133},{70,134},{71... | collective-permute-start | bytes 208904 | tf_op jit(solution)/shard_map/ppermute | solution.py:585
  45.4 7.7 %collective-permute-start.5 = (s32[29,8,128]{2,1,0:T(8,128)S(1)}, s32[29,8,128]{2,1,0:T(8,128)S(1)}, u32[]{:S(2)}, u32[]{:S(2)}) collective-permute-start(s32[29,8,128]{2,1,0:T(8,128)S(1)} %get-tuple-element.60), channel_id=1, source_target_pairs={{192,128},{193,129},{194,130},{195,131},{196,132},{197,133},{198,1... | collective-permute-start | bytes 356360 | tf_op jit(solution)/shard_map/ppermute | solution.py:585
  53.0 10.8 %collective-permute-start.7 = (s32[25,8,128]{2,1,0:T(8,128)S(1)}, s32[25,8,128]{2,1,0:T(8,128)S(1)}, u32[]{:S(2)}, u32[]{:S(2)}) collective-permute-start(s32[25,8,128]{2,1,0:T(8,128)S(1)} %get-tuple-element.63), channel_id=1, source_target_pairs={{129,64},{130,65},{131,66},{132,67},{133,68},{134,69},{135,70},{13... | collective-permute-start | bytes 307208 | tf_op jit(solution)/shard_map/ppermute | solution.py:585
  54.3 9.5 %collective-permute-start.6 = (s32[17,8,128]{2,1,0:T(8,128)S(1)}, s32[17,8,128]{2,1,0:T(8,128)S(1)}, u32[]{:S(2)}, u32[]{:S(2)}) collective-permute-start(s32[17,8,128]{2,1,0:T(8,128)S(1)} %get-tuple-element.62), channel_id=1, source_target_pairs={{128,64},{129,65},{130,66},{131,67},{132,68},{133,69},{134,70},{13... | collective-permute-start | bytes 208904 | tf_op jit(solution)/shard_map/ppermute | solution.py:585
  65.4 11.0 %collective-permute-start.8 = (s32[49,8,128]{2,1,0:T(8,128)S(1)}, s32[49,8,128]{2,1,0:T(8,128)S(1)}, u32[]{:S(2)}, u32[]{:S(2)}) collective-permute-start(s32[49,8,128]{2,1,0:T(8,128)S(1)} %get-tuple-element.65), channel_id=1, source_target_pairs={{1,0},{2,1},{3,2},{4,3},{5,4},{6,5},{7,6},{8,7},{9,8},{10,9},{11,1... | collective-permute-start | bytes 602120 | tf_op jit(solution)/shard_map/ppermute | solution.py:585
  69.3 7.1 %collective-permute-start.9 = (s32[37,8,128]{2,1,0:T(8,128)S(1)}, s32[37,8,128]{2,1,0:T(8,128)S(1)}, u32[]{:S(2)}, u32[]{:S(2)}) collective-permute-start(s32[37,8,128]{2,1,0:T(8,128)S(1)} %get-tuple-element.66), channel_id=1, source_target_pairs={{2,0},{3,1},{4,2},{5,3},{6,4},{7,5},{8,6},{9,7},{10,8},{11,9},{12,... | collective-permute-start | bytes 454664 | tf_op jit(solution)/shard_map/ppermute | solution.py:585

commit v6 on v5

--- a/solution.py
+++ b/solution.py
@@ -124,14 +124,15 @@
 
 
 def adjoint_step(current, wind_x, wind_y, low):
-    result = {low - 1: wind_y(low) * current[low]}
-    for row in range(low, ROWS):
+    result = {}
+    carried = None
+    for row in reversed(range(low, ROWS)):
         here = current[row]
-        along = wind_x(row)
-        value = here * (1.0 - along - wind_y(row)) + pltpu.roll(along * here, WIDTH - 1, 1)
-        if row + 1 < ROWS:
-            value = value + wind_y(row + 1) * current[row + 1]
-        result[row] = value
+        along, across = wind_x(row) * here, wind_y(row) * here
+        value = (here - along) + (pltpu.roll(along, WIDTH - 1, 1) - across)
+        result[row] = value if carried is None else value + carried
+        carried = across
+    result[low - 1] = carried
     return result
 
 
@@ -249,19 +250,12 @@
     return top, middle, (rest - middle.astype(f32)).astype(bf16)
 
 
-def pack_kernel(innovation, cells, weight, owner, channel_weight, rinv, send, mixing):
+def pack_kernel(innovation, cells, weight, owner, channel_weight, rinv, send):
     sub_id = lax.broadcasted_iota(jnp.int32, (RECORDS, RECORDS), 0)
     lane_id = lax.broadcasted_iota(jnp.int32, (RECORDS, RECORDS), 1)
     not_later = lane_id <= sub_id
 
-    scaled = channel_weight[...] * (rinv[...] * rinv[...])
-    matrix = lax.dot_general(
-        scaled, channel_weight[...], (((1,), (1,)), ((), ())),
-        precision=highest, preferred_element_type=f32,
-    )
-    for level in range(LEVELS):
-        mixing[level] = jnp.broadcast_to(matrix[:, level : level + 1], (LEVELS, LANES))
-    scaled = jnp.concatenate(three(scaled), axis=0)
+    scaled = jnp.concatenate(three(channel_weight[...] * (rinv[...] * rinv[...])), axis=0)
 
     spread_row = lax.broadcasted_iota(jnp.int32, (2 * LEVELS, LANES), 0)
     spread_lane = lax.broadcasted_iota(jnp.int32, (2 * LEVELS, LANES), 1)
@@ -302,7 +296,13 @@
         send[pl.ds(spare, TILES, stride=8), :] = jnp.zeros((TILES, LANES), f32)
 
 
-def stencil_kernel(received, slots, stencil, pieces):
+def stencil_kernel(received, channel_weight, rinv, slots, stencil, mixing, pieces):
+    matrix = lax.dot_general(
+        channel_weight[...] * (rinv[...] * rinv[...]), channel_weight[...],
+        (((1,), (1,)), ((), ())), precision=highest, preferred_element_type=f32,
+    )
+    for level in range(LEVELS):
+        mixing[level] = jnp.broadcast_to(matrix[:, level : level + 1], (LEVELS, LANES))
     rows_id = lax.broadcasted_iota(jnp.int32, (HALF, LANES), 0)
 
     def one_sub(sub, _):
@@ -406,7 +406,7 @@
     listed = [current[row] for row in range(-REACH, ROWS)]
     for number, row in enumerate(listed):
         mine[number] = row
-    encode(listed, own)
+    encode(listed[REACH - DROP :], own)
 
 
 def time_is(condition):
@@ -428,14 +428,14 @@
     def _():
         across = lower_winds(winds, winds_below, lower_edge)
         first = time_is(lambda index: index == 0)
-        rows = decode(other, REACH + ROWS)
+        rows = dict(zip(range(-DROP, ROWS), decode(other, DROP + ROWS)))
         current = {
-            row: jnp.where(first, mine[row + REACH], rows[row + REACH])
+            row: jnp.where(first, mine[row + REACH], rows.get(row, 0.0))
             for row in range(-REACH, ROWS)
         }
         current, low = forward_steps(current, across, -REACH, 6)
         listed = [
-            current[row] + jnp.where(first, rows[row + REACH], mine[row + REACH])
+            current[row] + jnp.where(first, rows[row], mine[row + REACH])
             for row in range(-EXTRA, ROWS)
         ]
         encode(listed[EXTRA:], own)
@@ -452,11 +452,11 @@
     forced = lower_forces(forces, forces_below)
     half_way = lower_state(pair_own, pair_extended)
     current, low = forward_steps(half_way, across, -(ROWS + EXTRA), 6)
-    before = decode(before, REACH + ROWS)
+    before = decode(before, DROP + ROWS)
     third = time_is(lambda index: index == 2)
     odd = time_is(lambda index: (index & 1) == 1)
     current = {
-        row: jnp.where(third, half_way[row], value) + jnp.where(odd, before[row + REACH], 0.0)
+        row: jnp.where(third, half_way[row], value) + jnp.where(odd, before[row + DROP], 0.0)
         for row, value in current.items()
     }
     for sub in range(SUBS):
@@ -615,9 +615,9 @@
     )
     below = moved(below, STAY, 1)
     down_edge = moved(down_edge, STAY, 2)
-    send, mixing = run(
+    send = run(
         pack_kernel,
-        (struct(TILES * 8, LANES), struct(LEVELS, LEVELS, LANES)),
+        struct(TILES * 8, LANES),
         records,
         name="pack",
     )
@@ -628,7 +628,7 @@
     own, mine, winds_below, lower_edge, forces_below = run(
         forward_local_kernel,
         (
-            message(message_tiles(REACH + ROWS)),
+            message(message_tiles(DROP + ROWS)),
             struct(REACH + ROWS, LEVELS, WIDTH),
             struct(WINDS * ROWS, LEVELS, WIDTH),
             struct(WINDS * ROWS, LEVELS, WIDTH),
@@ -636,6 +636,7 @@
         ),
         (winds, forces, below, down_edge),
         name="forward_local",
+        flops=2_000_000_000,
     )
     before = moved(own, FORWARD_FIRST, 0)
     pair_shapes = (message(message_tiles(ROWS)), message(message_tiles(ROWS + EXTRA)))
@@ -646,13 +647,14 @@
         name="forward_pair",
     )
     pair = (moved(own, FORWARD_SECOND, 0), moved(extended, FORWARD_SECOND, 1))
-    slots, stencil = run(
+    slots, stencil, mixing = run(
         stencil_kernel,
         (
             struct(SUBS, LANES, LANES),
             struct(SUBS, CHUNKS, HALF, CORNERS * LANES, dtype=bf16),
-        ),
-        (received,),
+            struct(LEVELS, LEVELS, LANES),
+        ),
+        (received, *records[-2:]),
         scratch=(pltpu.VMEM((LANES, LANES), f32),),
         name="stencil",
     )

time: 77.7 us -> 77.2 us (level)
  transfers between devices with their start and end apart: 11 -> 11, of which waited for: 4 -> 4; matrix products, arithmetic and copies ran while one was open for 0% -> 0% of each run, Pallas kernels for 8% -> 9%
where the time goes in v6:
time: 77.2 us; the launch traced here: 76.8 us
  starting transfers between devices  35.9 us (47%)
  waiting for transfers between devices  23.4 us (30%)
  Pallas kernels  17.3 us (22%)
    ppermute x10, starting transfers between devices, moved(): return lax.ppermute(array, ('tm', 'space'), pairs)  24.3 us
    ppermute x10, waiting for transfers between devices, moved(): return lax.ppermute(array, ('tm', 'space'), pairs)  23.4 us
    pallas_call x9, Pallas kernels, run(): pl.pallas_call(kernel, out_shape=outputs, in_specs=[pl.BlockSpec(memory_s...  17.3 us
    all_to_all x1, starting transfers between devices, shards(): lax.all_to_all(send.reshape(TILES, 8, LANES), 'space', split_axis=0, conc...  11.6 us
  transfers between devices with their start and end apart: 11, of which 4 were waited for; matrix products, arithmetic and copies ran while one was open for 0% of the time, Pallas kernels for 9%

profile of v6, /device:TPU:4, one launch (start us, length us, event | category | flops | bytes accessed | tf_op | source)
XLA Modules:
  0.0 76.8 jit_solution(2142309675332638322)
XLA Ops:
  0.0 1.7 %rows.1 = (f32[16,8,512]{2,1,0:T(8,128)S(1)}, f32[24,8,512]{2,1,0:T(8,128)S(1)}, s32[81,8,128]{2,1,0:T(8,128)S(1)}, s32[69,8,128]{2,1,0:T(8,128)S(1)}, bf16[3,25...) custom-call(f32[3,8,8,512]{3,2,1,0:T(8,128)} %refs_0_.1, ...), custom_call_target="tpu_custom_call" | custom-call | flops 2000000 | bytes 1079296 | tf_op jit(solution)/shard_map/rows/pallas_call | solution.py:561
  1.7 1.9 %collective-permute-start = (s32[81,8,128]{2,1,0:T(8,128)S(1)}, s32[81,8,128]{2,1,0:T(8,128)S(1)}, u32[]{:S(2)}, u32[]{:S(2)}) collective-permute-start(s32[81,8,128]{2,1,0:T(8,128)S(1)} %get-tuple-element.37), channel_id=1, source_target_pairs={{0,1},{1,2},{2,3},{3,4},{4,5},{5,6},{6,7},{7,8},{8,9},{9,10},{10,1... | collective-permute-start | bytes 995336 | tf_op jit(solution)/shard_map/ppermute | solution.py:585
  3.6 3.8 %collective-permute-start.1 = (s32[69,8,128]{2,1,0:T(8,128)S(1)}, s32[69,8,128]{2,1,0:T(8,128)S(1)}, u32[]{:S(2)}, u32[]{:S(2)}) collective-permute-start(s32[69,8,128]{2,1,0:T(8,128)S(1)} %get-tuple-element.38), channel_id=1, source_target_pairs={{0,2},{1,3},{2,4},{3,5},{4,6},{5,7},{6,8},{7,9},{8,10},{9,11},{10,... | collective-permute-start | bytes 847880 | tf_op jit(solution)/shard_map/ppermute | solution.py:585
  7.5 2.2 %pack.1 = f32[512,128]{1,0:T(8,128)} custom-call(bf16[3,256,256]{2,1,0:T(8,128)(2,1)S(1)} %get-tuple-element.39.innovation, s32[3,4,256]{2,1,0:T(4,128)S(1)} %get-tuple-element.40.cells, bf16[3,4,256]{2,1,0:T(4,128)(2,1)S(1)} %get-tuple-element.41.weight, s32[3,1,256]{2,1,0:T(1,128)S(1)} %get-tuple-element.42.owner, ...), custom_call_target="tpu_custom_call" | custom-call | flops 2000000 | bytes 423936 | tf_op jit(solution)/shard_map/pack/pallas_call | solution.py:561
  9.7 11.6 %all-to-all-start = ((f32[64,8,128]{2,1,0:T(8,128)}), f32[64,8,128]{2,1,0:T(8,128)S(1)}, u32[]{:S(2)}, u32[]{:S(2)}) async-start(f32[64,8,128]{2,1,0:T(8,128)} %bitcast.3), calls=%async_computation | async-start | bytes 524288 | tf_op jit(solution)/shard_map/all_to_all | solution.py:624
  21.3 0.0 collective-permute-done.1.down_edge
  21.3 1.0 %forward_local.1 = (s32[29,8,128]{2,1,0:T(8,128)S(1)}, f32[18,8,512]{2,1,0:T(8,128)S(1)}, f32[16,8,512]{2,1,0:T(8,128)S(1)}, f32[16,8,512]{2,1,0:T(8,128)S(1)}, f32[24,8,512]{2,1,0:T(8,128)S(1)}) custom-call(f32[16,8,512]{2,1,0:T(8,128)S(1)} %get-tuple-element.35.winds, f32[24,8,512]{2,1,0:T(8,128)S(1)} %get-tuple-element.36.forces, ...), custom_call_target="tpu_custom_call" | custom-call | flops 2000000000 | bytes 1269760 | tf_op jit(solution)/shard_map/forward_local/pallas_call | solution.py:561
  22.3 3.5 %collective-permute-start.2 = (s32[29,8,128]{2,1,0:T(8,128)S(1)}, s32[29,8,128]{2,1,0:T(8,128)S(1)}, u32[]{:S(2)}, u32[]{:S(2)}) collective-permute-start(s32[29,8,128]{2,1,0:T(8,128)S(1)} %get-tuple-element.50), channel_id=1, source_target_pairs={{0,64},{1,65},{2,66},{3,67},{4,68},{5,69},{6,70},{7,71},{8,72},{9,... | collective-permute-start | bytes 356360 | tf_op jit(solution)/shard_map/ppermute | solution.py:585
  25.8 3.7 %collective-permute-done.2.other.before = s32[29,8,128]{2,1,0:T(8,128)S(1)} collective-permute-done((s32[29,8,128]{2,1,0:T(8,128)S(1)}, s32[29,8,128]{2,1,0:T(8,128)S(1)}, u32[]{:S(2)}, u32[]{:S(2)}) %collective-permute-start.2) | collective-permute-done | bytes 118816 | tf_op jit(solution)/shard_map/ppermute | solution.py:585
  29.5 0.9 %forward_pair.1 = (s32[17,8,128]{2,1,0:T(8,128)S(1)}, s32[25,8,128]{2,1,0:T(8,128)S(1)}) custom-call(f32[16,8,512]{2,1,0:T(8,128)S(1)} %get-tuple-element.35.winds, f32[16,8,512]{2,1,0:T(8,128)S(1)} %get-tuple-element.47.winds_below, f32[16,8,512]{2,1,0:T(8,128)S(1)} %get-tuple-element.48.lower_edge, f32[18,8,512]{2,1,0:T(8,128)S(1)} %get-tuple-element.51.mine, ...), custom_call_target="tpu_custom_call" | custom-call | flops 2000000 | bytes 1200128 | tf_op jit(solution)/shard_map/forward_pair/pallas_call | solution.py:561
  30.4 3.0 %collective-permute-start.4 = (s32[25,8,128]{2,1,0:T(8,128)S(1)}, s32[25,8,128]{2,1,0:T(8,128)S(1)}, u32[]{:S(2)}, u32[]{:S(2)}) collective-permute-start(s32[25,8,128]{2,1,0:T(8,128)S(1)} %get-tuple-element.53), channel_id=1, source_target_pairs={{64,129},{65,130},{66,131},{67,132},{68,133},{69,134},{70,135},{71... | collective-permute-start | bytes 307208 | tf_op jit(solution)/shard_map/ppermute | solution.py:585
  33.4 2.4 %collective-permute-start.3 = (s32[17,8,128]{2,1,0:T(8,128)S(1)}, s32[17,8,128]{2,1,0:T(8,128)S(1)}, u32[]{:S(2)}, u32[]{:S(2)}) collective-permute-start(s32[17,8,128]{2,1,0:T(8,128)S(1)} %get-tuple-element.52), channel_id=1, source_target_pairs={{64,128},{65,129},{66,130},{67,131},{68,132},{69,133},{70,134},{71... | collective-permute-start | bytes 208904 | tf_op jit(solution)/shard_map/ppermute | solution.py:585
  35.7 2.6 %stencil.1 = (f32[3,128,128]{2,1,0:T(8,128)S(1)}, bf16[3,8,256,512]{3,2,1,0:T(8,128)(2,1)S(1)}, f32[8,8,128]{2,1,0:T(8,128)S(1)}) custom-call(f32[512,128]{1,0:T(8,128)S(1)} %bitcast.5, f32[8,256]{1,0:T(8,128)S(1)} %get-tuple-element.43.channel_weight, f32[1,256]{1,0:T(1,128)S(1)} %get-tuple-element.44.rinv), custom_call_target="tpu_custom_call" | custom-call | flops 2000000 | bytes 271360 | tf_op jit(solution)/shard_map/stencil/pallas_call | solution.py:561
  38.3 6.4 %forward_final.1 = (f32[24,8,512]{2,1,0:T(8,128)S(1)}, f32[14,8,512]{2,1,0:T(8,128)S(1)}, s32[29,8,128]{2,1,0:T(8,128)S(1)}) custom-call(f32[16,8,512]{2,1,0:T(8,128)S(1)} %get-tuple-element.35.winds, f32[24,8,512]{2,1,0:T(8,128)S(1)} %get-tuple-element.36.forces, f32[16,8,512]{2,1,0:T(8,128)S(1)} %get-tuple-element.47.winds_below, ...), custom_call_target="tpu_custom_call" | custom-call | flops 2000000 | bytes 8384512 | tf_op jit(solution)/shard_map/forward_final/pallas_call | solution.py:561
  44.8 1.3 %collective-permute-start.5 = (s32[29,8,128]{2,1,0:T(8,128)S(1)}, s32[29,8,128]{2,1,0:T(8,128)S(1)}, u32[]{:S(2)}, u32[]{:S(2)}) collective-permute-start(s32[29,8,128]{2,1,0:T(8,128)S(1)} %get-tuple-element.58), channel_id=1, source_target_pairs={{192,128},{193,129},{194,130},{195,131},{196,132},{197,133},{198,1... | collective-permute-start | bytes 356360 | tf_op jit(solution)/shard_map/ppermute | solution.py:585
  46.1 6.5 %collective-permute-done.5.other.after = s32[29,8,128]{2,1,0:T(8,128)S(1)} collective-permute-done((s32[29,8,128]{2,1,0:T(8,128)S(1)}, s32[29,8,128]{2,1,0:T(8,128)S(1)}, u32[]{:S(2)}, u32[]{:S(2)}) %collective-permute-start.5) | collective-permute-done | bytes 118816 | tf_op jit(solution)/shard_map/ppermute | solution.py:585
  52.6 1.3 %collective-permute-start.7 = (s32[25,8,128]{2,1,0:T(8,128)S(1)}, s32[25,8,128]{2,1,0:T(8,128)S(1)}, u32[]{:S(2)}, u32[]{:S(2)}) collective-permute-start(s32[25,8,128]{2,1,0:T(8,128)S(1)} %get-tuple-element.61), channel_id=1, source_target_pairs={{129,64},{130,65},{131,66},{132,67},{133,68},{134,69},{135,70},{13... | collective-permute-start | bytes 307208 | tf_op jit(solution)/shard_map/ppermute | solution.py:585
  53.9 1.3 %collective-permute-start.6 = (s32[17,8,128]{2,1,0:T(8,128)S(1)}, s32[17,8,128]{2,1,0:T(8,128)S(1)}, u32[]{:S(2)}, u32[]{:S(2)}) collective-permute-start(s32[17,8,128]{2,1,0:T(8,128)S(1)} %get-tuple-element.60), channel_id=1, source_target_pairs={{128,64},{129,65},{130,66},{131,67},{132,68},{133,69},{134,70},{13... | collective-permute-start | bytes 208904 | tf_op jit(solution)/shard_map/ppermute | solution.py:585
  55.2 8.0 %collective-permute-done.6.pair_own = s32[17,8,128]{2,1,0:T(8,128)S(1)} collective-permute-done((s32[17,8,128]{2,1,0:T(8,128)S(1)}, s32[17,8,128]{2,1,0:T(8,128)S(1)}, u32[]{:S(2)}, u32[]{:S(2)}) %collective-permute-start.6) | collective-permute-done | bytes 69664 | tf_op jit(solution)/shard_map/ppermute | solution.py:585
  63.2 1.6 %adjoint_final.1 = (f32[24,8,512]{2,1,0:T(8,128)S(1)}, s32[49,8,128]{2,1,0:T(8,128)S(1)}, s32[37,8,128]{2,1,0:T(8,128)S(1)}) custom-call(f32[24,8,512]{2,1,0:T(8,128)S(1)} %get-tuple-element.57.sources, f32[16,8,512]{2,1,0:T(8,128)S(1)} %get-tuple-element.35.winds, f32[16,8,512]{2,1,0:T(8,128)S(1)} %get-tuple-element.47.winds_below, ...), custom_call_target="tpu_custom_call" | custom-call | flops 2000000 | bytes 1470464 | tf_op jit(solution)/shard_map/adjoint_final/pallas_call | solution.py:561
  64.8 3.9 %collective-permute-start.8 = (s32[49,8,128]{2,1,0:T(8,128)S(1)}, s32[49,8,128]{2,1,0:T(8,128)S(1)}, u32[]{:S(2)}, u32[]{:S(2)}) collective-permute-start(s32[49,8,128]{2,1,0:T(8,128)S(1)} %get-tuple-element.63), channel_id=1, source_target_pairs={{1,0},{2,1},{3,2},{4,3},{5,4},{6,5},{7,6},{8,7},{9,8},{10,9},{11,1... | collective-permute-start | bytes 602120 | tf_op jit(solution)/shard_map/ppermute | solution.py:585
  68.8 1.9 %collective-permute-start.9 = (s32[37,8,128]{2,1,0:T(8,128)S(1)}, s32[37,8,128]{2,1,0:T(8,128)S(1)}, u32[]{:S(2)}, u32[]{:S(2)}) collective-permute-start(s32[37,8,128]{2,1,0:T(8,128)S(1)} %get-tuple-element.64), channel_id=1, source_target_pairs={{2,0},{3,1},{4,2},{5,3},{6,4},{7,5},{8,6},{9,7},{10,8},{11,9},{12,... | collective-permute-start | bytes 454664 | tf_op jit(solution)/shard_map/ppermute | solution.py:585
  70.7 5.2 %collective-permute-done.9.pushed_far = s32[37,8,128]{2,1,0:T(8,128)S(1)} collective-permute-done((s32[37,8,128]{2,1,0:T(8,128)S(1)}, s32[37,8,128]{2,1,0:T(8,128)S(1)}, u32[]{:S(2)}, u32[]{:S(2)}) %collective-permute-start.9) | collective-permute-done | bytes 151584 | tf_op jit(solution)/shard_map/ppermute | solution.py:585
  75.9 0.9 %finish.1 = f32[3,8,8,512]{3,2,1,0:T(8,128)} custom-call(f32[24,8,512]{2,1,0:T(8,128)S(1)} %get-tuple-element.62.part, s32[49,8,128]{2,1,0:T(8,128)S(1)} %collective-permute-done.8.pushed, s32[37,8,128]{2,1,0:T(8,128)S(1)} %collective-permute-done.9.pushed_far), custom_call_target="tpu_custom_call" | custom-call | flops 2000000 | bytes 745472 | tf_op jit(solution)/shard_map/finish/pallas_call | solution.py:561
  (7 shorter events, 0.0 us)
Async XLA Ops:
  1.7 19.6 %collective-permute-start = (s32[81,8,128]{2,1,0:T(8,128)S(1)}, s32[81,8,128]{2,1,0:T(8,128)S(1)}, u32[]{:S(2)}, u32[]{:S(2)}) collective-permute-start(s32[81,8,128]{2,1,0:T(8,128)S(1)} %get-tuple-element.37), channel_id=1, source_target_pairs={{0,1},{1,2},{2,3},{3,4},{4,5},{5,6},{6,7},{7,8},{8,9},{9,10},{10,1... | collective-permute-start | bytes 995336 | tf_op jit(solution)/shard_map/ppermute | solution.py:585
  3.6 17.7 %collective-permute-start.1 = (s32[69,8,128]{2,1,0:T(8,128)S(1)}, s32[69,8,128]{2,1,0:T(8,128)S(1)}, u32[]{:S(2)}, u32[]{:S(2)}) collective-permute-start(s32[69,8,128]{2,1,0:T(8,128)S(1)} %get-tuple-element.38), channel_id=1, source_target_pairs={{0,2},{1,3},{2,4},{3,5},{4,6},{5,7},{6,8},{7,9},{8,10},{9,11},{10,... | collective-permute-start | bytes 847880 | tf_op jit(solution)/shard_map/ppermute | solution.py:585
  9.7 26.1 %all-to-all-start = ((f32[64,8,128]{2,1,0:T(8,128)}), f32[64,8,128]{2,1,0:T(8,128)S(1)}, u32[]{:S(2)}, u32[]{:S(2)}) async-start(f32[64,8,128]{2,1,0:T(8,128)} %bitcast.3), calls=%async_computation | async-start | bytes 524288 | tf_op jit(solution)/shard_map/all_to_all | solution.py:624
  22.3 7.2 %collective-permute-start.2 = (s32[29,8,128]{2,1,0:T(8,128)S(1)}, s32[29,8,128]{2,1,0:T(8,128)S(1)}, u32[]{:S(2)}, u32[]{:S(2)}) collective-permute-start(s32[29,8,128]{2,1,0:T(8,128)S(1)} %get-tuple-element.50), channel_id=1, source_target_pairs={{0,64},{1,65},{2,66},{3,67},{4,68},{5,69},{6,70},{7,71},{8,72},{9,... | collective-permute-start | bytes 356360 | tf_op jit(solution)/shard_map/ppermute | solution.py:585
  30.4 8.0 %collective-permute-start.4 = (s32[25,8,128]{2,1,0:T(8,128)S(1)}, s32[25,8,128]{2,1,0:T(8,128)S(1)}, u32[]{:S(2)}, u32[]{:S(2)}) collective-permute-start(s32[25,8,128]{2,1,0:T(8,128)S(1)} %get-tuple-element.53), channel_id=1, source_target_pairs={{64,129},{65,130},{66,131},{67,132},{68,133},{69,134},{70,135},{71... | collective-permute-start | bytes 307208 | tf_op jit(solution)/shard_map/ppermute | solution.py:585
  33.4 5.0 %collective-permute-start.3 = (s32[17,8,128]{2,1,0:T(8,128)S(1)}, s32[17,8,128]{2,1,0:T(8,128)S(1)}, u32[]{:S(2)}, u32[]{:S(2)}) collective-permute-start(s32[17,8,128]{2,1,0:T(8,128)S(1)} %get-tuple-element.52), channel_id=1, source_target_pairs={{64,128},{65,129},{66,130},{67,131},{68,132},{69,133},{70,134},{71... | collective-permute-start | bytes 208904 | tf_op jit(solution)/shard_map/ppermute | solution.py:585
  44.8 7.8 %collective-permute-start.5 = (s32[29,8,128]{2,1,0:T(8,128)S(1)}, s32[29,8,128]{2,1,0:T(8,128)S(1)}, u32[]{:S(2)}, u32[]{:S(2)}) collective-permute-start(s32[29,8,128]{2,1,0:T(8,128)S(1)} %get-tuple-element.58), channel_id=1, source_target_pairs={{192,128},{193,129},{194,130},{195,131},{196,132},{197,133},{198,1... | collective-permute-start | bytes 356360 | tf_op jit(solution)/shard_map/ppermute | solution.py:585
  52.6 10.6 %collective-permute-start.7 = (s32[25,8,128]{2,1,0:T(8,128)S(1)}, s32[25,8,128]{2,1,0:T(8,128)S(1)}, u32[]{:S(2)}, u32[]{:S(2)}) collective-permute-start(s32[25,8,128]{2,1,0:T(8,128)S(1)} %get-tuple-element.61), channel_id=1, source_target_pairs={{129,64},{130,65},{131,66},{132,67},{133,68},{134,69},{135,70},{13... | collective-permute-start | bytes 307208 | tf_op jit(solution)/shard_map/ppermute | solution.py:585
  53.9 9.3 %collective-permute-start.6 = (s32[17,8,128]{2,1,0:T(8,128)S(1)}, s32[17,8,128]{2,1,0:T(8,128)S(1)}, u32[]{:S(2)}, u32[]{:S(2)}) collective-permute-start(s32[17,8,128]{2,1,0:T(8,128)S(1)} %get-tuple-element.60), channel_id=1, source_target_pairs={{128,64},{129,65},{130,66},{131,67},{132,68},{133,69},{134,70},{13... | collective-permute-start | bytes 208904 | tf_op jit(solution)/shard_map/ppermute | solution.py:585
  64.8 11.0 %collective-permute-start.8 = (s32[49,8,128]{2,1,0:T(8,128)S(1)}, s32[49,8,128]{2,1,0:T(8,128)S(1)}, u32[]{:S(2)}, u32[]{:S(2)}) collective-permute-start(s32[49,8,128]{2,1,0:T(8,128)S(1)} %get-tuple-element.63), channel_id=1, source_target_pairs={{1,0},{2,1},{3,2},{4,3},{5,4},{6,5},{7,6},{8,7},{9,8},{10,9},{11,1... | collective-permute-start | bytes 602120 | tf_op jit(solution)/shard_map/ppermute | solution.py:585
  68.8 7.1 %collective-permute-start.9 = (s32[37,8,128]{2,1,0:T(8,128)S(1)}, s32[37,8,128]{2,1,0:T(8,128)S(1)}, u32[]{:S(2)}, u32[]{:S(2)}) collective-permute-start(s32[37,8,128]{2,1,0:T(8,128)S(1)} %get-tuple-element.64), channel_id=1, source_target_pairs={{2,0},{3,1},{4,2},{5,3},{6,4},{7,5},{8,6},{9,7},{10,8},{11,9},{12,... | collective-permute-start | bytes 454664 | tf_op jit(solution)/shard_map/ppermute | solution.py:585

commit v7 on v6

--- a/solution.py
+++ b/solution.py
@@ -124,15 +124,14 @@
 
 
 def adjoint_step(current, wind_x, wind_y, low):
-    result = {}
-    carried = None
-    for row in reversed(range(low, ROWS)):
+    result = {low - 1: wind_y(low) * current[low]}
+    for row in range(low, ROWS):
         here = current[row]
-        along, across = wind_x(row) * here, wind_y(row) * here
-        value = (here - along) + (pltpu.roll(along, WIDTH - 1, 1) - across)
-        result[row] = value if carried is None else value + carried
-        carried = across
-    result[low - 1] = carried
+        along = wind_x(row)
+        value = here * (1.0 - along - wind_y(row)) + pltpu.roll(along * here, WIDTH - 1, 1)
+        if row + 1 < ROWS:
+            value = value + wind_y(row + 1) * current[row + 1]
+        result[row] = value
     return result
 
 
@@ -484,7 +483,7 @@
     }
 
 
-def adjoint_pair_kernel(winds, winds_below, lower_edge, mine, other, own, extended):
+def adjoint_pair_kernel(winds, winds_below, lower_edge, mine, other, own, near, far):
     @pl.when(lax.axis_index("tm") >= 2)
     def _():
         across = lower_winds(winds, winds_below, lower_edge)
@@ -497,33 +496,32 @@
         for row in range(-DROP, ROWS):
             current[row] = current[row] + jnp.where(last, rows[row + DROP], mine[row + DROP])
         encode([current[row] for row in range(ROWS)], own)
-        encode([current[row] for row in range(low, 0)], extended)
+        encode([current[row] for row in range(-ROWS, 0)], near)
+        encode([current[row] for row in range(low, -ROWS)], far)
 
 
 PUSHED = [(sub, row) for sub in range(SUBS) for row in range(ROWS)]
-PUSHED_FAR = [(sub, row) for sub in range(SUBS) for row in range(2 * sub, ROWS)]
+PUSHED_FAR = [(sub, row) for sub in range(SUBS) for row in range(EXTRA + 2 * sub, ROWS)]
 
 
 def adjoint_final_kernel(
-    sources, winds, winds_below, lower_edge, after, pair_own, pair_extended,
+    sources, winds, winds_below, lower_edge, after, pair_own, pair_near, pair_far,
     gradient, pushed, pushed_far,
 ):
     across = lower_winds(winds, winds_below, lower_edge)
     own = decode(pair_own, ROWS)
-    above = decode(pair_extended, ROWS + EXTRA)
-    low = -EXTRA
-    half_way = {
-        row: above[row + EXTRA] + own[row] if row >= 0 else above[row + EXTRA]
-        for row in range(low, ROWS)
-    }
-    current, low = adjoint_steps(half_way, across, low, 6)
+    near = decode(pair_near, ROWS)
+    far = decode(pair_far, EXTRA)
+    half_way = {row: own[row] + near[row] for row in range(ROWS)}
+    for number, value in enumerate(far):
+        half_way[ROWS - EXTRA + number] = half_way[ROWS - EXTRA + number] + value
+    current, low = adjoint_steps(half_way, across, 0, 6)
     after = decode(after, DROP + ROWS)
     second = time_is(lambda index: index == 1)
     even = time_is(lambda index: (index & 1) == 0)
     for row in current:
         current[row] = jnp.where(second, half_way.get(row, 0.0), current[row])
-        if row >= -DROP:
-            current[row] = current[row] + jnp.where(even, after[row + DROP], 0.0)
+        current[row] = current[row] + jnp.where(even, after[row + DROP], 0.0)
     results = [None] * SUBS
     for sub in reversed(range(SUBS)):
         current = add_sources(current, sources, sub)
@@ -678,13 +676,17 @@
     )
 
     after = moved(response, ADJOINT_FIRST, 0)
-    own, extended = run(
+    own, near, far = run(
         adjoint_pair_kernel,
-        pair_shapes,
+        tuple(message(message_tiles(count)) for count in (ROWS, ROWS, EXTRA)),
         (winds, winds_below, lower_edge, mine, after),
         name="adjoint_pair",
     )
-    pair = (moved(own, ADJOINT_SECOND, 0), moved(extended, ADJOINT_SECOND, -1))
+    pair = (
+        moved(own, ADJOINT_SECOND, 0),
+        moved(near, ADJOINT_SECOND, -1),
+        moved(far, ADJOINT_SECOND, -2),
+    )
     part, pushed, pushed_far = run(
         adjoint_final_kernel,
         (

time: 77.2 us -> 77.2 us (level)
  starting transfers between devices: 35.9 us -> 39.9 us
  waiting for transfers between devices: 23.4 us -> 19.7 us
    ppermute x10 -> x11, starting transfers between devices: 24.3 us -> 28.3 us  [moved(): return lax.ppermute(array, ('tm', 'space'), pairs)]
    ppermute x10 -> x11, waiting for transfers between devices: 23.4 us -> 19.7 us  [moved(): return lax.ppermute(array, ('tm', 'space'), pairs)]
  transfers between devices with their start and end apart: 11 -> 12, of which waited for: 4 -> 4; matrix products, arithmetic and copies ran while one was open for 0% -> 0% of each run, Pallas kernels for 9% -> 9%
where the time goes in v7:
time: 77.2 us; the launch traced here: 76.8 us
  starting transfers between devices  39.9 us (52%)
  waiting for transfers between devices  19.7 us (26%)
  Pallas kernels  17 us (22%)
    ppermute x11, starting transfers between devices, moved(): return lax.ppermute(array, ('tm', 'space'), pairs)  28.3 us
    ppermute x11, waiting for transfers between devices, moved(): return lax.ppermute(array, ('tm', 'space'), pairs)  19.7 us
    pallas_call x9, Pallas kernels, run(): pl.pallas_call(kernel, out_shape=outputs, in_specs=[pl.BlockSpec(memory_s...  17 us
    all_to_all x1, starting transfers between devices, shards(): lax.all_to_all(send.reshape(TILES, 8, LANES), 'space', split_axis=0, conc...  11.6 us
  transfers between devices with their start and end apart: 12, of which 4 were waited for; matrix products, arithmetic and copies ran while one was open for 0% of the time, Pallas kernels for 9%

profile of v7, /device:TPU:4, one launch (start us, length us, event | category | flops | bytes accessed | tf_op | source)
XLA Modules:
  0.0 76.8 jit_solution(10294683197666533556)
XLA Ops:
  0.0 1.7 %rows.1 = (f32[16,8,512]{2,1,0:T(8,128)S(1)}, f32[24,8,512]{2,1,0:T(8,128)S(1)}, s32[81,8,128]{2,1,0:T(8,128)S(1)}, s32[69,8,128]{2,1,0:T(8,128)S(1)}, bf16[3,25...) custom-call(f32[3,8,8,512]{3,2,1,0:T(8,128)} %refs_0_.1, ...), custom_call_target="tpu_custom_call" | custom-call | flops 2000000 | bytes 1079296 | tf_op jit(solution)/shard_map/rows/pallas_call | solution.py:559
  1.7 1.9 %collective-permute-start = (s32[81,8,128]{2,1,0:T(8,128)S(1)}, s32[81,8,128]{2,1,0:T(8,128)S(1)}, u32[]{:S(2)}, u32[]{:S(2)}) collective-permute-start(s32[81,8,128]{2,1,0:T(8,128)S(1)} %get-tuple-element.38), channel_id=1, source_target_pairs={{0,1},{1,2},{2,3},{3,4},{4,5},{5,6},{6,7},{7,8},{8,9},{9,10},{10,1... | collective-permute-start | bytes 995336 | tf_op jit(solution)/shard_map/ppermute | solution.py:583
  3.6 3.8 %collective-permute-start.1 = (s32[69,8,128]{2,1,0:T(8,128)S(1)}, s32[69,8,128]{2,1,0:T(8,128)S(1)}, u32[]{:S(2)}, u32[]{:S(2)}) collective-permute-start(s32[69,8,128]{2,1,0:T(8,128)S(1)} %get-tuple-element.39), channel_id=1, source_target_pairs={{0,2},{1,3},{2,4},{3,5},{4,6},{5,7},{6,8},{7,9},{8,10},{9,11},{10,... | collective-permute-start | bytes 847880 | tf_op jit(solution)/shard_map/ppermute | solution.py:583
  7.5 2.2 %pack.1 = f32[512,128]{1,0:T(8,128)} custom-call(bf16[3,256,256]{2,1,0:T(8,128)(2,1)S(1)} %get-tuple-element.40.innovation, s32[3,4,256]{2,1,0:T(4,128)S(1)} %get-tuple-element.41.cells, bf16[3,4,256]{2,1,0:T(4,128)(2,1)S(1)} %get-tuple-element.42.weight, s32[3,1,256]{2,1,0:T(1,128)S(1)} %get-tuple-element.43.owner, ...), custom_call_target="tpu_custom_call" | custom-call | flops 2000000 | bytes 423936 | tf_op jit(solution)/shard_map/pack/pallas_call | solution.py:559
  9.7 11.6 %all-to-all-start = ((f32[64,8,128]{2,1,0:T(8,128)}), f32[64,8,128]{2,1,0:T(8,128)S(1)}, u32[]{:S(2)}, u32[]{:S(2)}) async-start(f32[64,8,128]{2,1,0:T(8,128)} %bitcast.3), calls=%async_computation | async-start | bytes 524288 | tf_op jit(solution)/shard_map/all_to_all | solution.py:622
  21.3 1.0 %forward_local.1 = (s32[29,8,128]{2,1,0:T(8,128)S(1)}, f32[18,8,512]{2,1,0:T(8,128)S(1)}, f32[16,8,512]{2,1,0:T(8,128)S(1)}, f32[16,8,512]{2,1,0:T(8,128)S(1)}, f32[24,8,512]{2,1,0:T(8,128)S(1)}) custom-call(f32[16,8,512]{2,1,0:T(8,128)S(1)} %get-tuple-element.36.winds, f32[24,8,512]{2,1,0:T(8,128)S(1)} %get-tuple-element.37.forces, ...), custom_call_target="tpu_custom_call" | custom-call | flops 2000000000 | bytes 1269760 | tf_op jit(solution)/shard_map/forward_local/pallas_call | solution.py:559
  22.3 3.5 %collective-permute-start.2 = (s32[29,8,128]{2,1,0:T(8,128)S(1)}, s32[29,8,128]{2,1,0:T(8,128)S(1)}, u32[]{:S(2)}, u32[]{:S(2)}) collective-permute-start(s32[29,8,128]{2,1,0:T(8,128)S(1)} %get-tuple-element.51), channel_id=1, source_target_pairs={{0,64},{1,65},{2,66},{3,67},{4,68},{5,69},{6,70},{7,71},{8,72},{9,... | collective-permute-start | bytes 356360 | tf_op jit(solution)/shard_map/ppermute | solution.py:583
  25.8 3.7 %collective-permute-done.2.other.before = s32[29,8,128]{2,1,0:T(8,128)S(1)} collective-permute-done((s32[29,8,128]{2,1,0:T(8,128)S(1)}, s32[29,8,128]{2,1,0:T(8,128)S(1)}, u32[]{:S(2)}, u32[]{:S(2)}) %collective-permute-start.2) | collective-permute-done | bytes 118816 | tf_op jit(solution)/shard_map/ppermute | solution.py:583
  29.5 0.9 %forward_pair.1 = (s32[17,8,128]{2,1,0:T(8,128)S(1)}, s32[25,8,128]{2,1,0:T(8,128)S(1)}) custom-call(f32[16,8,512]{2,1,0:T(8,128)S(1)} %get-tuple-element.36.winds, f32[16,8,512]{2,1,0:T(8,128)S(1)} %get-tuple-element.48.winds_below, f32[16,8,512]{2,1,0:T(8,128)S(1)} %get-tuple-element.49.lower_edge, f32[18,8,512]{2,1,0:T(8,128)S(1)} %get-tuple-element.52.mine, ...), custom_call_target="tpu_custom_call" | custom-call | flops 2000000 | bytes 1200128 | tf_op jit(solution)/shard_map/forward_pair/pallas_call | solution.py:559
  30.4 3.0 %collective-permute-start.4 = (s32[25,8,128]{2,1,0:T(8,128)S(1)}, s32[25,8,128]{2,1,0:T(8,128)S(1)}, u32[]{:S(2)}, u32[]{:S(2)}) collective-permute-start(s32[25,8,128]{2,1,0:T(8,128)S(1)} %get-tuple-element.54), channel_id=1, source_target_pairs={{64,129},{65,130},{66,131},{67,132},{68,133},{69,134},{70,135},{71... | collective-permute-start | bytes 307208 | tf_op jit(solution)/shard_map/ppermute | solution.py:583
  33.4 2.4 %collective-permute-start.3 = (s32[17,8,128]{2,1,0:T(8,128)S(1)}, s32[17,8,128]{2,1,0:T(8,128)S(1)}, u32[]{:S(2)}, u32[]{:S(2)}) collective-permute-start(s32[17,8,128]{2,1,0:T(8,128)S(1)} %get-tuple-element.53), channel_id=1, source_target_pairs={{64,128},{65,129},{66,130},{67,131},{68,132},{69,133},{70,134},{71... | collective-permute-start | bytes 208904 | tf_op jit(solution)/shard_map/ppermute | solution.py:583
  35.7 2.6 %stencil.1 = (f32[3,128,128]{2,1,0:T(8,128)S(1)}, bf16[3,8,256,512]{3,2,1,0:T(8,128)(2,1)S(1)}, f32[8,8,128]{2,1,0:T(8,128)S(1)}) custom-call(f32[512,128]{1,0:T(8,128)S(1)} %bitcast.5, f32[8,256]{1,0:T(8,128)S(1)} %get-tuple-element.44.channel_weight, f32[1,256]{1,0:T(1,128)S(1)} %get-tuple-element.45.rinv), custom_call_target="tpu_custom_call" | custom-call | flops 2000000 | bytes 271360 | tf_op jit(solution)/shard_map/stencil/pallas_call | solution.py:559
  38.3 6.4 %forward_final.1 = (f32[24,8,512]{2,1,0:T(8,128)S(1)}, f32[14,8,512]{2,1,0:T(8,128)S(1)}, s32[29,8,128]{2,1,0:T(8,128)S(1)}) custom-call(f32[16,8,512]{2,1,0:T(8,128)S(1)} %get-tuple-element.36.winds, f32[24,8,512]{2,1,0:T(8,128)S(1)} %get-tuple-element.37.forces, f32[16,8,512]{2,1,0:T(8,128)S(1)} %get-tuple-element.48.winds_below, ...), custom_call_target="tpu_custom_call" | custom-call | flops 2000000 | bytes 8384512 | tf_op jit(solution)/shard_map/forward_final/pallas_call | solution.py:559
  44.7 1.3 %collective-permute-start.5 = (s32[29,8,128]{2,1,0:T(8,128)S(1)}, s32[29,8,128]{2,1,0:T(8,128)S(1)}, u32[]{:S(2)}, u32[]{:S(2)}) collective-permute-start(s32[29,8,128]{2,1,0:T(8,128)S(1)} %get-tuple-element.59), channel_id=1, source_target_pairs={{192,128},{193,129},{194,130},{195,131},{196,132},{197,133},{198,1... | collective-permute-start | bytes 356360 | tf_op jit(solution)/shard_map/ppermute | solution.py:583
  46.0 6.5 %collective-permute-done.5.other.after = s32[29,8,128]{2,1,0:T(8,128)S(1)} collective-permute-done((s32[29,8,128]{2,1,0:T(8,128)S(1)}, s32[29,8,128]{2,1,0:T(8,128)S(1)}, u32[]{:S(2)}, u32[]{:S(2)}) %collective-permute-start.5) | collective-permute-done | bytes 118816 | tf_op jit(solution)/shard_map/ppermute | solution.py:583
  52.6 1.3 %collective-permute-start.6 = (s32[17,8,128]{2,1,0:T(8,128)S(1)}, s32[17,8,128]{2,1,0:T(8,128)S(1)}, u32[]{:S(2)}, u32[]{:S(2)}) collective-permute-start(s32[17,8,128]{2,1,0:T(8,128)S(1)} %get-tuple-element.61), channel_id=1, source_target_pairs={{128,64},{129,65},{130,66},{131,67},{132,68},{133,69},{134,70},{13... | collective-permute-start | bytes 208904 | tf_op jit(solution)/shard_map/ppermute | solution.py:583
  53.8 1.3 %collective-permute-start.7 = (s32[17,8,128]{2,1,0:T(8,128)S(1)}, s32[17,8,128]{2,1,0:T(8,128)S(1)}, u32[]{:S(2)}, u32[]{:S(2)}) collective-permute-start(s32[17,8,128]{2,1,0:T(8,128)S(1)} %get-tuple-element.62), channel_id=1, source_target_pairs={{129,64},{130,65},{131,66},{132,67},{133,68},{134,69},{135,70},{13... | collective-permute-start | bytes 208904 | tf_op jit(solution)/shard_map/ppermute | solution.py:583
  55.1 1.3 %collective-permute-start.8 = (s32[9,8,128]{2,1,0:T(8,128)S(1)}, s32[9,8,128]{2,1,0:T(8,128)S(1)}, u32[]{:S(2)}, u32[]{:S(2)}) collective-permute-start(s32[9,8,128]{2,1,0:T(8,128)S(1)} %get-tuple-element.63), channel_id=1, source_target_pairs={{130,64},{131,65},{132,66},{133,67},{134,68},{135,69},{136,70},{13... | collective-permute-start | bytes 110600 | tf_op jit(solution)/shard_map/ppermute | solution.py:583
  56.4 6.8 %collective-permute-done.8.pair_far = s32[9,8,128]{2,1,0:T(8,128)S(1)} collective-permute-done((s32[9,8,128]{2,1,0:T(8,128)S(1)}, s32[9,8,128]{2,1,0:T(8,128)S(1)}, u32[]{:S(2)}, u32[]{:S(2)}) %collective-permute-start.8) | collective-permute-done | bytes 36896 | tf_op jit(solution)/shard_map/ppermute | solution.py:583
  63.3 1.4 %adjoint_final.1 = (f32[24,8,512]{2,1,0:T(8,128)S(1)}, s32[49,8,128]{2,1,0:T(8,128)S(1)}, s32[13,8,128]{2,1,0:T(8,128)S(1)}) custom-call(f32[24,8,512]{2,1,0:T(8,128)S(1)} %get-tuple-element.58.sources, f32[16,8,512]{2,1,0:T(8,128)S(1)} %get-tuple-element.36.winds, f32[16,8,512]{2,1,0:T(8,128)S(1)} %get-tuple-element.48.winds_below, ...), custom_call_target="tpu_custom_call" | custom-call | flops 2000000 | bytes 1474560 | tf_op jit(solution)/shard_map/adjoint_final/pallas_call | solution.py:559
  64.7 5.2 %collective-permute-start.9 = (s32[49,8,128]{2,1,0:T(8,128)S(1)}, s32[49,8,128]{2,1,0:T(8,128)S(1)}, u32[]{:S(2)}, u32[]{:S(2)}) collective-permute-start(s32[49,8,128]{2,1,0:T(8,128)S(1)} %get-tuple-element.65), channel_id=1, source_target_pairs={{1,0},{2,1},{3,2},{4,3},{5,4},{6,5},{7,6},{8,7},{9,8},{10,9},{11,1... | collective-permute-start | bytes 602120 | tf_op jit(solution)/shard_map/ppermute | solution.py:583
  69.9 3.3 %collective-permute-start.10 = (s32[13,8,128]{2,1,0:T(8,128)S(1)}, s32[13,8,128]{2,1,0:T(8,128)S(1)}, u32[]{:S(2)}, u32[]{:S(2)}) collective-permute-start(s32[13,8,128]{2,1,0:T(8,128)S(1)} %get-tuple-element.66), channel_id=1, source_target_pairs={{2,0},{3,1},{4,2},{5,3},{6,4},{7,5},{8,6},{9,7},{10,8},{11,9},{12,... | collective-permute-start | bytes 159752 | tf_op jit(solution)/shard_map/ppermute | solution.py:583
  73.2 2.7 %collective-permute-done.10.pushed_far = s32[13,8,128]{2,1,0:T(8,128)S(1)} collective-permute-done((s32[13,8,128]{2,1,0:T(8,128)S(1)}, s32[13,8,128]{2,1,0:T(8,128)S(1)}, u32[]{:S(2)}, u32[]{:S(2)}) %collective-permute-start.10) | collective-permute-done | bytes 53280 | tf_op jit(solution)/shard_map/ppermute | solution.py:583
  75.9 0.9 %finish.1 = f32[3,8,8,512]{3,2,1,0:T(8,128)} custom-call(f32[24,8,512]{2,1,0:T(8,128)S(1)} %get-tuple-element.64.part, s32[49,8,128]{2,1,0:T(8,128)S(1)} %collective-permute-done.9.pushed, s32[13,8,128]{2,1,0:T(8,128)S(1)} %collective-permute-done.10.pushed_far), custom_call_target="tpu_custom_call" | custom-call | flops 2000000 | bytes 647168 | tf_op jit(solution)/shard_map/finish/pallas_call | solution.py:559
  (9 shorter events, 0.0 us)
Async XLA Ops:
  1.7 19.6 %collective-permute-start = (s32[81,8,128]{2,1,0:T(8,128)S(1)}, s32[81,8,128]{2,1,0:T(8,128)S(1)}, u32[]{:S(2)}, u32[]{:S(2)}) collective-permute-start(s32[81,8,128]{2,1,0:T(8,128)S(1)} %get-tuple-element.38), channel_id=1, source_target_pairs={{0,1},{1,2},{2,3},{3,4},{4,5},{5,6},{6,7},{7,8},{8,9},{9,10},{10,1... | collective-permute-start | bytes 995336 | tf_op jit(solution)/shard_map/ppermute | solution.py:583
  3.6 17.7 %collective-permute-start.1 = (s32[69,8,128]{2,1,0:T(8,128)S(1)}, s32[69,8,128]{2,1,0:T(8,128)S(1)}, u32[]{:S(2)}, u32[]{:S(2)}) collective-permute-start(s32[69,8,128]{2,1,0:T(8,128)S(1)} %get-tuple-element.39), channel_id=1, source_target_pairs={{0,2},{1,3},{2,4},{3,5},{4,6},{5,7},{6,8},{7,9},{8,10},{9,11},{10,... | collective-permute-start | bytes 847880 | tf_op jit(solution)/shard_map/ppermute | solution.py:583
  9.7 26.1 %all-to-all-start = ((f32[64,8,128]{2,1,0:T(8,128)}), f32[64,8,128]{2,1,0:T(8,128)S(1)}, u32[]{:S(2)}, u32[]{:S(2)}) async-start(f32[64,8,128]{2,1,0:T(8,128)} %bitcast.3), calls=%async_computation | async-start | bytes 524288 | tf_op jit(solution)/shard_map/all_to_all | solution.py:622
  22.3 7.2 %collective-permute-start.2 = (s32[29,8,128]{2,1,0:T(8,128)S(1)}, s32[29,8,128]{2,1,0:T(8,128)S(1)}, u32[]{:S(2)}, u32[]{:S(2)}) collective-permute-start(s32[29,8,128]{2,1,0:T(8,128)S(1)} %get-tuple-element.51), channel_id=1, source_target_pairs={{0,64},{1,65},{2,66},{3,67},{4,68},{5,69},{6,70},{7,71},{8,72},{9,... | collective-permute-start | bytes 356360 | tf_op jit(solution)/shard_map/ppermute | solution.py:583
  30.4 8.0 %collective-permute-start.4 = (s32[25,8,128]{2,1,0:T(8,128)S(1)}, s32[25,8,128]{2,1,0:T(8,128)S(1)}, u32[]{:S(2)}, u32[]{:S(2)}) collective-permute-start(s32[25,8,128]{2,1,0:T(8,128)S(1)} %get-tuple-element.54), channel_id=1, source_target_pairs={{64,129},{65,130},{66,131},{67,132},{68,133},{69,134},{70,135},{71... | collective-permute-start | bytes 307208 | tf_op jit(solution)/shard_map/ppermute | solution.py:583
  33.4 5.0 %collective-permute-start.3 = (s32[17,8,128]{2,1,0:T(8,128)S(1)}, s32[17,8,128]{2,1,0:T(8,128)S(1)}, u32[]{:S(2)}, u32[]{:S(2)}) collective-permute-start(s32[17,8,128]{2,1,0:T(8,128)S(1)} %get-tuple-element.53), channel_id=1, source_target_pairs={{64,128},{65,129},{66,130},{67,131},{68,132},{69,133},{70,134},{71... | collective-permute-start | bytes 208904 | tf_op jit(solution)/shard_map/ppermute | solution.py:583
  44.7 7.8 %collective-permute-start.5 = (s32[29,8,128]{2,1,0:T(8,128)S(1)}, s32[29,8,128]{2,1,0:T(8,128)S(1)}, u32[]{:S(2)}, u32[]{:S(2)}) collective-permute-start(s32[29,8,128]{2,1,0:T(8,128)S(1)} %get-tuple-element.59), channel_id=1, source_target_pairs={{192,128},{193,129},{194,130},{195,131},{196,132},{197,133},{198,1... | collective-permute-start | bytes 356360 | tf_op jit(solution)/shard_map/ppermute | solution.py:583
  52.6 10.7 %collective-permute-start.6 = (s32[17,8,128]{2,1,0:T(8,128)S(1)}, s32[17,8,128]{2,1,0:T(8,128)S(1)}, u32[]{:S(2)}, u32[]{:S(2)}) collective-permute-start(s32[17,8,128]{2,1,0:T(8,128)S(1)} %get-tuple-element.61), channel_id=1, source_target_pairs={{128,64},{129,65},{130,66},{131,67},{132,68},{133,69},{134,70},{13... | collective-permute-start | bytes 208904 | tf_op jit(solution)/shard_map/ppermute | solution.py:583
  53.8 9.4 %collective-permute-start.7 = (s32[17,8,128]{2,1,0:T(8,128)S(1)}, s32[17,8,128]{2,1,0:T(8,128)S(1)}, u32[]{:S(2)}, u32[]{:S(2)}) collective-permute-start(s32[17,8,128]{2,1,0:T(8,128)S(1)} %get-tuple-element.62), channel_id=1, source_target_pairs={{129,64},{130,65},{131,66},{132,67},{133,68},{134,69},{135,70},{13... | collective-permute-start | bytes 208904 | tf_op jit(solution)/shard_map/ppermute | solution.py:583
  55.1 8.1 %collective-permute-start.8 = (s32[9,8,128]{2,1,0:T(8,128)S(1)}, s32[9,8,128]{2,1,0:T(8,128)S(1)}, u32[]{:S(2)}, u32[]{:S(2)}) collective-permute-start(s32[9,8,128]{2,1,0:T(8,128)S(1)} %get-tuple-element.63), channel_id=1, source_target_pairs={{130,64},{131,65},{132,66},{133,67},{134,68},{135,69},{136,70},{13... | collective-permute-start | bytes 110600 | tf_op jit(solution)/shard_map/ppermute | solution.py:583
  64.7 11.2 %collective-permute-start.9 = (s32[49,8,128]{2,1,0:T(8,128)S(1)}, s32[49,8,128]{2,1,0:T(8,128)S(1)}, u32[]{:S(2)}, u32[]{:S(2)}) collective-permute-start(s32[49,8,128]{2,1,0:T(8,128)S(1)} %get-tuple-element.65), channel_id=1, source_target_pairs={{1,0},{2,1},{3,2},{4,3},{5,4},{6,5},{7,6},{8,7},{9,8},{10,9},{11,1... | collective-permute-start | bytes 602120 | tf_op jit(solution)/shard_map/ppermute | solution.py:583
  69.9 6.0 %collective-permute-start.10 = (s32[13,8,128]{2,1,0:T(8,128)S(1)}, s32[13,8,128]{2,1,0:T(8,128)S(1)}, u32[]{:S(2)}, u32[]{:S(2)}) collective-permute-start(s32[13,8,128]{2,1,0:T(8,128)S(1)} %get-tuple-element.66), channel_id=1, source_target_pairs={{2,0},{3,1},{4,2},{5,3},{6,4},{7,5},{8,6},{9,7},{10,8},{11,9},{12,... | collective-permute-start | bytes 159752 | tf_op jit(solution)/shard_map/ppermute | solution.py:583

commit v8 on v7

--- a/solution.py
+++ b/solution.py
@@ -422,41 +422,64 @@
     }
 
 
-def forward_pair_kernel(winds, winds_below, lower_edge, mine, other, own, extended):
-    @pl.when(lax.axis_index("tm") < 2)
+def forward_ahead_kernel(winds, winds_below, lower_edge, mine, ahead):
+    @pl.when(lax.axis_index("tm") == 0)
     def _():
         across = lower_winds(winds, winds_below, lower_edge)
-        first = time_is(lambda index: index == 0)
-        rows = dict(zip(range(-DROP, ROWS), decode(other, DROP + ROWS)))
-        current = {
-            row: jnp.where(first, mine[row + REACH], rows.get(row, 0.0))
-            for row in range(-REACH, ROWS)
-        }
+        current = {row: mine[row + REACH] for row in range(-REACH, ROWS)}
         current, low = forward_steps(current, across, -REACH, 6)
-        listed = [
-            current[row] + jnp.where(first, rows[row], mine[row + REACH])
-            for row in range(-EXTRA, ROWS)
-        ]
+        for row in range(low, ROWS):
+            ahead[row - low] = current[row]
+
+
+def forward_pair_kernel(winds, winds_below, lower_edge, mine, ahead, other, own, extended):
+    def finish(listed):
         encode(listed[EXTRA:], own)
         encode(listed, extended)
+
+    @pl.when(lax.axis_index("tm") == 0)
+    def _():
+        rows = dict(zip(range(-DROP, ROWS), decode(other, DROP + ROWS)))
+        finish([ahead[row + EXTRA] + rows[row] for row in range(-EXTRA, ROWS)])
+
+    @pl.when(lax.axis_index("tm") == 1)
+    def _():
+        across = lower_winds(winds, winds_below, lower_edge)
+        current = dict(zip(range(-DROP, ROWS), decode(other, DROP + ROWS)))
+        current, low = forward_steps(current, across, -DROP, 6)
+        listed = [mine[row + REACH] for row in range(-EXTRA, ROWS)]
+        finish([
+            value if row < low else value + current[row]
+            for row, value in zip(range(-EXTRA, ROWS), listed)
+        ])
 
 
 def forward_final_kernel(
     winds, forces, winds_below, lower_edge, forces_below,
     before, pair_own, pair_extended, slots, stencil, mixing,
     sources, mine, response,
-    found, spread,
+    found, spread, reached,
 ):
     across = lower_winds(winds, winds_below, lower_edge)
     forced = lower_forces(forces, forces_below)
-    half_way = lower_state(pair_own, pair_extended)
-    current, low = forward_steps(half_way, across, -(ROWS + EXTRA), 6)
+    low = -DROP
+
+    def keep(rows):
+        for row in range(low, ROWS):
+            reached[row - low] = rows[row]
+
+    third = lax.axis_index("tm") == 2
+    pl.when(third)(lambda: keep(lower_state(pair_own, pair_extended)))
+    pl.when(jnp.logical_not(third))(
+        lambda: keep(
+            forward_steps(lower_state(pair_own, pair_extended), across, -(ROWS + EXTRA), 6)[0]
+        )
+    )
     before = decode(before, DROP + ROWS)
-    third = time_is(lambda index: index == 2)
     odd = time_is(lambda index: (index & 1) == 1)
     current = {
-        row: jnp.where(third, half_way[row], value) + jnp.where(odd, before[row + DROP], 0.0)
-        for row, value in current.items()
+        row: reached[row - low] + jnp.where(odd, before[row + DROP], 0.0)
+        for row in range(low, ROWS)
     }
     for sub in range(SUBS):
         current = add_rows(current, forced[sub], low, ROWS)
@@ -483,21 +506,40 @@
     }
 
 
-def adjoint_pair_kernel(winds, winds_below, lower_edge, mine, other, own, near, far):
-    @pl.when(lax.axis_index("tm") >= 2)
+def adjoint_ahead_kernel(winds, winds_below, lower_edge, mine, ahead):
+    @pl.when(lax.axis_index("tm") == 3)
     def _():
         across = lower_winds(winds, winds_below, lower_edge)
-        last = time_is(lambda index: index == 3)
-        rows = decode(other, DROP + ROWS)
-        current = {
-            row: jnp.where(last, mine[row + DROP], rows[row + DROP]) for row in range(-DROP, ROWS)
-        }
+        current = {row: mine[row + DROP] for row in range(-DROP, ROWS)}
         current, low = adjoint_steps(current, across, -DROP, 6)
-        for row in range(-DROP, ROWS):
-            current[row] = current[row] + jnp.where(last, rows[row + DROP], mine[row + DROP])
+        for row in range(low, ROWS):
+            ahead[row - low] = current[row]
+
+
+def adjoint_pair_kernel(winds, winds_below, lower_edge, mine, ahead, other, own, near, far):
+    low = -2 * DROP
+
+    def finish(current):
         encode([current[row] for row in range(ROWS)], own)
         encode([current[row] for row in range(-ROWS, 0)], near)
         encode([current[row] for row in range(low, -ROWS)], far)
+
+    @pl.when(lax.axis_index("tm") == 3)
+    def _():
+        rows = decode(other, DROP + ROWS)
+        current = {row: ahead[row - low] for row in range(low, ROWS)}
+        for row in range(-DROP, ROWS):
+            current[row] = current[row] + rows[row + DROP]
+        finish(current)
+
+    @pl.when(lax.axis_index("tm") == 2)
+    def _():
+        across = lower_winds(winds, winds_below, lower_edge)
+        current = dict(zip(range(-DROP, ROWS), decode(other, DROP + ROWS)))
+        current, _ = adjoint_steps(current, across, -DROP, 6)
+        for row in range(-DROP, ROWS):
+            current[row] = current[row] + mine[row + DROP]
+        finish(current)
 
 
 PUSHED = [(sub, row) for sub in range(SUBS) for row in range(ROWS)]
@@ -638,10 +680,16 @@
     )
     before = moved(own, FORWARD_FIRST, 0)
     pair_shapes = (message(message_tiles(ROWS)), message(message_tiles(ROWS + EXTRA)))
+    ahead = run(
+        forward_ahead_kernel,
+        struct(EXTRA + ROWS, LEVELS, WIDTH),
+        (winds, winds_below, lower_edge, mine),
+        name="forward_ahead",
+    )
     own, extended = run(
         forward_pair_kernel,
         pair_shapes,
-        (winds, winds_below, lower_edge, mine, before),
+        (winds, winds_below, lower_edge, mine, ahead, before),
         name="forward_pair",
     )
     pair = (moved(own, FORWARD_SECOND, 0), moved(extended, FORWARD_SECOND, 1))
@@ -671,15 +719,22 @@
         scratch=(
             pltpu.VMEM((SUBS, CHUNKS, 2 * size, CORNERS * LANES), f32),
             pltpu.VMEM((SUBS, CHUNKS, 2 * size, CORNERS * LANES), bf16),
+            pltpu.VMEM((DROP + ROWS, LEVELS, WIDTH), f32),
         ),
         name="forward_final",
     )
 
     after = moved(response, ADJOINT_FIRST, 0)
+    ahead = run(
+        adjoint_ahead_kernel,
+        struct(2 * DROP + ROWS, LEVELS, WIDTH),
+        (winds, winds_below, lower_edge, mine),
+        name="adjoint_ahead",
+    )
     own, near, far = run(
         adjoint_pair_kernel,
         tuple(message(message_tiles(count)) for count in (ROWS, ROWS, EXTRA)),
-        (winds, winds_below, lower_edge, mine, after),
+        (winds, winds_below, lower_edge, mine, ahead, after),
         name="adjoint_pair",
     )
     pair = (

time: 77.2 us -> 77.4 us (level)
    pallas_call x9 -> x11, Pallas kernels: 17 us -> 17.1 us  [run(): pl.pallas_call(kernel, out_shape=outputs, in_specs=[pl.BlockSpec(memory_s...]
where the time goes in v8:
time: 77.4 us; the launch traced here: 77 us
  starting transfers between devices  40.4 us (52%)
  waiting for transfers between devices  19.1 us (25%)
  Pallas kernels  17.1 us (22%)
    ppermute x11, starting transfers between devices, moved(): return lax.ppermute(array, ('tm', 'space'), pairs)  28.8 us
    ppermute x11, waiting for transfers between devices, moved(): return lax.ppermute(array, ('tm', 'space'), pairs)  19.1 us
    pallas_call x11, Pallas kernels, run(): pl.pallas_call(kernel, out_shape=outputs, in_specs=[pl.BlockSpec(memory_s...  17.1 us
    all_to_all x1, starting transfers between devices, shards(): lax.all_to_all(send.reshape(TILES, 8, LANES), 'space', split_axis=0, conc...  11.6 us
  transfers between devices with their start and end apart: 12, of which 4 were waited for; matrix products, arithmetic and copies ran while one was open for 0% of the time, Pallas kernels for 9%

profile of v8, /device:TPU:4, one launch (start us, length us, event | category | flops | bytes accessed | tf_op | source)
XLA Modules:
  0.0 77.0 jit_solution(14915138332740299077)
XLA Ops:
  0.0 1.7 %rows.1 = (f32[16,8,512]{2,1,0:T(8,128)S(1)}, f32[24,8,512]{2,1,0:T(8,128)S(1)}, s32[81,8,128]{2,1,0:T(8,128)S(1)}, s32[69,8,128]{2,1,0:T(8,128)S(1)}, bf16[3,25...) custom-call(f32[3,8,8,512]{3,2,1,0:T(8,128)} %refs_0_.1, ...), custom_call_target="tpu_custom_call" | custom-call | flops 2000000 | bytes 1079296 | tf_op jit(solution)/shard_map/rows/pallas_call | solution.py:601
  1.7 1.9 %collective-permute-start = (s32[81,8,128]{2,1,0:T(8,128)S(1)}, s32[81,8,128]{2,1,0:T(8,128)S(1)}, u32[]{:S(2)}, u32[]{:S(2)}) collective-permute-start(s32[81,8,128]{2,1,0:T(8,128)S(1)} %get-tuple-element.38), channel_id=1, source_target_pairs={{0,1},{1,2},{2,3},{3,4},{4,5},{5,6},{6,7},{7,8},{8,9},{9,10},{10,1... | collective-permute-start | bytes 995336 | tf_op jit(solution)/shard_map/ppermute | solution.py:625
  3.6 3.8 %collective-permute-start.1 = (s32[69,8,128]{2,1,0:T(8,128)S(1)}, s32[69,8,128]{2,1,0:T(8,128)S(1)}, u32[]{:S(2)}, u32[]{:S(2)}) collective-permute-start(s32[69,8,128]{2,1,0:T(8,128)S(1)} %get-tuple-element.39), channel_id=1, source_target_pairs={{0,2},{1,3},{2,4},{3,5},{4,6},{5,7},{6,8},{7,9},{8,10},{9,11},{10,... | collective-permute-start | bytes 847880 | tf_op jit(solution)/shard_map/ppermute | solution.py:625
  7.5 2.2 %pack.1 = f32[512,128]{1,0:T(8,128)} custom-call(bf16[3,256,256]{2,1,0:T(8,128)(2,1)S(1)} %get-tuple-element.40.innovation, s32[3,4,256]{2,1,0:T(4,128)S(1)} %get-tuple-element.41.cells, bf16[3,4,256]{2,1,0:T(4,128)(2,1)S(1)} %get-tuple-element.42.weight, s32[3,1,256]{2,1,0:T(1,128)S(1)} %get-tuple-element.43.owner, ...), custom_call_target="tpu_custom_call" | custom-call | flops 2000000 | bytes 423936 | tf_op jit(solution)/shard_map/pack/pallas_call | solution.py:601
  9.7 11.6 %all-to-all-start = ((f32[64,8,128]{2,1,0:T(8,128)}), f32[64,8,128]{2,1,0:T(8,128)S(1)}, u32[]{:S(2)}, u32[]{:S(2)}) async-start(f32[64,8,128]{2,1,0:T(8,128)} %bitcast.3), calls=%async_computation | async-start | bytes 524288 | tf_op jit(solution)/shard_map/all_to_all | solution.py:664
  21.3 1.0 %forward_local.1 = (s32[29,8,128]{2,1,0:T(8,128)S(1)}, f32[18,8,512]{2,1,0:T(8,128)S(1)}, f32[16,8,512]{2,1,0:T(8,128)S(1)}, f32[16,8,512]{2,1,0:T(8,128)S(1)}, f32[24,8,512]{2,1,0:T(8,128)S(1)}) custom-call(f32[16,8,512]{2,1,0:T(8,128)S(1)} %get-tuple-element.36.winds, f32[24,8,512]{2,1,0:T(8,128)S(1)} %get-tuple-element.37.forces, ...), custom_call_target="tpu_custom_call" | custom-call | flops 2000000000 | bytes 1269760 | tf_op jit(solution)/shard_map/forward_local/pallas_call | solution.py:601
  22.3 3.5 %collective-permute-start.2 = (s32[29,8,128]{2,1,0:T(8,128)S(1)}, s32[29,8,128]{2,1,0:T(8,128)S(1)}, u32[]{:S(2)}, u32[]{:S(2)}) collective-permute-start(s32[29,8,128]{2,1,0:T(8,128)S(1)} %get-tuple-element.51), channel_id=1, source_target_pairs={{0,64},{1,65},{2,66},{3,67},{4,68},{5,69},{6,70},{7,71},{8,72},{9,... | collective-permute-start | bytes 356360 | tf_op jit(solution)/shard_map/ppermute | solution.py:625
  25.8 0.5 forward_ahead.1.ahead
  26.3 3.2 %collective-permute-done.2.other.before = s32[29,8,128]{2,1,0:T(8,128)S(1)} collective-permute-done((s32[29,8,128]{2,1,0:T(8,128)S(1)}, s32[29,8,128]{2,1,0:T(8,128)S(1)}, u32[]{:S(2)}, u32[]{:S(2)}) %collective-permute-start.2) | collective-permute-done | bytes 118816 | tf_op jit(solution)/shard_map/ppermute | solution.py:625
  29.9 3.4 %collective-permute-start.4 = (s32[25,8,128]{2,1,0:T(8,128)S(1)}, s32[25,8,128]{2,1,0:T(8,128)S(1)}, u32[]{:S(2)}, u32[]{:S(2)}) collective-permute-start(s32[25,8,128]{2,1,0:T(8,128)S(1)} %get-tuple-element.54), channel_id=1, source_target_pairs={{64,129},{65,130},{66,131},{67,132},{68,133},{69,134},{70,135},{71... | collective-permute-start | bytes 307208 | tf_op jit(solution)/shard_map/ppermute | solution.py:625
  33.4 2.4 %collective-permute-start.3 = (s32[17,8,128]{2,1,0:T(8,128)S(1)}, s32[17,8,128]{2,1,0:T(8,128)S(1)}, u32[]{:S(2)}, u32[]{:S(2)}) collective-permute-start(s32[17,8,128]{2,1,0:T(8,128)S(1)} %get-tuple-element.53), channel_id=1, source_target_pairs={{64,128},{65,129},{66,130},{67,131},{68,132},{69,133},{70,134},{71... | collective-permute-start | bytes 208904 | tf_op jit(solution)/shard_map/ppermute | solution.py:625
  35.7 2.6 %stencil.1 = (f32[3,128,128]{2,1,0:T(8,128)S(1)}, bf16[3,8,256,512]{3,2,1,0:T(8,128)(2,1)S(1)}, f32[8,8,128]{2,1,0:T(8,128)S(1)}) custom-call(f32[512,128]{1,0:T(8,128)S(1)} %bitcast.5, f32[8,256]{1,0:T(8,128)S(1)} %get-tuple-element.44.channel_weight, f32[1,256]{1,0:T(1,128)S(1)} %get-tuple-element.45.rinv), custom_call_target="tpu_custom_call" | custom-call | flops 2000000 | bytes 271360 | tf_op jit(solution)/shard_map/stencil/pallas_call | solution.py:601
  38.3 6.4 %forward_final.1 = (f32[24,8,512]{2,1,0:T(8,128)S(1)}, f32[14,8,512]{2,1,0:T(8,128)S(1)}, s32[29,8,128]{2,1,0:T(8,128)S(1)}) custom-call(f32[16,8,512]{2,1,0:T(8,128)S(1)} %get-tuple-element.36.winds, f32[24,8,512]{2,1,0:T(8,128)S(1)} %get-tuple-element.37.forces, f32[16,8,512]{2,1,0:T(8,128)S(1)} %get-tuple-element.48.winds_below, ...), custom_call_target="tpu_custom_call" | custom-call | flops 2000000 | bytes 8384512 | tf_op jit(solution)/shard_map/forward_final/pallas_call | solution.py:601
  44.7 1.3 %collective-permute-start.5 = (s32[29,8,128]{2,1,0:T(8,128)S(1)}, s32[29,8,128]{2,1,0:T(8,128)S(1)}, u32[]{:S(2)}, u32[]{:S(2)}) collective-permute-start(s32[29,8,128]{2,1,0:T(8,128)S(1)} %get-tuple-element.59), channel_id=1, source_target_pairs={{192,128},{193,129},{194,130},{195,131},{196,132},{197,133},{198,1... | collective-permute-start | bytes 356360 | tf_op jit(solution)/shard_map/ppermute | solution.py:625
  46.1 6.5 %collective-permute-done.5.other.after = s32[29,8,128]{2,1,0:T(8,128)S(1)} collective-permute-done((s32[29,8,128]{2,1,0:T(8,128)S(1)}, s32[29,8,128]{2,1,0:T(8,128)S(1)}, u32[]{:S(2)}, u32[]{:S(2)}) %collective-permute-start.5) | collective-permute-done | bytes 118816 | tf_op jit(solution)/shard_map/ppermute | solution.py:625
  52.6 1.3 %collective-permute-start.6 = (s32[17,8,128]{2,1,0:T(8,128)S(1)}, s32[17,8,128]{2,1,0:T(8,128)S(1)}, u32[]{:S(2)}, u32[]{:S(2)}) collective-permute-start(s32[17,8,128]{2,1,0:T(8,128)S(1)} %get-tuple-element.61), channel_id=1, source_target_pairs={{128,64},{129,65},{130,66},{131,67},{132,68},{133,69},{134,70},{13... | collective-permute-start | bytes 208904 | tf_op jit(solution)/shard_map/ppermute | solution.py:625
  53.9 1.3 %collective-permute-start.7 = (s32[17,8,128]{2,1,0:T(8,128)S(1)}, s32[17,8,128]{2,1,0:T(8,128)S(1)}, u32[]{:S(2)}, u32[]{:S(2)}) collective-permute-start(s32[17,8,128]{2,1,0:T(8,128)S(1)} %get-tuple-element.62), channel_id=1, source_target_pairs={{129,64},{130,65},{131,66},{132,67},{133,68},{134,69},{135,70},{13... | collective-permute-start | bytes 208904 | tf_op jit(solution)/shard_map/ppermute | solution.py:625
  55.2 1.3 %collective-permute-start.8 = (s32[9,8,128]{2,1,0:T(8,128)S(1)}, s32[9,8,128]{2,1,0:T(8,128)S(1)}, u32[]{:S(2)}, u32[]{:S(2)}) collective-permute-start(s32[9,8,128]{2,1,0:T(8,128)S(1)} %get-tuple-element.63), channel_id=1, source_target_pairs={{130,64},{131,65},{132,66},{133,67},{134,68},{135,69},{136,70},{13... | collective-permute-start | bytes 110600 | tf_op jit(solution)/shard_map/ppermute | solution.py:625
  56.5 6.8 %collective-permute-done.8.pair_far = s32[9,8,128]{2,1,0:T(8,128)S(1)} collective-permute-done((s32[9,8,128]{2,1,0:T(8,128)S(1)}, s32[9,8,128]{2,1,0:T(8,128)S(1)}, u32[]{:S(2)}, u32[]{:S(2)}) %collective-permute-start.8) | collective-permute-done | bytes 36896 | tf_op jit(solution)/shard_map/ppermute | solution.py:625
  63.3 1.4 %adjoint_final.1 = (f32[24,8,512]{2,1,0:T(8,128)S(1)}, s32[49,8,128]{2,1,0:T(8,128)S(1)}, s32[13,8,128]{2,1,0:T(8,128)S(1)}) custom-call(f32[24,8,512]{2,1,0:T(8,128)S(1)} %get-tuple-element.58.sources, f32[16,8,512]{2,1,0:T(8,128)S(1)} %get-tuple-element.36.winds, f32[16,8,512]{2,1,0:T(8,128)S(1)} %get-tuple-element.48.winds_below, ...), custom_call_target="tpu_custom_call" | custom-call | flops 2000000 | bytes 1474560 | tf_op jit(solution)/shard_map/adjoint_final/pallas_call | solution.py:601
  64.6 5.3 %collective-permute-start.9 = (s32[49,8,128]{2,1,0:T(8,128)S(1)}, s32[49,8,128]{2,1,0:T(8,128)S(1)}, u32[]{:S(2)}, u32[]{:S(2)}) collective-permute-start(s32[49,8,128]{2,1,0:T(8,128)S(1)} %get-tuple-element.65), channel_id=1, source_target_pairs={{1,0},{2,1},{3,2},{4,3},{5,4},{6,5},{7,6},{8,7},{9,8},{10,9},{11,1... | collective-permute-start | bytes 602120 | tf_op jit(solution)/shard_map/ppermute | solution.py:625
  69.9 3.3 %collective-permute-start.10 = (s32[13,8,128]{2,1,0:T(8,128)S(1)}, s32[13,8,128]{2,1,0:T(8,128)S(1)}, u32[]{:S(2)}, u32[]{:S(2)}) collective-permute-start(s32[13,8,128]{2,1,0:T(8,128)S(1)} %get-tuple-element.66), channel_id=1, source_target_pairs={{2,0},{3,1},{4,2},{5,3},{6,4},{7,5},{8,6},{9,7},{10,8},{11,9},{12,... | collective-permute-start | bytes 159752 | tf_op jit(solution)/shard_map/ppermute | solution.py:625
  73.2 2.7 %collective-permute-done.10.pushed_far = s32[13,8,128]{2,1,0:T(8,128)S(1)} collective-permute-done((s32[13,8,128]{2,1,0:T(8,128)S(1)}, s32[13,8,128]{2,1,0:T(8,128)S(1)}, u32[]{:S(2)}, u32[]{:S(2)}) %collective-permute-start.10) | collective-permute-done | bytes 53280 | tf_op jit(solution)/shard_map/ppermute | solution.py:625
  75.9 0.9 %finish.1 = f32[3,8,8,512]{3,2,1,0:T(8,128)} custom-call(f32[24,8,512]{2,1,0:T(8,128)S(1)} %get-tuple-element.64.part, s32[49,8,128]{2,1,0:T(8,128)S(1)} %collective-permute-done.9.pushed, s32[13,8,128]{2,1,0:T(8,128)S(1)} %collective-permute-done.10.pushed_far), custom_call_target="tpu_custom_call" | custom-call | flops 2000000 | bytes 647168 | tf_op jit(solution)/shard_map/finish/pallas_call | solution.py:601
  (11 shorter events, 0.4 us)
Async XLA Ops:
  1.7 19.6 %collective-permute-start = (s32[81,8,128]{2,1,0:T(8,128)S(1)}, s32[81,8,128]{2,1,0:T(8,128)S(1)}, u32[]{:S(2)}, u32[]{:S(2)}) collective-permute-start(s32[81,8,128]{2,1,0:T(8,128)S(1)} %get-tuple-element.38), channel_id=1, source_target_pairs={{0,1},{1,2},{2,3},{3,4},{4,5},{5,6},{6,7},{7,8},{8,9},{9,10},{10,1... | collective-permute-start | bytes 995336 | tf_op jit(solution)/shard_map/ppermute | solution.py:625
  3.6 17.7 %collective-permute-start.1 = (s32[69,8,128]{2,1,0:T(8,128)S(1)}, s32[69,8,128]{2,1,0:T(8,128)S(1)}, u32[]{:S(2)}, u32[]{:S(2)}) collective-permute-start(s32[69,8,128]{2,1,0:T(8,128)S(1)} %get-tuple-element.39), channel_id=1, source_target_pairs={{0,2},{1,3},{2,4},{3,5},{4,6},{5,7},{6,8},{7,9},{8,10},{9,11},{10,... | collective-permute-start | bytes 847880 | tf_op jit(solution)/shard_map/ppermute | solution.py:625
  9.7 26.1 %all-to-all-start = ((f32[64,8,128]{2,1,0:T(8,128)}), f32[64,8,128]{2,1,0:T(8,128)S(1)}, u32[]{:S(2)}, u32[]{:S(2)}) async-start(f32[64,8,128]{2,1,0:T(8,128)} %bitcast.3), calls=%async_computation | async-start | bytes 524288 | tf_op jit(solution)/shard_map/all_to_all | solution.py:664
  22.3 7.2 %collective-permute-start.2 = (s32[29,8,128]{2,1,0:T(8,128)S(1)}, s32[29,8,128]{2,1,0:T(8,128)S(1)}, u32[]{:S(2)}, u32[]{:S(2)}) collective-permute-start(s32[29,8,128]{2,1,0:T(8,128)S(1)} %get-tuple-element.51), channel_id=1, source_target_pairs={{0,64},{1,65},{2,66},{3,67},{4,68},{5,69},{6,70},{7,71},{8,72},{9,... | collective-permute-start | bytes 356360 | tf_op jit(solution)/shard_map/ppermute | solution.py:625
  29.9 8.4 %collective-permute-start.4 = (s32[25,8,128]{2,1,0:T(8,128)S(1)}, s32[25,8,128]{2,1,0:T(8,128)S(1)}, u32[]{:S(2)}, u32[]{:S(2)}) collective-permute-start(s32[25,8,128]{2,1,0:T(8,128)S(1)} %get-tuple-element.54), channel_id=1, source_target_pairs={{64,129},{65,130},{66,131},{67,132},{68,133},{69,134},{70,135},{71... | collective-permute-start | bytes 307208 | tf_op jit(solution)/shard_map/ppermute | solution.py:625
  33.4 5.0 %collective-permute-start.3 = (s32[17,8,128]{2,1,0:T(8,128)S(1)}, s32[17,8,128]{2,1,0:T(8,128)S(1)}, u32[]{:S(2)}, u32[]{:S(2)}) collective-permute-start(s32[17,8,128]{2,1,0:T(8,128)S(1)} %get-tuple-element.53), channel_id=1, source_target_pairs={{64,128},{65,129},{66,130},{67,131},{68,132},{69,133},{70,134},{71... | collective-permute-start | bytes 208904 | tf_op jit(solution)/shard_map/ppermute | solution.py:625
  44.7 7.8 %collective-permute-start.5 = (s32[29,8,128]{2,1,0:T(8,128)S(1)}, s32[29,8,128]{2,1,0:T(8,128)S(1)}, u32[]{:S(2)}, u32[]{:S(2)}) collective-permute-start(s32[29,8,128]{2,1,0:T(8,128)S(1)} %get-tuple-element.59), channel_id=1, source_target_pairs={{192,128},{193,129},{194,130},{195,131},{196,132},{197,133},{198,1... | collective-permute-start | bytes 356360 | tf_op jit(solution)/shard_map/ppermute | solution.py:625
  52.6 10.7 %collective-permute-start.6 = (s32[17,8,128]{2,1,0:T(8,128)S(1)}, s32[17,8,128]{2,1,0:T(8,128)S(1)}, u32[]{:S(2)}, u32[]{:S(2)}) collective-permute-start(s32[17,8,128]{2,1,0:T(8,128)S(1)} %get-tuple-element.61), channel_id=1, source_target_pairs={{128,64},{129,65},{130,66},{131,67},{132,68},{133,69},{134,70},{13... | collective-permute-start | bytes 208904 | tf_op jit(solution)/shard_map/ppermute | solution.py:625
  53.9 9.4 %collective-permute-start.7 = (s32[17,8,128]{2,1,0:T(8,128)S(1)}, s32[17,8,128]{2,1,0:T(8,128)S(1)}, u32[]{:S(2)}, u32[]{:S(2)}) collective-permute-start(s32[17,8,128]{2,1,0:T(8,128)S(1)} %get-tuple-element.62), channel_id=1, source_target_pairs={{129,64},{130,65},{131,66},{132,67},{133,68},{134,69},{135,70},{13... | collective-permute-start | bytes 208904 | tf_op jit(solution)/shard_map/ppermute | solution.py:625
  55.2 8.1 %collective-permute-start.8 = (s32[9,8,128]{2,1,0:T(8,128)S(1)}, s32[9,8,128]{2,1,0:T(8,128)S(1)}, u32[]{:S(2)}, u32[]{:S(2)}) collective-permute-start(s32[9,8,128]{2,1,0:T(8,128)S(1)} %get-tuple-element.63), channel_id=1, source_target_pairs={{130,64},{131,65},{132,66},{133,67},{134,68},{135,69},{136,70},{13... | collective-permute-start | bytes 110600 | tf_op jit(solution)/shard_map/ppermute | solution.py:625
  64.6 11.3 %collective-permute-start.9 = (s32[49,8,128]{2,1,0:T(8,128)S(1)}, s32[49,8,128]{2,1,0:T(8,128)S(1)}, u32[]{:S(2)}, u32[]{:S(2)}) collective-permute-start(s32[49,8,128]{2,1,0:T(8,128)S(1)} %get-tuple-element.65), channel_id=1, source_target_pairs={{1,0},{2,1},{3,2},{4,3},{5,4},{6,5},{7,6},{8,7},{9,8},{10,9},{11,1... | collective-permute-start | bytes 602120 | tf_op jit(solution)/shard_map/ppermute | solution.py:625
  69.9 6.0 %collective-permute-start.10 = (s32[13,8,128]{2,1,0:T(8,128)S(1)}, s32[13,8,128]{2,1,0:T(8,128)S(1)}, u32[]{:S(2)}, u32[]{:S(2)}) collective-permute-start(s32[13,8,128]{2,1,0:T(8,128)S(1)} %get-tuple-element.66), channel_id=1, source_target_pairs={{2,0},{3,1},{4,2},{5,3},{6,4},{7,5},{8,6},{9,7},{10,8},{11,9},{12,... | collective-permute-start | bytes 159752 | tf_op jit(solution)/shard_map/ppermute | solution.py:625
